TPU v7x, 32 devices: a whole 2x2x4 slice. The times are simulated.
32 devices in a mesh: grp: 4 (over y, x), mem: 8 (over z, core).
Axes of the slice: x: 2, y: 2, z: 4, core: 2. Of those that a mesh axis runs over, the one named last changes fastest.
Arguments:
- images: bfloat16 [1024, 18432], P(('grp', 'mem')), may hold values from -24 to 24
- classes: int32 [1024], P(('grp', 'mem')), may hold values from 0 to 199, as said below
- rotations: int32 [1024], P(('grp', 'mem')), may hold values from 0 to 35
- bins: int32 [1024], P(('grp', 'mem')), may hold values from 0 to 15
- ctf_table: float32 [16, 18432], replicated, may hold values from -1 to 1
Outputs:
- averages: float32 [200, 18432], P('grp', 'mem')
Inputs may be any that keep to these rules, and one draw needn't show every extreme that they name: The owner of a class c is c // 50. In each aligned block of 32 particles (one device's), at most 16 particles belong to classes of one owner, and exactly 16 do for some owner in every block.
All inputs are finite; a program needn't handle non-finite values.
Results may differ from a plain program's by a relative error of at most 0.0003.
Values may be sent and summed in bfloat16 or wider, within the bound.
No kernel may reach another device: no remote copies, remote signals or barrier semaphores. Data moves between devices by JAX's collectives and lax.ppermute only.
A program may use at most 256 MiB of HBM per device.

v0:
```python
import jax
import jax.numpy as jnp
from jax import lax
from jax.sharding import PartitionSpec as P

ANGLES = 144
ROTS = 36
BINS = 16
CPG = 50
SHIFT = 4


wiener_term = 1.0


def rotate(values, turns):
    count = values.shape[0]
    shaped = values.reshape(count, -1, ANGLES)
    levels = max(ROTS - 1, 1).bit_length()
    for level in range(levels):
        amount = SHIFT * (1 << level) % ANGLES
        rolled = jnp.concatenate([shaped[:, :, amount:], shaped[:, :, :amount]], axis=2)
        chosen = turns >> level & 1 == 1
        shaped = jnp.where(chosen[:, None, None], rolled, shaped)
    return shaped.reshape(count, -1)


def on_device(images, classes, rotations, bins, ctf_table):
    arrived = lax.all_to_all(images, "mem", split_axis=1, concat_axis=0, tiled=True)
    span = arrived.shape[1]
    labels = jnp.stack([classes, bins, rotations], axis=1)
    tags = lax.all_gather(labels, "mem", axis=0, tiled=True)
    class_here = tags[:, 0]
    bin_here = tags[:, 1]
    turn_here = tags[:, 2]
    member = (
        jnp.arange(CPG * lax.axis_size("grp"), dtype=jnp.int32)[:, None] == class_here[None, :]
    ).astype(jnp.float32)
    bin_pick = (bin_here[:, None] == jnp.arange(BINS, dtype=jnp.int32)[None, :]).astype(jnp.float32)
    ctf_slice = lax.dynamic_slice_in_dim(ctf_table, lax.axis_index("mem") * span, span, 1)
    ctf_rows = jnp.dot(bin_pick, ctf_slice, precision=lax.Precision.HIGHEST)
    aligned = rotate(ctf_rows * arrived.astype(jnp.float32), turn_here)
    numer = jnp.dot(member, aligned, precision=lax.Precision.HIGHEST)
    weights = rotate(ctf_rows * ctf_rows, turn_here)
    denom_part = jnp.dot(member, weights, precision=lax.Precision.HIGHEST)
    numer_here, denom_here = (
        lax.psum_scatter(numer, "grp", scatter_dimension=0, tiled=True),
        lax.psum_scatter(denom_part, "grp", scatter_dimension=0, tiled=True),
    )
    return numer_here / (denom_here + wiener_term)


def solution(mesh):
    in_specs = (
        P(("grp", "mem"), None),
        P(("grp", "mem")),
        P(("grp", "mem")),
        P(("grp", "mem")),
        P(),
    )
    out_specs = P("grp", "mem")
    return jax.shard_map(
        on_device, mesh=mesh, in_specs=in_specs, out_specs=out_specs, check_vma=False
    )
```

profile of v0, /device:TPU:0, one launch (start us, length us, event | category | flops | bytes accessed | tf_op | source)
XLA Modules:
  0.0 238.8 jit_solution(11630020243048273355)
XLA Ops:
  0.0 2.5 %copy.41 = bf16[4,8,8,2304]{3,2,0,1:T(8,128)(2,1)} copy(bf16[4,8,8,2304]{3,2,1,0:T(8,128)(2,1)} %bitcast.55) | data formatting | bytes 2359296 | tf_op jit(solution)/shard_map/all_to_all | solution.py:29
  2.5 6.3 %all-to-all-start = ((bf16[32,8,2304]{2,0,1:T(8,128)(2,1)}), bf16[32,8,2304]{2,0,1:T(8,128)(2,1)S(1)}, u32[]{:S(2)}, u32[]{:S(2)}) async-start(bf16[32,8,2304]{2,0,1:T(8,128)(2,1)} %bitcast.36), calls=%async_computation | async-start | bytes 2359296 | tf_op jit(solution)/shard_map/all_to_all | solution.py:29
  8.9 35.3 %all-gather = s32[8,32,3]{1,2,0:T(4,128)S(1)} all-gather(s32[1,32,3]{1,2,0:T(4,128)S(1)} %add_bitcast_fusion), channel_id=1, replica_groups=mesh['grp'=4,'mem'=8] {'mem'}, dimensions={0}, use_global_device_ids=true | all-gather | bytes 3456 | tf_op jit(solution)/shard_map/all_gather | solution.py:32
  44.9 4.3 %bitcast_multiply_fusion = (f32[256,2304]{1,0:T(8,128)}, f32[256,2304]{1,0:T(8,128)}, f32[256,2304]{1,0:T(8,128)}) fusion(bf16[32,8,2304]{2,0,1:T(8,128)(2,1)S(1)} %all-to-all-done, f32[16,18432]{1,0:T(8,128)S(1)} %copy-done, s32[]{:T(128)S(6)} %select_n.72, s32[256]{0:T(256)S(1)} %bitcast.58), kind=kOutput, calls=%fused_computation.12 | convolution fusion | flops 115019776 | bytes 8406020 | tf_op jit(solution)/shard_map/dot_general | solution.py:41
  49.2 2.0 copy.25
  52.9 3.0 %copy.32 = f32[256,2304]{0,1:T(8,128)} copy(f32[256,2304]{1,0:T(8,128)} %get-tuple-element.20) | data formatting | bytes 4718592 | tf_op jit(solution)/shard_map/mul | solution.py:44
  56.0 2.0 slice.123
  59.1 3.1 %broadcast_select_fusion.1 = (f32[256,16,144]{0,2,1:T(8,128)S(1)}, f32[256,16,144]{0,2,1:T(8,128)}, f32[256,16,144]{0,2,1:T(8,128)S(1)}, f32[256,16,144]{0,2,1:T(8,128)}) fusion(f32[256,16,144]{0,2,1:T(8,128)S(1)} %bitcast.39, pred[256]{0:T(512)(128)(4,1)S(1)} %copy-done.21, f32[256,16,4]{0,2,1:T(4,128)S(1)} %slice.112, f32[256,16,140]{0,2,1:T(8,128)S(1)} %copy-done.15, ...), kind=kLoop, calls=%fused_computation.41 | loop fusion | flops 2359296 | bytes 18874624 | tf_op jit(solution)/shard_map/jit(_where)/select_n | solution.py:24
  63.0 3.1 %pad_maximum_fusion.1 = (f32[256,16,144]{0,2,1:T(8,128)}, f32[256,16,144]{0,2,1:T(8,128)S(1)}, f32[256,16,144]{0,2,1:T(8,128)S(1)}, f32[256,16,144]{0,2,1:T(8,128)}) fusion(f32[256,16,8]{0,2,1:T(8,128)S(1)} %slice.114, f32[256,16,136]{0,2,1:T(8,128)S(1)} %slice.113, f32[256,16,144]{0,2,1:T(8,128)S(1)} %get-tuple-element.15, pred[256]{0:T(512)(128)(4,1)S(1)} %copy-done.20, ...), kind=kLoop, calls=%fused_computation.1 | loop fusion | flops 2359296 | bytes 18874624 | tf_op jit(solution)/shard_map/concatenate | solution.py:22
  66.3 2.0 pad_maximum_fusion.2
  80.4 1.9 copy.31
  82.4 3.1 %copy.30 = f32[256,2304]{1,0:T(8,128)} copy(f32[256,2304]{0,1:T(8,128)} %bitcast.53) | data formatting | bytes 4718592 | tf_op jit(solution)/shard_map/concatenate | solution.py:22
  85.5 3.2 %copy.29 = f32[256,2304]{1,0:T(8,128)} copy(f32[256,2304]{0,1:T(8,128)} %bitcast.51) | data formatting | bytes 4718592 | tf_op jit(solution)/shard_map/concatenate | solution.py:22
  88.7 1.9 copy.28
  90.6 3.2 %copy.27 = f32[256,2304]{1,0:T(8,128)} copy(f32[256,2304]{0,1:T(8,128)} %bitcast.48) | data formatting | bytes 4718592 | tf_op jit(solution)/shard_map/concatenate | solution.py:22
  93.8 2.0 copy.26
  97.6 2.0 copy.38
  99.7 3.2 %copy.37 = f32[256,2304]{1,0:T(8,128)} copy(f32[256,2304]{0,1:T(8,128)} %bitcast.54) | data formatting | bytes 4718592 | tf_op jit(solution)/shard_map/concatenate | solution.py:22
  102.9 1.9 copy.36
  104.8 3.2 %copy.35 = f32[256,2304]{1,0:T(8,128)} copy(f32[256,2304]{0,1:T(8,128)} %bitcast.50) | data formatting | bytes 4718592 | tf_op jit(solution)/shard_map/concatenate | solution.py:22
  108.1 2.0 copy.34
  110.1 3.2 %copy.33 = f32[256,2304]{1,0:T(8,128)} copy(f32[256,2304]{0,1:T(8,128)} %bitcast.45) | data formatting | bytes 4718592 | tf_op jit(solution)/shard_map/concatenate | solution.py:22
  113.4 8.5 %fusion.9 = f32[200,2304]{1,0:T(8,128)} fusion(f32[256,2304]{1,0:T(8,128)} %copy.31, f32[256,2304]{1,0:T(8,128)} %copy.30, f32[256,2304]{1,0:T(8,128)} %copy.29, f32[256,2304]{1,0:T(8,128)} %copy.28, f32[256,2304]{1,0:T(8,128)} %copy.27, f32[256,2304]{1,0:T(8,128)} %copy.26, f32[256,2304]{1,0:T(8,128)S(1)} %copy-done.3, pred[256]{0:T(512)(128)(4,1)S(1)} %copy-done.21, ...), kind=kOutput, calls=%fused_computation.20 | convolution fusion | flops 1419167744 | bytes 18360832 | tf_op jit(solution)/shard_map/dot_general | solution.py:43
  123.9 3.6 %fusion.2 = f32[200,2304]{1,0:T(8,128)} fusion(f32[256,2304]{1,0:T(8,128)S(1)} %copy-done.5, f32[256,2304]{1,0:T(8,128)S(1)} %copy-done.6, f32[256,2304]{1,0:T(8,128)S(1)} %copy-done.7, f32[256,2304]{1,0:T(8,128)S(1)} %copy-done.8, f32[256,2304]{1,0:T(8,128)S(1)} %copy-done.9, f32[256,2304]{1,0:T(8,128)S(1)} %copy-done.10, ...), kind=kOutput, calls=%fused_computation.13 | convolution fusion | flops 1419757568 | bytes 18360832 | tf_op jit(solution)/shard_map/dot_general | solution.py:45
  127.4 82.7 %fusion.36 = (f32[64,2304]{1,0:T(8,128)S(1)}, f32[64,2304]{1,0:T(8,128)S(1)}) fusion(f32[200,2304]{1,0:T(8,128)} %fusion.2, f32[200,2304]{1,0:T(8,128)S(1)} %copy-done.16), kind=kCustom, calls=%all-reduce-scatter.2 | all-reduce-scatter fusion | flops 1179649 | bytes 4866560
  210.2 4.2 %collective-permute-start = (f32[42,2304]{1,0:T(8,128)S(1)}, f32[42,2304]{1,0:T(8,128)}, u32[]{:S(2)}, u32[]{:S(2)}) collective-permute-start(f32[42,2304]{1,0:T(8,128)S(1)} %slice.135), channel_id=1, source_target_pairs={{0,8},{8,16},{16,24},{1,9},{9,17},{17,25},{2,10},{10,18},{18,26},{... | collective-permute-start | bytes 1161224
  214.5 3.3 %collective-permute-start.1 = (f32[42,2304]{1,0:T(8,128)S(1)}, f32[42,2304]{1,0:T(8,128)}, u32[]{:S(2)}, u32[]{:S(2)}) collective-permute-start(f32[42,2304]{1,0:T(8,128)S(1)} %slice.136), channel_id=1, source_target_pairs={{0,8},{8,16},{16,24},{1,9},{9,17},{17,25},{2,10},{10,18},{18,26},{... | collective-permute-start | bytes 1161224
  219.0 5.2 %collective-permute-done = f32[42,2304]{1,0:T(8,128)} collective-permute-done((f32[42,2304]{1,0:T(8,128)S(1)}, f32[42,2304]{1,0:T(8,128)}, u32[]{:S(2)}, u32[]{:S(2)}) %collective-permute-start) | collective-permute-done | bytes 387104
  224.2 3.2 %concatenate.84 = f32[106,2304]{1,0:T(8,128)S(1)} concatenate(f32[42,2304]{1,0:T(8,128)} %collective-permute-done, f32[64,2304]{1,0:T(8,128)} %copy-done.19), dimensions={0} | concatenate | bytes 1953792
  227.4 4.7 %collective-permute-done.1 = f32[42,2304]{1,0:T(8,128)} collective-permute-done((f32[42,2304]{1,0:T(8,128)S(1)}, f32[42,2304]{1,0:T(8,128)}, u32[]{:S(2)}, u32[]{:S(2)}) %collective-permute-start.1) | collective-permute-done | bytes 387104
  232.2 4.7 %concatenate.85 = f32[106,2304]{1,0:T(8,128)} concatenate(f32[42,2304]{1,0:T(8,128)} %collective-permute-done.1, f32[64,2304]{1,0:T(8,128)S(1)} %copy-done.18), dimensions={0} | concatenate | bytes 1953792
  236.8 2.0 fusion.28
  (93 shorter events, 20.9 us)
Async XLA Ops:
  0.0 44.9 %copy-start = (f32[16,18432]{1,0:T(8,128)S(1)}, f32[16,18432]{1,0:T(8,128)}, u32[]{:S(2)}) copy-start(f32[16,18432]{1,0:T(8,128)} %param.9) | copy-start | bytes 3538948
  0.0 8.8 %copy-start.23 = (s32[32]{0:T(128)S(1)}, s32[32]{0:T(128)}, u32[]{:S(2)}) copy-start(s32[32]{0:T(128)} %param.7) | copy-start | bytes 388
  0.0 8.8 %copy-start.24 = (s32[32]{0:T(128)S(1)}, s32[32]{0:T(128)}, u32[]{:S(2)}) copy-start(s32[32]{0:T(128)} %param.8) | copy-start | bytes 388
  0.0 8.8 %copy-start.25 = (s32[32]{0:T(128)S(1)}, s32[32]{0:T(128)}, u32[]{:S(2)}) copy-start(s32[32]{0:T(128)} %param.6) | copy-start | bytes 388
  2.5 42.4 %all-to-all-start = ((bf16[32,8,2304]{2,0,1:T(8,128)(2,1)}), bf16[32,8,2304]{2,0,1:T(8,128)(2,1)S(1)}, u32[]{:S(2)}, u32[]{:S(2)}) async-start(bf16[32,8,2304]{2,0,1:T(8,128)(2,1)} %bitcast.36), calls=%async_computation | async-start | bytes 2359296 | tf_op jit(solution)/shard_map/all_to_all | solution.py:29
  56.0 2.4 copy-start.2
  56.0 3.1 %copy-start.15 = (f32[256,16,140]{0,2,1:T(8,128)S(1)}, f32[256,16,140]{0,2,1:T(8,128)}, u32[]{:S(2)}) copy-start(f32[256,16,140]{0,2,1:T(8,128)} %slice.111) | copy-start | bytes 6881284
  56.0 3.1 %copy-start.21 = (pred[256]{0:T(512)(128)(4,1)S(1)}, pred[256]{0:T(512)(128)(4,1)}, u32[]{:S(2)}) copy-start(pred[256]{0:T(512)(128)(4,1)} %get-tuple-element.10) | copy-start | bytes 772
  62.4 0.7 copy-start.20
  85.5 3.2 %copy-start.13 = (f32[256,16,144]{0,2,1:T(8,128)S(1)}, f32[256,16,144]{0,2,1:T(8,128)}, u32[]{:S(2)}) copy-start(f32[256,16,144]{0,2,1:T(8,128)} %get-tuple-element.23) | copy-start | bytes 7077892
  90.6 3.2 %copy-start.11 = (f32[256,16,144]{0,2,1:T(8,128)S(1)}, f32[256,16,144]{0,2,1:T(8,128)}, u32[]{:S(2)}) copy-start(f32[256,16,144]{0,2,1:T(8,128)} %get-tuple-element.16) | copy-start | bytes 7077892
  99.7 3.2 %copy-start.14 = (f32[256,16,144]{0,2,1:T(8,128)S(1)}, f32[256,16,144]{0,2,1:T(8,128)}, u32[]{:S(2)}) copy-start(f32[256,16,144]{0,2,1:T(8,128)} %get-tuple-element.33) | copy-start | bytes 7077892
  104.8 3.2 %copy-start.12 = (f32[256,16,144]{0,2,1:T(8,128)S(1)}, f32[256,16,144]{0,2,1:T(8,128)}, u32[]{:S(2)}) copy-start(f32[256,16,144]{0,2,1:T(8,128)} %get-tuple-element.43) | copy-start | bytes 7077892
  110.1 3.2 %copy-start.3 = (f32[256,2304]{1,0:T(8,128)S(1)}, f32[256,2304]{1,0:T(8,128)}, u32[]{:S(2)}) copy-start(f32[256,2304]{1,0:T(8,128)} %get-tuple-element.19) | copy-start | bytes 7077892
  110.1 3.2 %copy-start.22 = (pred[256]{0:T(512)(128)(4,1)S(1)}, pred[256]{0:T(512)(128)(4,1)}, u32[]{:S(2)}) copy-start(pred[256]{0:T(512)(128)(4,1)} %get-tuple-element.5) | copy-start | bytes 772
  113.3 8.6 %copy-start.4 = (f32[256,2304]{1,0:T(8,128)S(1)}, f32[256,2304]{1,0:T(8,128)}, u32[]{:S(2)}) copy-start(f32[256,2304]{1,0:T(8,128)} %get-tuple-element.41) | copy-start | bytes 7077892
  113.3 8.6 %copy-start.5 = (f32[256,2304]{1,0:T(8,128)S(1)}, f32[256,2304]{1,0:T(8,128)}, u32[]{:S(2)}) copy-start(f32[256,2304]{1,0:T(8,128)} %copy.38) | copy-start | bytes 7077892
  113.3 8.6 %copy-start.6 = (f32[256,2304]{1,0:T(8,128)S(1)}, f32[256,2304]{1,0:T(8,128)}, u32[]{:S(2)}) copy-start(f32[256,2304]{1,0:T(8,128)} %copy.37) | copy-start | bytes 7077892
  113.3 8.6 %copy-start.7 = (f32[256,2304]{1,0:T(8,128)S(1)}, f32[256,2304]{1,0:T(8,128)}, u32[]{:S(2)}) copy-start(f32[256,2304]{1,0:T(8,128)} %copy.36) | copy-start | bytes 7077892
  113.3 8.9 %copy-start.8 = (f32[256,2304]{1,0:T(8,128)S(1)}, f32[256,2304]{1,0:T(8,128)}, u32[]{:S(2)}) copy-start(f32[256,2304]{1,0:T(8,128)} %copy.35) | copy-start | bytes 7077892
  113.3 9.8 %copy-start.9 = (f32[256,2304]{1,0:T(8,128)S(1)}, f32[256,2304]{1,0:T(8,128)}, u32[]{:S(2)}) copy-start(f32[256,2304]{1,0:T(8,128)} %copy.34) | copy-start | bytes 7077892
  113.4 10.5 %copy-start.10 = (f32[256,2304]{1,0:T(8,128)S(1)}, f32[256,2304]{1,0:T(8,128)}, u32[]{:S(2)}) copy-start(f32[256,2304]{1,0:T(8,128)} %copy.33) | copy-start | bytes 7077892
  123.9 3.6 %copy-start.16 = (f32[200,2304]{1,0:T(8,128)S(1)}, f32[200,2304]{1,0:T(8,128)}, u32[]{:S(2)}) copy-start(f32[200,2304]{1,0:T(8,128)} %fusion.9) | copy-start | bytes 5529604
  127.4 90.3 %copy-start.26 = (u32[32]{0:T(128)S(1)}, u32[32]{0:T(128)}, u32[]{:S(2)}) copy-start(u32[32]{0:T(128)} %constant.25) | copy-start | bytes 388
  210.1 4.3 %copy-start.17 = (f32[64,2304]{1,0:T(8,128)}, f32[64,2304]{1,0:T(8,128)S(1)}, u32[]{:S(2)}) copy-start(f32[64,2304]{1,0:T(8,128)S(1)} %get-tuple-element.13) | copy-start | bytes 1769476
  210.1 4.3 %copy-start.19 = (f32[64,2304]{1,0:T(8,128)}, f32[64,2304]{1,0:T(8,128)S(1)}, u32[]{:S(2)}) copy-start(f32[64,2304]{1,0:T(8,128)S(1)} %get-tuple-element.14) | copy-start | bytes 1769476
  210.2 14.0 %collective-permute-start = (f32[42,2304]{1,0:T(8,128)S(1)}, f32[42,2304]{1,0:T(8,128)}, u32[]{:S(2)}, u32[]{:S(2)}) collective-permute-start(f32[42,2304]{1,0:T(8,128)S(1)} %slice.135), channel_id=1, source_target_pairs={{0,8},{8,16},{16,24},{1,9},{9,17},{17,25},{2,10},{10,18},{18,26},{... | collective-permute-start | bytes 1161224
  214.5 17.7 %copy-start.18 = (f32[64,2304]{1,0:T(8,128)S(1)}, f32[64,2304]{1,0:T(8,128)}, u32[]{:S(2)}) copy-start(f32[64,2304]{1,0:T(8,128)} %copy-done.17) | copy-start | bytes 1769476
  214.5 17.7 %collective-permute-start.1 = (f32[42,2304]{1,0:T(8,128)S(1)}, f32[42,2304]{1,0:T(8,128)}, u32[]{:S(2)}, u32[]{:S(2)}) collective-permute-start(f32[42,2304]{1,0:T(8,128)S(1)} %slice.136), channel_id=1, source_target_pairs={{0,8},{8,16},{16,24},{1,9},{9,17},{17,25},{2,10},{10,18},{18,26},{... | collective-permute-start | bytes 1161224
  219.0 19.8 %copy-start.1 = (f32[16,18432]{1,0:T(8,128)S(1)}, f32[16,18432]{1,0:T(8,128)}, u32[]{:S(2)}) copy-start(f32[16,18432]{1,0:T(8,128)} %param.9) | copy-start | bytes 3538948
where the time goes:
time: 240 us; the launch traced here: 239 us
  blocking collectives  118 us (49%)
  local copies, waits for them, and re-layouts  57.7 us (24%)
  other arithmetic  21.9 us (9%)
  matrix products  16.4 us (7%)
  starting transfers between devices  13.8 us (6%)
  waiting for transfers between devices  9.98 us (4%)
    unnamed x1, blocking collectives  82.7 us
    all_gather x1, blocking collectives, on_device(): tags = lax.all_gather(labels, 'mem', axis=0, tiled=True)  35.3 us
    concatenate x12, local copies, waits for them, and re-layouts, rotate(): jnp.concatenate([shaped[:, :, amount:], shaped[:, :, :amount]], axis=2)  31.1 us
    concatenate x9, other arithmetic, rotate(): jnp.concatenate([shaped[:, :, amount:], shaped[:, :, :amount]], axis=2)  16.2 us
    unnamed x60, local copies, waits for them, and re-layouts  12.1 us
    unnamed x2, waiting for transfers between devices  9.98 us
    dot_general x1, matrix products, on_device(): numer = jnp.dot(member, aligned, precision=lax.Precision.HIGHEST)  8.54 us
    unnamed x2, starting transfers between devices  7.5 us
  transfers between devices with their start and end apart: 3, of which 2 were waited for; matrix products, arithmetic and copies ran while one was open for 2% of the time, Pallas kernels for 0%

commit v1 on v0

v1 whole, which is shorter than its diff:
```python
import functools

import jax
import jax.numpy as jnp
from jax import lax
from jax.experimental import pallas as pl
from jax.experimental.pallas import tpu as pltpu
from jax.sharding import PartitionSpec as P

ANGLES = 144
ROTS = 36
BINS = 16
CPG = 50
SHIFT = 4

LANES = 128
ROWS = 8
CPAD = -(-CPG // ROWS) * ROWS
PIECES = 3
PAIRS = -(-ROTS * BINS // LANES) * LANES
LEVELS = max(ROTS - 1, 1).bit_length()
VMEM_LIMIT = 56 * 1024 * 1024

wiener_term = 1.0

F32 = jnp.float32
BF16 = jnp.bfloat16
NT = (((1,), (1,)), ((), ()))
ANY = pl.BlockSpec(memory_space=pl.ANY)
VMEM = pl.BlockSpec(memory_space=pltpu.VMEM)


def partner(index, step, size):
    if size & (size - 1) == 0:
        return index ^ step
    return (index + step) % size


def send(value, axis, step):
    size = lax.axis_size(axis)
    return lax.ppermute(value, axis, [(i, partner(i, step, size)) for i in range(size)])


def identity():
    rows = lax.broadcasted_iota(jnp.int32, (LANES, LANES), 0)
    cols = lax.broadcasted_iota(jnp.int32, (LANES, LANES), 1)
    return (rows == cols).astype(BF16)


def turned(block, amount):
    amount %= ANGLES
    if amount == 0:
        return block
    if amount % ROWS == 0:
        return jnp.concatenate([block[amount:], block[:amount]], axis=0)
    return pltpu.roll(block, ANGLES - amount, 0)


def split(value):
    high = value.astype(BF16)
    low = (value - high.astype(F32)).astype(BF16)
    return high, low


def params(flops, moved):
    return dict(
        compiler_params=pltpu.CompilerParams(vmem_limit_bytes=VMEM_LIMIT),
        cost_estimate=pl.CostEstimate(flops=flops, bytes_accessed=moved, transcendentals=0),
    )


def pack_kernel(mem, cols, edges, img, cls, rot, bns, own_tag, *rest):
    size = mem
    count = cls.shape[1]
    groups = count // ROWS
    chunks = len(edges) - 1
    msgs = rest[: chunks * (size - 1)]
    tagbuf, sems, tag_sems = rest[chunks * (size - 1) :]
    me = lax.axis_index("mem")
    copies = []
    for chunk in range(chunks):
        width = (edges[chunk + 1] - edges[chunk]) * LANES
        for step in range(1, size):
            dest = partner(me, step, size)
            start = pl.multiple_of(dest * cols + edges[chunk] * LANES, LANES)
            out = msgs[chunk * (size - 1) + step - 1]
            for g in range(groups):
                copies.append(
                    pltpu.make_async_copy(
                        img.at[pl.ds(g * ROWS, ROWS), pl.ds(start, width)],
                        out.at[:, pl.ds(g * width, width)],
                        sems.at[len(copies)],
                    )
                )
                copies[-1].start()
    label = cls[...]
    owner = jnp.zeros_like(label)
    for g in range(1, lax.axis_size("grp")):
        owner += (label >= g * CPG).astype(jnp.int32)
    row = lax.broadcasted_iota(jnp.int32, (ROWS, count), 0)
    stack = jnp.where(
        row == 0,
        owner,
        jnp.where(
            row == 1,
            label - owner * CPG,
            jnp.where(row == 2, bns[...], jnp.where(row == 3, rot[...], 0)),
        ),
    )
    spread = (
        lax.broadcasted_iota(jnp.int32, (count, LANES), 1) % count
        == lax.broadcasted_iota(jnp.int32, (count, LANES), 0)
    ).astype(BF16)
    tags = jnp.dot(stack.astype(F32).astype(BF16), spread, preferred_element_type=F32)
    place = lax.broadcasted_iota(jnp.int32, (ROWS, LANES), 1) // count
    per_tile = LANES // count
    width = (edges[1] - edges[0]) * LANES
    tag_copies = []
    for step in range(size):
        mine = jnp.where(place == step % per_tile, tags, 0.0).astype(BF16)
        if step == 0:
            own_tag[...] = mine
            continue
        tagbuf[step] = mine
    for step in range(1, size):
        tag_copies.append(
            pltpu.make_async_copy(
                tagbuf.at[step],
                msgs[step - 1].at[:, pl.ds(groups * width, LANES)],
                tag_sems.at[step - 1],
            )
        )
        tag_copies[-1].start()
    for copy in copies + tag_copies:
        copy.wait()


def pack(images, classes, rotations, bins, cols, edges):
    size = lax.axis_size("mem")
    count = images.shape[0]
    groups = count // ROWS
    shapes = [jax.ShapeDtypeStruct((ROWS, LANES), BF16)]
    for chunk in range(len(edges) - 1):
        width = groups * (edges[chunk + 1] - edges[chunk]) * LANES + (LANES if chunk == 0 else 0)
        shapes += [jax.ShapeDtypeStruct((ROWS, width), BF16)] * (size - 1)
    total = (size - 1) * groups * (len(edges) - 1)
    outs = pl.pallas_call(
        functools.partial(pack_kernel, size, cols, edges),
        out_shape=shapes,
        in_specs=[ANY, VMEM, VMEM, VMEM],
        out_specs=[VMEM] + [ANY] * (len(shapes) - 1),
        scratch_shapes=[
            pltpu.VMEM((size, ROWS, LANES), BF16),
            pltpu.SemaphoreType.DMA((total,)),
            pltpu.SemaphoreType.DMA((size - 1,)),
        ],
        name="pack",
        **params(1 << 16, 4 * images.size),
    )(images, classes.reshape(1, -1), rotations.reshape(1, -1), bins.reshape(1, -1))
    own_tag, msgs = outs[0], outs[1:]
    return own_tag, [msgs[c * (size - 1) : (c + 1) * (size - 1)] for c in range(len(edges) - 1)]


def table_kernel(turns, ctf, pieces, weights, square):
    cols = ctf.shape[1]
    value = ctf[...]
    high = value.astype(BF16).astype(F32)
    mid = (value - high).astype(BF16).astype(F32)
    low = value - high - mid
    stacked = jnp.concatenate([high, mid, low], axis=0).astype(BF16)
    eye = identity()
    pick = (
        lax.broadcasted_iota(jnp.int32, (PIECES * BINS, PAIRS), 0) % BINS
        == lax.broadcasted_iota(jnp.int32, (PIECES * BINS, PAIRS), 1) % BINS
    ).astype(BF16)
    for tile in range(cols // LANES):
        rows = pl.ds(tile * LANES, LANES)
        flipped = lax.dot_general(
            eye, stacked[:, tile * LANES : (tile + 1) * LANES], NT, preferred_element_type=F32
        ).astype(BF16)
        pieces[rows, :] = flipped
        spread = jnp.dot(flipped, pick, preferred_element_type=F32)
        square[rows, :] = spread * spread
    per_tile = LANES // BINS
    turn = lax.broadcasted_iota(jnp.int32, (1, LANES), 1) // BINS
    levels = max(per_tile - 1, 1).bit_length()

    def one(q, carry):
        rows = pl.ds(pl.multiple_of(q * ANGLES, ROWS), ANGLES)
        for tile in range(PAIRS // LANES):
            block = turned(square[rows, pl.ds(tile * LANES, LANES)], SHIFT * per_tile * tile)
            for level in range(levels):
                chosen = (turn >> level & 1) == 1
                block = jnp.where(chosen, turned(block, SHIFT << level), block)
            high, low = split(block)
            weights[rows, pl.ds(tile * LANES, LANES)] = high
            weights[rows, pl.ds(PAIRS + tile * LANES, LANES)] = low
        return carry

    lax.fori_loop(0, turns, one, 0)


def tables(ctf, turns):
    cols = ctf.shape[1]
    return pl.pallas_call(
        functools.partial(table_kernel, turns),
        out_shape=[
            jax.ShapeDtypeStruct((cols, PIECES * BINS), BF16),
            jax.ShapeDtypeStruct((turns * ANGLES, 2 * PAIRS), BF16),
        ],
        in_specs=[VMEM],
        out_specs=[VMEM, VMEM],
        scratch_shapes=[pltpu.VMEM((cols, PAIRS), F32)],
        name="tables",
        **params(40 * cols * PAIRS, 4 * cols * PAIRS),
    )(ctf)


def numer_kernel(mem, cols, count, first, rows, base, tiles, segments, *refs):
    refs = list(refs)
    grp = lax.axis_size("grp")
    lanes = mem * count
    groups = count // ROWS
    img, pieces, tag_in = refs[:3]
    refs = refs[3:]
    msgs = []
    for _ in segments:
        msgs.append(refs[: mem - 1])
        refs = refs[mem - 1 :]
    if first:
        tags = refs.pop(0)
    else:
        tags = tag_in
    sums = refs[:grp]
    refs = refs[grp:]
    data, tagbuf, product, parts, sems, tag_sems = refs
    me = lax.axis_index("mem")
    own = lax.axis_index("grp")

    copies, tag_copies = [], []
    start = pl.multiple_of(me * cols + base * LANES, LANES)
    copies.append(
        pltpu.make_async_copy(
            img.at[:, pl.ds(start, tiles * LANES)], data.at[pl.ds(0, count)], sems.at[0]
        )
    )
    for seg, (wide, src, dst, width) in enumerate(segments):
        for step in range(1, mem):
            for g in range(groups):
                copies.append(
                    pltpu.make_async_copy(
                        msgs[seg][step - 1].at[:, pl.ds((g * wide + src) * LANES, width * LANES)],
                        data.at[
                            pl.ds(step * count + g * ROWS, ROWS), pl.ds(dst * LANES, width * LANES)
                        ],
                        sems.at[len(copies)],
                    )
                )
    if first:
        wide = segments[0][0]
        for step in range(1, mem):
            tag_copies.append(
                pltpu.make_async_copy(
                    msgs[0][step - 1].at[:, pl.ds(groups * wide * LANES, LANES)],
                    tagbuf.at[step],
                    tag_sems.at[step - 1],
                )
            )
    for copy in tag_copies + copies:
        copy.start()
    for copy in tag_copies:
        copy.wait()
    if first:
        per_tile = LANES // count
        for tile in range(lanes // LANES):
            total = None
            for step in range(tile * per_tile, (tile + 1) * per_tile):
                part = (tag_in[...] if step == 0 else tagbuf[step]).astype(F32)
                total = part if total is None else total + part
            tags[:, pl.ds(tile * LANES, LANES)] = total
    label = tags[...].astype(jnp.int32)
    key = label[0:1] * CPAD + label[1:2]
    spot = label[2:3]
    turn = label[3:4]
    pick = (
        lax.broadcasted_iota(jnp.int32, (PIECES * BINS, lanes), 0) % BINS == spot
    ).astype(BF16)
    klass = lax.broadcasted_iota(jnp.int32, (CPAD, lanes), 0)
    member = []
    for step in range(grp):
        one = (klass + CPAD * partner(own, step, grp) == key).astype(BF16)
        member.append(jnp.concatenate([one, one], axis=1))
    eye = identity()
    for copy in copies:
        copy.wait()

    def flip(tile, carry):
        across = pl.ds(pl.multiple_of(tile * LANES, LANES), LANES)
        flipped = lax.dot_general(eye, data[:, across], NT, preferred_element_type=F32)
        ctf = jnp.dot(
            pieces[pl.ds(pl.multiple_of((base + tile) * LANES, LANES), LANES), :],
            pick,
            preferred_element_type=F32,
        )
        product[across, :] = flipped * ctf
        return carry

    lax.fori_loop(0, tiles, flip, 0)
    offset = rows[0] * ANGLES - base * LANES

    def rotate(q, carry):
        for tile in range(lanes // LANES):
            block = product[
                pl.ds(pl.multiple_of(offset + q * ANGLES, ROWS), ANGLES),
                pl.ds(tile * LANES, LANES),
            ]
            bits = turn[:, tile * LANES : (tile + 1) * LANES]
            for level in range(LEVELS):
                chosen = (bits >> level & 1) == 1
                block = jnp.where(chosen, turned(block, SHIFT << level), block)
            high, low = split(block)
            where = pl.ds(pl.multiple_of(q * ANGLES, 2 * ROWS), ANGLES)
            parts[where, pl.ds(tile * LANES, LANES)] = high
            parts[where, pl.ds(lanes + tile * LANES, LANES)] = low
        return carry

    lax.fori_loop(0, rows[1] - rows[0], rotate, 0)
    result = lax.dot_general(
        jnp.concatenate(member, axis=0), parts[...], NT, preferred_element_type=F32
    )
    for step in range(grp):
        sums[step][...] = result[step * CPAD : (step + 1) * CPAD]


def numerators(images, pieces, tags, arrived, chunk, cols, edges, rows):
    mem, grp = lax.axis_size("mem"), lax.axis_size("grp")
    count = images.shape[0]
    first = chunk == 0
    here = (rows[chunk], rows[chunk + 1])
    base = here[0] * ANGLES // LANES
    stop = min(-(-here[1] * ANGLES // LANES), edges[-1])
    segments, msgs = [], []
    for c in range(chunk + 1):
        low, high = max(edges[c], base), min(edges[c + 1], stop)
        if low < high:
            segments.append((edges[c + 1] - edges[c], low - edges[c], low - base, high - low))
            msgs += arrived[c]
    lanes = mem * count
    span = (here[1] - here[0]) * ANGLES
    tiles = stop - base
    copies = 1 + len(segments) * (mem - 1) * (count // ROWS)
    shapes = [jax.ShapeDtypeStruct((ROWS, lanes), F32)] if first else []
    shapes += [jax.ShapeDtypeStruct((CPAD, span), F32)] * grp
    outs = pl.pallas_call(
        functools.partial(numer_kernel, mem, cols, count, first, here, base, tiles, tuple(segments)),
        out_shape=shapes,
        in_specs=[ANY, VMEM, VMEM] + [ANY] * len(msgs),
        out_specs=[VMEM] * len(shapes),
        scratch_shapes=[
            pltpu.VMEM((lanes, tiles * LANES), BF16),
            pltpu.VMEM((mem, ROWS, LANES), BF16),
            pltpu.VMEM((tiles * LANES, lanes), F32),
            pltpu.VMEM((span, 2 * lanes), BF16),
            pltpu.SemaphoreType.DMA((copies,)),
            pltpu.SemaphoreType.DMA((mem - 1,)),
        ],
        name="numerators",
        **params(40 * lanes * span + 4 * grp * CPAD * lanes * span, 8 * lanes * span),
    )(images, pieces, tags, *msgs)
    if first:
        return outs[0], outs[1:]
    return tags, outs


def denom_kernel(weights, *refs):
    tags, denom = refs[:-1], refs[-1]
    own = lax.axis_index("grp")
    lanes = tags[0].shape[1]
    klass = lax.broadcasted_iota(jnp.int32, (CPAD, lanes), 0)
    pair = lax.broadcasted_iota(jnp.int32, (PAIRS, lanes), 0)
    count = jnp.zeros((CPAD, PAIRS), F32)
    for ref in tags:
        label = ref[...].astype(jnp.int32)
        key = label[0:1] * CPAD + label[1:2]
        member = (klass + CPAD * own == key).astype(BF16)
        which = (pair == label[3:4] * BINS + label[2:3]).astype(BF16)
        count += lax.dot_general(member, which, NT, preferred_element_type=F32)
    high, low = split(count)
    left = jnp.concatenate(
        [jnp.concatenate([high, high], axis=1), jnp.concatenate([low, low], axis=1)], axis=0
    )
    both = lax.dot_general(left, weights[...], NT, preferred_element_type=F32)
    denom[...] = both[:CPAD] + both[CPAD:]


def denominators(weights, tags):
    span = weights.shape[0]
    lanes = tags[0].shape[1]
    return pl.pallas_call(
        denom_kernel,
        out_shape=jax.ShapeDtypeStruct((CPAD, span), F32),
        in_specs=[VMEM] * (1 + len(tags)),
        out_specs=VMEM,
        name="denominators",
        **params(4 * CPAD * span * PAIRS * 2 + len(tags) * lanes * PAIRS * 4, 4 * weights.size),
    )(weights, *tags)


def average_kernel(grp, rows, denom, *refs):
    sums, out = refs[:-1], refs[-1]
    for chunk in range(len(rows) - 1):
        across = pl.ds(rows[chunk] * ANGLES, (rows[chunk + 1] - rows[chunk]) * ANGLES)
        total = sums[chunk * grp][:CPG]
        for step in range(1, grp):
            total += sums[chunk * grp + step][:CPG]
        out[:, across] = total / (denom[:CPG, across] + wiener_term)


def averages(denom, sums, grp, rows):
    span = denom.shape[1]
    return pl.pallas_call(
        functools.partial(average_kernel, grp, rows),
        out_shape=jax.ShapeDtypeStruct((CPG, span), F32),
        in_specs=[VMEM] * (1 + len(sums)),
        out_specs=VMEM,
        name="averages",
        **params(8 * CPG * span, 4 * CPG * span * (grp + 2)),
    )(denom, *sums)


def plan(span):
    turns = span // ANGLES
    tiles = -(-span // LANES)
    edges = [0, tiles // 2, tiles] if tiles % 2 == 0 else [0, tiles]
    rows = [min(edge * LANES // ANGLES, turns) for edge in edges]
    return tuple(edges), tuple(rows)


def on_device(images, classes, rotations, bins, ctf_table):
    mem, grp = lax.axis_size("mem"), lax.axis_size("grp")
    count = images.shape[0]
    span = images.shape[1] // mem
    edges, rows = plan(span)
    cols = edges[-1] * LANES
    ctf = lax.dynamic_slice_in_dim(ctf_table, lax.axis_index("mem") * span, span, 1)
    if cols != span:
        images = jnp.pad(images.reshape(count, mem, span), ((0, 0), (0, 0), (0, cols - span)))
        images = images.reshape(count, mem * cols)
        ctf = jnp.pad(ctf, ((0, 0), (0, cols - span)))
    own_tag, packed = pack(images, classes, rotations, bins, cols, edges)
    arrived = [[send(msg, "mem", step + 1) for step, msg in enumerate(msgs)] for msgs in packed]
    pieces, weights = tables(ctf, span // ANGLES)
    tags, sums = own_tag, []
    for chunk in range(len(edges) - 1):
        tags, here = numerators(images, pieces, tags, arrived, chunk, cols, edges, rows)
        sums += [here[0]] + [send(here[step], "grp", step) for step in range(1, grp)]
    others = [send(tags, "grp", step) for step in range(1, grp)]
    denom = denominators(weights, [tags] + others)
    return averages(denom, sums, grp, rows)


def solution(mesh):
    in_specs = (
        P(("grp", "mem"), None),
        P(("grp", "mem")),
        P(("grp", "mem")),
        P(("grp", "mem")),
        P(),
    )
    out_specs = P("grp", "mem")
    return jax.shard_map(
        on_device, mesh=mesh, in_specs=in_specs, out_specs=out_specs, check_vma=False
    )
```

time: 240 us -> 112 us (0.47)
  blocking collectives: 118 us -> 0 us
  Pallas kernels: 0 us -> 64.1 us
  local copies, waits for them, and re-layouts: 57.7 us -> 2.12 us
  other arithmetic: 21.9 us -> 0 us
  starting transfers between devices: 13.8 us -> 31 us
  matrix products: 16.4 us -> 0 us
  waiting for transfers between devices: 9.98 us -> 14 us
    unnamed x1 -> x0, blocking collectives: 82.7 us -> none
    pallas_call x0 -> x6, Pallas kernels: none -> 64.1 us  [the longest x1 34.3 us: pack(): pl.pallas_call(functools.partial(pack_kernel, size, cols, edges), out_sha...]
    all_gather x1 -> x0, blocking collectives: 35.3 us -> none  [on_device(): tags = lax.all_gather(labels, 'mem', axis=0, tiled=True)]
    concatenate x12 -> x0, local copies, waits for them, and re-layouts: 31.1 us -> none  [rotate(): jnp.concatenate([shaped[:, :, amount:], shaped[:, :, :amount]], axis=2)]
    ppermute x0 -> x23, starting transfers between devices: none -> 31 us  [send(): lax.ppermute(value, axis, [(i, partner(i, step, size)) for i in range(siz...]
    dot_general x3 -> x0, matrix products: 16.4 us -> none  [the longest x1 8.54 us: on_device(): numer = jnp.dot(member, aligned, precision=lax.Precision.HIGHEST)]
    concatenate x9 -> x0, other arithmetic: 16.2 us -> none  [rotate(): jnp.concatenate([shaped[:, :, amount:], shaped[:, :, :amount]], axis=2)]
    ppermute x0 -> x23, waiting for transfers between devices: none -> 14 us  [send(): lax.ppermute(value, axis, [(i, partner(i, step, size)) for i in range(siz...]
  transfers between devices with their start and end apart: 3 -> 23, of which waited for: 2 -> 5; matrix products, arithmetic and copies ran while one was open for 2% -> 1% of each run, Pallas kernels for 0% -> 19%
where the time goes in v1:
time: 112 us
  Pallas kernels  64.1 us (57%)
  starting transfers between devices  31 us (28%)
  waiting for transfers between devices  14 us (12%)
  local copies, waits for them, and re-layouts  2.12 us (2%)
    pallas_call x1, Pallas kernels, pack(): pl.pallas_call(functools.partial(pack_kernel, size, cols, edges), out_sha...  34.3 us
    ppermute x23, starting transfers between devices, send(): lax.ppermute(value, axis, [(i, partner(i, step, size)) for i in range(siz...  31 us
    ppermute x23, waiting for transfers between devices, send(): lax.ppermute(value, axis, [(i, partner(i, step, size)) for i in range(siz...  14 us
    pallas_call x2, Pallas kernels, numerators(): pl.pallas_call(functools.partial(numer_kernel, mem, cols, count, first, h...  12.4 us
    pallas_call x1, Pallas kernels, tables(): pl.pallas_call(functools.partial(table_kernel, turns), out_shape=[jax.Sha...  8.59 us
    pallas_call x1, Pallas kernels, denominators(): pl.pallas_call(denom_kernel, out_shape=jax.ShapeDtypeStruct((CPAD, span),...  6.14 us
    pallas_call x1, Pallas kernels, averages(): pl.pallas_call(functools.partial(average_kernel, grp, rows), out_shape=ja...  2.7 us
  transfers between devices with their start and end apart: 23, of which 5 were waited for; matrix products, arithmetic and copies ran while one was open for 1% of the time, Pallas kernels for 19%

profile of v1, /device:TPU:0, one launch (start us, length us, event | category | flops | bytes accessed | tf_op | source)
XLA Modules:
  0.0 111.5 jit_solution(3429936965548442382)
XLA Ops:
  0.0 34.3 %pack.1 = (bf16[8,128]{1,0:T(8,128)(2,1)}, bf16[8,4736]{1,0:T(8,128)(2,1)}, bf16[8,4736]{1,0:T(8,128)(2,1)}, bf16[8,4736]{1,0:T(8,128)(2,1)}, bf16[8,4736]{1,0:T...) custom-call(bf16[32,18432]{1,0:T(8,128)(2,1)} %refs_0_.3, ...), custom_call_target="tpu_custom_call" | custom-call | flops 65536 | bytes 2359296 | tf_op jit(solution)/shard_map/pack/pallas_call | solution.py:147
  34.3 0.5 collective-permute-start
  34.9 2.6 %collective-permute-start.1 = (bf16[8,4736]{1,0:T(8,128)(2,1)}, bf16[8,4736]{1,0:T(8,128)(2,1)S(1)}, u32[]{:S(2)}, u32[]{:S(2)}) collective-permute-start(bf16[8,4736]{1,0:T(8,128)(2,1)} %get-tuple-element.35), channel_id=1, source_target_pairs={{0,2},{1,3},{2,0},{3,1},{4,6},{5,7},{6,4},{7,5},{8,10},{9,11},{10,... | collective-permute-start | bytes 227336 | tf_op jit(solution)/shard_map/ppermute | solution.py:41
  37.6 2.8 %collective-permute-start.3 = (bf16[8,4736]{1,0:T(8,128)(2,1)}, bf16[8,4736]{1,0:T(8,128)(2,1)S(1)}, u32[]{:S(2)}, u32[]{:S(2)}) collective-permute-start(bf16[8,4736]{1,0:T(8,128)(2,1)} %get-tuple-element.37), channel_id=1, source_target_pairs={{0,4},{1,5},{2,6},{3,7},{4,0},{5,1},{6,2},{7,3},{8,12},{9,13},{10,... | collective-permute-start | bytes 227336 | tf_op jit(solution)/shard_map/ppermute | solution.py:41
  40.3 3.6 %collective-permute-start.5 = (bf16[8,4736]{1,0:T(8,128)(2,1)}, bf16[8,4736]{1,0:T(8,128)(2,1)S(1)}, u32[]{:S(2)}, u32[]{:S(2)}) collective-permute-start(bf16[8,4736]{1,0:T(8,128)(2,1)} %get-tuple-element.39), channel_id=1, source_target_pairs={{0,6},{1,7},{2,4},{3,5},{4,2},{5,3},{6,0},{7,1},{8,14},{9,15},{10,... | collective-permute-start | bytes 227336 | tf_op jit(solution)/shard_map/ppermute | solution.py:41
  44.1 0.7 constant_dynamic-slice_fusion.ctf
  44.7 8.6 %tables.1 = (bf16[2304,48]{1,0:T(8,128)(2,1)}, bf16[2304,1280]{1,0:T(8,128)(2,1)}) custom-call(f32[16,2304]{1,0:T(8,128)} %constant_dynamic-slice_fusion.ctf), custom_call_target="tpu_custom_call" | custom-call | flops 58982400 | bytes 5898240 | tf_op jit(solution)/shard_map/tables/pallas_call | solution.py:205
  53.5 0.5 copy-done.9
  54.2 6.2 %numerators.2 = (f32[8,256]{1,0:T(8,128)}, f32[56,1152]{1,0:T(8,128)}, f32[56,1152]{1,0:T(8,128)}, f32[56,1152]{1,0:T(8,128)}, f32[56,1152]{1,0:T(8,128)}) custom-call(bf16[32,18432]{1,0:T(8,128)(2,1)} %refs_0_.3, bf16[2304,48]{1,0:T(8,128)(2,1)} %get-tuple-element.32.refs_1_, bf16[8,128]{1,0:T(8,128)(2,1)} %get-tuple-element.33.refs_2_, ...), custom_call_target="tpu_custom_call" | custom-call | flops 276037632 | bytes 2359296 | tf_op jit(solution)/shard_map/numerators/pallas_call | solution.py:354
  60.3 1.6 %collective-permute-start.10 = (f32[56,1152]{1,0:T(8,128)}, f32[56,1152]{1,0:T(8,128)S(1)}, u32[]{:S(2)}, u32[]{:S(2)}) collective-permute-start(f32[56,1152]{1,0:T(8,128)} %get-tuple-element.43), channel_id=1, source_target_pairs={{0,8},{8,0},{16,24},{24,16},{1,9},{9,1},{17,25},{25,17},{2,10},{10... | collective-permute-start | bytes 774152 | tf_op jit(solution)/shard_map/ppermute | solution.py:41
  61.9 0.6 collective-permute-start.13
  62.5 2.0 %collective-permute-start.14 = (bf16[8,4608]{1,0:T(8,128)(2,1)S(1)}, bf16[8,4608]{1,0:T(8,128)(2,1)S(1)}, u32[]{:S(2)}, u32[]{:S(2)}) collective-permute-start(bf16[8,4608]{1,0:T(8,128)(2,1)S(1)} %copy-done.30), channel_id=1, source_target_pairs={{0,2},{1,3},{2,0},{3,1},{4,6},{5,7},{6,4},{7,5},{8,10},{9,11},{10,... | collective-permute-start | bytes 221192 | tf_op jit(solution)/shard_map/ppermute | solution.py:41
  64.7 2.7 %collective-permute-start.16 = (bf16[8,4608]{1,0:T(8,128)(2,1)S(1)}, bf16[8,4608]{1,0:T(8,128)(2,1)S(1)}, u32[]{:S(2)}, u32[]{:S(2)}) collective-permute-start(bf16[8,4608]{1,0:T(8,128)(2,1)S(1)} %copy-done.28), channel_id=1, source_target_pairs={{0,4},{1,5},{2,6},{3,7},{4,0},{5,1},{6,2},{7,3},{8,12},{9,13},{10,... | collective-permute-start | bytes 221192 | tf_op jit(solution)/shard_map/ppermute | solution.py:41
  67.5 2.5 %collective-permute-start.18 = (bf16[8,4608]{1,0:T(8,128)(2,1)S(1)}, bf16[8,4608]{1,0:T(8,128)(2,1)S(1)}, u32[]{:S(2)}, u32[]{:S(2)}) collective-permute-start(bf16[8,4608]{1,0:T(8,128)(2,1)S(1)} %copy-done.26), channel_id=1, source_target_pairs={{0,6},{1,7},{2,4},{3,5},{4,2},{5,3},{6,0},{7,1},{8,14},{9,15},{10,... | collective-permute-start | bytes 221192 | tf_op jit(solution)/shard_map/ppermute | solution.py:41
  70.0 0.3 collective-permute-done.15.refs_5_
  70.4 2.5 %collective-permute-start.19 = (bf16[8,4608]{1,0:T(8,128)(2,1)S(1)}, bf16[8,4608]{1,0:T(8,128)(2,1)S(1)}, u32[]{:S(2)}, u32[]{:S(2)}) collective-permute-start(bf16[8,4608]{1,0:T(8,128)(2,1)S(1)} %copy-done.25), channel_id=1, source_target_pairs={{0,7},{1,6},{2,5},{3,4},{4,3},{5,2},{6,1},{7,0},{8,15},{9,14},{10,... | collective-permute-start | bytes 221192 | tf_op jit(solution)/shard_map/ppermute | solution.py:41
  72.9 0.5 collective-permute-start.7
  73.4 5.4 %collective-permute-done.17.refs_7_ = bf16[8,4608]{1,0:T(8,128)(2,1)S(1)} collective-permute-done((bf16[8,4608]{1,0:T(8,128)(2,1)S(1)}, bf16[8,4608]{1,0:T(8,128)(2,1)S(1)}, u32[]{:S(2)}, u32[]{:S(2)}) %collective-permute-start.17) | collective-permute-done | bytes 73760 | tf_op jit(solution)/shard_map/ppermute | solution.py:41
  78.8 1.5 %collective-permute-start.8 = (f32[8,256]{1,0:T(8,128)}, f32[8,256]{1,0:T(8,128)S(1)}, u32[]{:S(2)}, u32[]{:S(2)}) collective-permute-start(f32[8,256]{1,0:T(8,128)} %get-tuple-element.41.refs_0_.refs_2_), channel_id=1, source_target_pairs={{0,16},{8,24},{16,0},{24,8},{1,17},{9,25},{17,1},{25,9},{2,18},{10... | collective-permute-start | bytes 24584 | tf_op jit(solution)/shard_map/ppermute | solution.py:41
  80.3 0.5 collective-permute-start.9
  80.8 1.5 %collective-permute-start.11 = (f32[56,1152]{1,0:T(8,128)}, f32[56,1152]{1,0:T(8,128)S(1)}, u32[]{:S(2)}, u32[]{:S(2)}) collective-permute-start(f32[56,1152]{1,0:T(8,128)} %get-tuple-element.44), channel_id=1, source_target_pairs={{0,16},{8,24},{16,0},{24,8},{1,17},{9,25},{17,1},{25,9},{2,18},{10... | collective-permute-start | bytes 774152 | tf_op jit(solution)/shard_map/ppermute | solution.py:41
  82.4 6.2 %numerators.3 = (f32[56,1152]{1,0:T(8,128)}, f32[56,1152]{1,0:T(8,128)}, f32[56,1152]{1,0:T(8,128)}, f32[56,1152]{1,0:T(8,128)}) custom-call(bf16[32,18432]{1,0:T(8,128)(2,1)} %refs_0_.3, bf16[2304,48]{1,0:T(8,128)(2,1)} %get-tuple-element.32.refs_1_, f32[8,256]{1,0:T(8,128)} %get-tuple-element.41.refs_0_.refs_2_, bf16[8,4608]{1,0:T(8,128)(2,1)} %copy-done.14, ...), custom_call_target="tpu_custom_call" | custom-call | flops 276037632 | bytes 2359296 | tf_op jit(solution)/shard_map/numerators/pallas_call | solution.py:354
  88.6 1.6 %collective-permute-start.12 = (f32[56,1152]{1,0:T(8,128)S(1)}, f32[56,1152]{1,0:T(8,128)S(1)}, u32[]{:S(2)}, u32[]{:S(2)}) collective-permute-start(f32[56,1152]{1,0:T(8,128)S(1)} %copy-done.24), channel_id=1, source_target_pairs={{0,24},{8,16},{16,8},{24,0},{1,25},{9,17},{17,9},{25,1},{2,26},{10... | collective-permute-start | bytes 774152 | tf_op jit(solution)/shard_map/ppermute | solution.py:41
  90.2 0.5 collective-permute-start.20
  90.7 1.5 %collective-permute-start.21 = (f32[56,1152]{1,0:T(8,128)}, f32[56,1152]{1,0:T(8,128)S(1)}, u32[]{:S(2)}, u32[]{:S(2)}) collective-permute-start(f32[56,1152]{1,0:T(8,128)} %get-tuple-element.55), channel_id=1, source_target_pairs={{0,16},{8,24},{16,0},{24,8},{1,17},{9,25},{17,1},{25,9},{2,18},{10... | collective-permute-start | bytes 774152 | tf_op jit(solution)/shard_map/ppermute | solution.py:41
  92.2 1.5 %collective-permute-start.22 = (f32[56,1152]{1,0:T(8,128)}, f32[56,1152]{1,0:T(8,128)S(1)}, u32[]{:S(2)}, u32[]{:S(2)}) collective-permute-start(f32[56,1152]{1,0:T(8,128)} %get-tuple-element.56), channel_id=1, source_target_pairs={{0,24},{8,16},{16,8},{24,0},{1,25},{9,17},{17,9},{25,1},{2,26},{10... | collective-permute-start | bytes 774152 | tf_op jit(solution)/shard_map/ppermute | solution.py:41
  93.7 6.1 %denominators.1.denom = f32[56,2304]{1,0:T(8,128)} custom-call(bf16[2304,1280]{1,0:T(8,128)(2,1)} %get-tuple-element.31.weights, f32[8,256]{1,0:T(8,128)} %get-tuple-element.41.refs_0_.refs_2_, f32[8,256]{1,0:T(8,128)} %copy-done.21, f32[8,256]{1,0:T(8,128)} %copy-done.22, f32[8,256]{1,0:T(8,128)} %copy-done.23), custom_call_target="tpu_custom_call" | custom-call | flops 663224320 | bytes 11796480 | tf_op jit(solution)/shard_map/denominators/pallas_call | solution.py:399
  99.9 3.5 %collective-permute-done.20.refs_5_ = f32[56,1152]{1,0:T(8,128)S(1)} collective-permute-done((f32[56,1152]{1,0:T(8,128)}, f32[56,1152]{1,0:T(8,128)S(1)}, u32[]{:S(2)}, u32[]{:S(2)}) %collective-permute-start.20) | collective-permute-done | bytes 258080 | tf_op jit(solution)/shard_map/ppermute | solution.py:41
  103.4 0.8 collective-permute-done.21.refs_6_
  104.2 3.9 %collective-permute-done.22.refs_7_ = f32[56,1152]{1,0:T(8,128)S(1)} collective-permute-done((f32[56,1152]{1,0:T(8,128)}, f32[56,1152]{1,0:T(8,128)S(1)}, u32[]{:S(2)}, u32[]{:S(2)}) %collective-permute-start.22) | collective-permute-done | bytes 258080 | tf_op jit(solution)/shard_map/ppermute | solution.py:41
  108.1 0.7 copy-done.6
  108.8 2.7 %averages.1 = f32[50,2304]{1,0:T(8,128)} custom-call(f32[56,2304]{1,0:T(8,128)} %denominators.1.denom, f32[56,1152]{1,0:T(8,128)} %get-tuple-element.42.refs_0_, f32[56,1152]{1,0:T(8,128)} %copy-done.1, f32[56,1152]{1,0:T(8,128)} %copy-done.2, f32[56,1152]{1,0:T(8,128)} %copy-done.3, f32[56,1152]{1,0:T(8,128)} %get-tuple-element.53.refs_4_, ...), custom_call_target="tpu_custom_call" | custom-call | flops 921600 | bytes 2764800 | tf_op jit(solution)/shard_map/averages/pallas_call | solution.py:421
  (85 shorter events, 0.7 us)
Async XLA Ops:
  0.0 44.1 %copy-start = (f32[16,18432]{1,0:T(8,128)S(1)}, f32[16,18432]{1,0:T(8,128)}, u32[]{:S(2)}) copy-start(f32[16,18432]{1,0:T(8,128)} %param.9) | copy-start | bytes 3538948
  34.3 6.0 %collective-permute-start = (bf16[8,4736]{1,0:T(8,128)(2,1)}, bf16[8,4736]{1,0:T(8,128)(2,1)S(1)}, u32[]{:S(2)}, u32[]{:S(2)}) collective-permute-start(bf16[8,4736]{1,0:T(8,128)(2,1)} %get-tuple-element.34), channel_id=1, source_target_pairs={{0,1},{1,0},{2,3},{3,2},{4,5},{5,4},{6,7},{7,6},{8,9},{9,8},{10,11... | collective-permute-start | bytes 227336 | tf_op jit(solution)/shard_map/ppermute | solution.py:41
  34.9 9.1 %collective-permute-start.1 = (bf16[8,4736]{1,0:T(8,128)(2,1)}, bf16[8,4736]{1,0:T(8,128)(2,1)S(1)}, u32[]{:S(2)}, u32[]{:S(2)}) collective-permute-start(bf16[8,4736]{1,0:T(8,128)(2,1)} %get-tuple-element.35), channel_id=1, source_target_pairs={{0,2},{1,3},{2,0},{3,1},{4,6},{5,7},{6,4},{7,5},{8,10},{9,11},{10,... | collective-permute-start | bytes 227336 | tf_op jit(solution)/shard_map/ppermute | solution.py:41
  37.5 15.9 %collective-permute-start.2 = (bf16[8,4736]{1,0:T(8,128)(2,1)}, bf16[8,4736]{1,0:T(8,128)(2,1)S(1)}, u32[]{:S(2)}, u32[]{:S(2)}) collective-permute-start(bf16[8,4736]{1,0:T(8,128)(2,1)} %get-tuple-element.36), channel_id=1, source_target_pairs={{0,3},{1,2},{2,1},{3,0},{4,7},{5,6},{6,5},{7,4},{8,11},{9,10},{10,... | collective-permute-start | bytes 227336 | tf_op jit(solution)/shard_map/ppermute | solution.py:41
  37.6 15.8 %collective-permute-start.3 = (bf16[8,4736]{1,0:T(8,128)(2,1)}, bf16[8,4736]{1,0:T(8,128)(2,1)S(1)}, u32[]{:S(2)}, u32[]{:S(2)}) collective-permute-start(bf16[8,4736]{1,0:T(8,128)(2,1)} %get-tuple-element.37), channel_id=1, source_target_pairs={{0,4},{1,5},{2,6},{3,7},{4,0},{5,1},{6,2},{7,3},{8,12},{9,13},{10,... | collective-permute-start | bytes 227336 | tf_op jit(solution)/shard_map/ppermute | solution.py:41
  40.3 13.1 %collective-permute-start.4 = (bf16[8,4736]{1,0:T(8,128)(2,1)}, bf16[8,4736]{1,0:T(8,128)(2,1)S(1)}, u32[]{:S(2)}, u32[]{:S(2)}) collective-permute-start(bf16[8,4736]{1,0:T(8,128)(2,1)} %get-tuple-element.38), channel_id=1, source_target_pairs={{0,5},{1,4},{2,7},{3,6},{4,1},{5,0},{6,3},{7,2},{8,13},{9,12},{10,... | collective-permute-start | bytes 227336 | tf_op jit(solution)/shard_map/ppermute | solution.py:41
  40.3 13.1 %copy-start.7 = (bf16[8,4736]{1,0:T(8,128)(2,1)}, bf16[8,4736]{1,0:T(8,128)(2,1)S(1)}, u32[]{:S(2)}) copy-start(bf16[8,4736]{1,0:T(8,128)(2,1)S(1)} %collective-permute-done.refs_3_) | copy-start | bytes 227332
  40.3 13.1 %collective-permute-start.5 = (bf16[8,4736]{1,0:T(8,128)(2,1)}, bf16[8,4736]{1,0:T(8,128)(2,1)S(1)}, u32[]{:S(2)}, u32[]{:S(2)}) collective-permute-start(bf16[8,4736]{1,0:T(8,128)(2,1)} %get-tuple-element.39), channel_id=1, source_target_pairs={{0,6},{1,7},{2,4},{3,5},{4,2},{5,3},{6,0},{7,1},{8,14},{9,15},{10,... | collective-permute-start | bytes 227336 | tf_op jit(solution)/shard_map/ppermute | solution.py:41
  43.9 9.5 %collective-permute-start.6 = (bf16[8,4736]{1,0:T(8,128)(2,1)}, bf16[8,4736]{1,0:T(8,128)(2,1)S(1)}, u32[]{:S(2)}, u32[]{:S(2)}) collective-permute-start(bf16[8,4736]{1,0:T(8,128)(2,1)} %get-tuple-element.40), channel_id=1, source_target_pairs={{0,7},{1,6},{2,5},{3,4},{4,3},{5,2},{6,1},{7,0},{8,15},{9,14},{10,... | collective-permute-start | bytes 227336 | tf_op jit(solution)/shard_map/ppermute | solution.py:41
  53.3 14.0 %copy-start.27 = (bf16[8,4608]{1,0:T(8,128)(2,1)S(1)}, bf16[8,4608]{1,0:T(8,128)(2,1)}, u32[]{:S(2)}) copy-start(bf16[8,4608]{1,0:T(8,128)(2,1)} %get-tuple-element.50) | copy-start | bytes 221188
  53.3 14.1 %copy-start.26 = (bf16[8,4608]{1,0:T(8,128)(2,1)S(1)}, bf16[8,4608]{1,0:T(8,128)(2,1)}, u32[]{:S(2)}) copy-start(bf16[8,4608]{1,0:T(8,128)(2,1)} %get-tuple-element.51) | copy-start | bytes 221188
  53.4 17.0 %copy-start.25 = (bf16[8,4608]{1,0:T(8,128)(2,1)S(1)}, bf16[8,4608]{1,0:T(8,128)(2,1)}, u32[]{:S(2)}) copy-start(bf16[8,4608]{1,0:T(8,128)(2,1)} %get-tuple-element.52) | copy-start | bytes 221188
  60.3 28.3 %copy-start.24 = (f32[56,1152]{1,0:T(8,128)S(1)}, f32[56,1152]{1,0:T(8,128)}, u32[]{:S(2)}) copy-start(f32[56,1152]{1,0:T(8,128)} %get-tuple-element.45) | copy-start | bytes 774148
  60.3 31.9 %collective-permute-start.10 = (f32[56,1152]{1,0:T(8,128)}, f32[56,1152]{1,0:T(8,128)S(1)}, u32[]{:S(2)}, u32[]{:S(2)}) collective-permute-start(f32[56,1152]{1,0:T(8,128)} %get-tuple-element.43), channel_id=1, source_target_pairs={{0,8},{8,0},{16,24},{24,16},{1,9},{9,1},{17,25},{25,17},{2,10},{10... | collective-permute-start | bytes 774152 | tf_op jit(solution)/shard_map/ppermute | solution.py:41
  61.9 5.5 %collective-permute-start.13 = (bf16[8,4608]{1,0:T(8,128)(2,1)S(1)}, bf16[8,4608]{1,0:T(8,128)(2,1)S(1)}, u32[]{:S(2)}, u32[]{:S(2)}) collective-permute-start(bf16[8,4608]{1,0:T(8,128)(2,1)S(1)} %copy-done.31), channel_id=1, source_target_pairs={{0,1},{1,0},{2,3},{3,2},{4,5},{5,4},{6,7},{7,6},{8,9},{9,8},{10,11... | collective-permute-start | bytes 221192 | tf_op jit(solution)/shard_map/ppermute | solution.py:41
  62.5 5.0 %collective-permute-start.14 = (bf16[8,4608]{1,0:T(8,128)(2,1)S(1)}, bf16[8,4608]{1,0:T(8,128)(2,1)S(1)}, u32[]{:S(2)}, u32[]{:S(2)}) collective-permute-start(bf16[8,4608]{1,0:T(8,128)(2,1)S(1)} %copy-done.30), channel_id=1, source_target_pairs={{0,2},{1,3},{2,0},{3,1},{4,6},{5,7},{6,4},{7,5},{8,10},{9,11},{10,... | collective-permute-start | bytes 221192 | tf_op jit(solution)/shard_map/ppermute | solution.py:41
  64.6 5.8 %collective-permute-start.15 = (bf16[8,4608]{1,0:T(8,128)(2,1)S(1)}, bf16[8,4608]{1,0:T(8,128)(2,1)S(1)}, u32[]{:S(2)}, u32[]{:S(2)}) collective-permute-start(bf16[8,4608]{1,0:T(8,128)(2,1)S(1)} %copy-done.29), channel_id=1, source_target_pairs={{0,3},{1,2},{2,1},{3,0},{4,7},{5,6},{6,5},{7,4},{8,11},{9,10},{10,... | collective-permute-start | bytes 221192 | tf_op jit(solution)/shard_map/ppermute | solution.py:41
  64.7 8.2 %collective-permute-start.16 = (bf16[8,4608]{1,0:T(8,128)(2,1)S(1)}, bf16[8,4608]{1,0:T(8,128)(2,1)S(1)}, u32[]{:S(2)}, u32[]{:S(2)}) collective-permute-start(bf16[8,4608]{1,0:T(8,128)(2,1)S(1)} %copy-done.28), channel_id=1, source_target_pairs={{0,4},{1,5},{2,6},{3,7},{4,0},{5,1},{6,2},{7,3},{8,12},{9,13},{10,... | collective-permute-start | bytes 221192 | tf_op jit(solution)/shard_map/ppermute | solution.py:41
  67.4 15.0 %copy-start.14 = (bf16[8,4608]{1,0:T(8,128)(2,1)}, bf16[8,4608]{1,0:T(8,128)(2,1)S(1)}, u32[]{:S(2)}) copy-start(bf16[8,4608]{1,0:T(8,128)(2,1)S(1)} %collective-permute-done.13.refs_3_) | copy-start | bytes 221188
  67.4 11.4 %collective-permute-start.17 = (bf16[8,4608]{1,0:T(8,128)(2,1)S(1)}, bf16[8,4608]{1,0:T(8,128)(2,1)S(1)}, u32[]{:S(2)}, u32[]{:S(2)}) collective-permute-start(bf16[8,4608]{1,0:T(8,128)(2,1)S(1)} %copy-done.27), channel_id=1, source_target_pairs={{0,5},{1,4},{2,7},{3,6},{4,1},{5,0},{6,3},{7,2},{8,13},{9,12},{10,... | collective-permute-start | bytes 221192 | tf_op jit(solution)/shard_map/ppermute | solution.py:41
  67.5 14.9 %copy-start.15 = (bf16[8,4608]{1,0:T(8,128)(2,1)}, bf16[8,4608]{1,0:T(8,128)(2,1)S(1)}, u32[]{:S(2)}) copy-start(bf16[8,4608]{1,0:T(8,128)(2,1)S(1)} %collective-permute-done.14.refs_4_) | copy-start | bytes 221188
  67.5 12.8 %collective-permute-start.18 = (bf16[8,4608]{1,0:T(8,128)(2,1)S(1)}, bf16[8,4608]{1,0:T(8,128)(2,1)S(1)}, u32[]{:S(2)}, u32[]{:S(2)}) collective-permute-start(bf16[8,4608]{1,0:T(8,128)(2,1)S(1)} %copy-done.26), channel_id=1, source_target_pairs={{0,6},{1,7},{2,4},{3,5},{4,2},{5,3},{6,0},{7,1},{8,14},{9,15},{10,... | collective-permute-start | bytes 221192 | tf_op jit(solution)/shard_map/ppermute | solution.py:41
  70.4 12.0 %copy-start.16 = (bf16[8,4608]{1,0:T(8,128)(2,1)}, bf16[8,4608]{1,0:T(8,128)(2,1)S(1)}, u32[]{:S(2)}) copy-start(bf16[8,4608]{1,0:T(8,128)(2,1)S(1)} %collective-permute-done.15.refs_5_) | copy-start | bytes 221188
  70.4 10.5 %collective-permute-start.19 = (bf16[8,4608]{1,0:T(8,128)(2,1)S(1)}, bf16[8,4608]{1,0:T(8,128)(2,1)S(1)}, u32[]{:S(2)}, u32[]{:S(2)}) collective-permute-start(bf16[8,4608]{1,0:T(8,128)(2,1)S(1)} %copy-done.25), channel_id=1, source_target_pairs={{0,7},{1,6},{2,5},{3,4},{4,3},{5,2},{6,1},{7,0},{8,15},{9,14},{10,... | collective-permute-start | bytes 221192 | tf_op jit(solution)/shard_map/ppermute | solution.py:41
  72.9 15.7 %collective-permute-start.7 = (f32[8,256]{1,0:T(8,128)}, f32[8,256]{1,0:T(8,128)S(1)}, u32[]{:S(2)}, u32[]{:S(2)}) collective-permute-start(f32[8,256]{1,0:T(8,128)} %get-tuple-element.41.refs_0_.refs_2_), channel_id=1, source_target_pairs={{0,8},{8,0},{16,24},{24,16},{1,9},{9,1},{17,25},{25,17},{2,10},{10... | collective-permute-start | bytes 24584 | tf_op jit(solution)/shard_map/ppermute | solution.py:41
  78.8 11.4 %collective-permute-start.8 = (f32[8,256]{1,0:T(8,128)}, f32[8,256]{1,0:T(8,128)S(1)}, u32[]{:S(2)}, u32[]{:S(2)}) collective-permute-start(f32[8,256]{1,0:T(8,128)} %get-tuple-element.41.refs_0_.refs_2_), channel_id=1, source_target_pairs={{0,16},{8,24},{16,0},{24,8},{1,17},{9,25},{17,1},{25,9},{2,18},{10... | collective-permute-start | bytes 24584 | tf_op jit(solution)/shard_map/ppermute | solution.py:41
  80.3 10.4 %collective-permute-start.9 = (f32[8,256]{1,0:T(8,128)}, f32[8,256]{1,0:T(8,128)S(1)}, u32[]{:S(2)}, u32[]{:S(2)}) collective-permute-start(f32[8,256]{1,0:T(8,128)} %get-tuple-element.41.refs_0_.refs_2_), channel_id=1, source_target_pairs={{0,24},{8,16},{16,8},{24,0},{1,25},{9,17},{17,9},{25,1},{2,26},{10... | collective-permute-start | bytes 24584 | tf_op jit(solution)/shard_map/ppermute | solution.py:41
  80.8 19.0 %collective-permute-start.11 = (f32[56,1152]{1,0:T(8,128)}, f32[56,1152]{1,0:T(8,128)S(1)}, u32[]{:S(2)}, u32[]{:S(2)}) collective-permute-start(f32[56,1152]{1,0:T(8,128)} %get-tuple-element.44), channel_id=1, source_target_pairs={{0,16},{8,24},{16,0},{24,8},{1,17},{9,25},{17,1},{25,9},{2,18},{10... | collective-permute-start | bytes 774152 | tf_op jit(solution)/shard_map/ppermute | solution.py:41
  88.6 11.2 %collective-permute-start.12 = (f32[56,1152]{1,0:T(8,128)S(1)}, f32[56,1152]{1,0:T(8,128)S(1)}, u32[]{:S(2)}, u32[]{:S(2)}) collective-permute-start(f32[56,1152]{1,0:T(8,128)S(1)} %copy-done.24), channel_id=1, source_target_pairs={{0,24},{8,16},{16,8},{24,0},{1,25},{9,17},{17,9},{25,1},{2,26},{10... | collective-permute-start | bytes 774152 | tf_op jit(solution)/shard_map/ppermute | solution.py:41
  90.2 13.2 %collective-permute-start.20 = (f32[56,1152]{1,0:T(8,128)}, f32[56,1152]{1,0:T(8,128)S(1)}, u32[]{:S(2)}, u32[]{:S(2)}) collective-permute-start(f32[56,1152]{1,0:T(8,128)} %get-tuple-element.54), channel_id=1, source_target_pairs={{0,8},{8,0},{16,24},{24,16},{1,9},{9,1},{17,25},{25,17},{2,10},{10... | collective-permute-start | bytes 774152 | tf_op jit(solution)/shard_map/ppermute | solution.py:41
  90.7 13.5 %collective-permute-start.21 = (f32[56,1152]{1,0:T(8,128)}, f32[56,1152]{1,0:T(8,128)S(1)}, u32[]{:S(2)}, u32[]{:S(2)}) collective-permute-start(f32[56,1152]{1,0:T(8,128)} %get-tuple-element.55), channel_id=1, source_target_pairs={{0,16},{8,24},{16,0},{24,8},{1,17},{9,25},{17,1},{25,9},{2,18},{10... | collective-permute-start | bytes 774152 | tf_op jit(solution)/shard_map/ppermute | solution.py:41
  92.2 15.9 %collective-permute-start.22 = (f32[56,1152]{1,0:T(8,128)}, f32[56,1152]{1,0:T(8,128)S(1)}, u32[]{:S(2)}, u32[]{:S(2)}) collective-permute-start(f32[56,1152]{1,0:T(8,128)} %get-tuple-element.56), channel_id=1, source_target_pairs={{0,24},{8,16},{16,8},{24,0},{1,25},{9,17},{17,9},{25,1},{2,26},{10... | collective-permute-start | bytes 774152 | tf_op jit(solution)/shard_map/ppermute | solution.py:41
  (23 other events, 114.7 us)

commit v2 on v1

v2 whole, which is shorter than its diff:
```python
import functools

import jax
import jax.numpy as jnp
from jax import lax
from jax.experimental import pallas as pl
from jax.experimental.pallas import tpu as pltpu
from jax.sharding import PartitionSpec as P

ANGLES = 144
ROTS = 36
BINS = 16
CPG = 50
SHIFT = 4

LANES = 128
ROWS = 8
CORES = 2
CPAD = -(-CPG // ROWS) * ROWS
PIECES = 3
NEAR = LANES // BINS
PAIRS = -(-ROTS // NEAR) * LANES
LEVELS = max(ROTS - 1, 1).bit_length()

wiener_term = 1.0

F32 = jnp.float32
BF16 = jnp.bfloat16
NT = (((1,), (1,)), ((), ()))
ANY = pl.BlockSpec(memory_space=pl.ANY)
HBM = pl.BlockSpec(memory_space=pltpu.HBM)
VMEM = pl.BlockSpec(memory_space=pltpu.VMEM)


def partner(index, step, size):
    if size & (size - 1) == 0:
        return index ^ step
    return lax.rem(index + step, size) if not isinstance(index, int) else (index + step) % size


def send(value, axis, step, cores=1):
    size = lax.axis_size(axis) // cores
    pairs = [
        (i * cores + core, partner(i, step, size) * cores + core)
        for i in range(size)
        for core in range(cores)
    ]
    return lax.ppermute(value, axis, pairs)


def swap(value, axis):
    return lax.ppermute(value, axis, [(i, i ^ 1) for i in range(lax.axis_size(axis))])


def identity():
    rows = lax.broadcasted_iota(jnp.int32, (LANES, LANES), 0)
    cols = lax.broadcasted_iota(jnp.int32, (LANES, LANES), 1)
    return (rows == cols).astype(BF16)


def turned(block, amount):
    amount %= ANGLES
    if amount == 0:
        return block
    if amount % ROWS == 0:
        return jnp.concatenate([block[amount:], block[:amount]], axis=0)
    return pltpu.roll(block, ANGLES - amount, 0)


def split(value):
    high = value.astype(BF16)
    low = (value - high.astype(F32)).astype(BF16)
    return high, low


def params(mebibytes):
    return dict(
        compiler_params=pltpu.CompilerParams(vmem_limit_bytes=mebibytes << 20),
        cost_estimate=pl.CostEstimate(flops=1 << 20, bytes_accessed=1 << 16, transcendentals=0),
    )


def run(copies, sems):
    copies = [
        pltpu.make_async_copy(src, dst, sems.at[spot]) for spot, (src, dst) in enumerate(copies)
    ]
    for copy in copies:
        copy.start()
    return copies


def pack_first_kernel(mem, cols, width, img, labels, *refs):
    places = mem // CORES
    outs, (data, sems) = refs[:places], refs[places:]
    count = data.shape[0]
    groups = count // ROWS
    here = lax.axis_index("mem") // CORES
    copies = run(
        [
            (img.at[:, pl.ds(dest * cols, width)], data.at[:, pl.ds(dest * width, width)])
            for dest in range(mem)
        ],
        sems,
    )
    label = labels[0:1]
    owner = jnp.zeros_like(label)
    for g in range(1, lax.axis_size("grp")):
        owner += (label >= g * CPG).astype(jnp.int32)
    row = lax.broadcasted_iota(jnp.int32, (ROWS, count), 0)
    stack = jnp.where(
        row == 0,
        owner,
        jnp.where(
            row == 1,
            label - owner * CPG,
            jnp.where(row == 2, labels[1:2], jnp.where(row == 3, labels[2:3], 0)),
        ),
    )
    spread = (
        lax.broadcasted_iota(jnp.int32, (count, LANES), 1) % count
        == lax.broadcasted_iota(jnp.int32, (count, LANES), 0)
    ).astype(BF16)
    tags = jnp.dot(stack.astype(F32).astype(BF16), spread, preferred_element_type=F32)
    place = lax.broadcasted_iota(jnp.int32, (ROWS, LANES), 1) // count
    for step in range(places):
        mine = jnp.where(place == step % (LANES // count), tags, 0.0)
        outs[step][:, pl.ds(CORES * groups * width, LANES)] = mine.astype(BF16)
    for copy in copies:
        copy.wait()
    for step in range(places):
        dest = partner(here, step, places) * CORES
        for core in range(CORES):
            start = pl.multiple_of((dest + core) * width, LANES)
            for g in range(groups):
                outs[step][:, pl.ds((core * groups + g) * width, width)] = data[
                    pl.ds(g * ROWS, ROWS), pl.ds(start, width)
                ]


def pack_first(images, classes, rotations, bins, cols, edges):
    mem = lax.axis_size("mem")
    count = images.shape[0]
    width = edges[1] * LANES
    shape = jax.ShapeDtypeStruct((ROWS, CORES * (count // ROWS) * width + LANES), BF16)
    return pl.pallas_call(
        functools.partial(pack_first_kernel, mem, cols, width),
        out_shape=[shape] * (mem // CORES),
        in_specs=[HBM, VMEM],
        out_specs=[VMEM] * (mem // CORES),
        scratch_shapes=[
            pltpu.VMEM((count, mem * width), BF16),
            pltpu.SemaphoreType.DMA((mem,)),
        ],
        name="pack_first",
        **params(8),
    )(images, jnp.stack([classes, bins, rotations]))


def cross_first_kernel(places, *refs):
    blocks, out = refs[:places], refs[-1]
    other = 1 - lax.rem(lax.axis_index("mem"), CORES)
    span = (blocks[0].shape[1] - LANES) // CORES
    for step, block in enumerate(blocks):
        out[step, :, pl.ds(0, span)] = block[:, pl.ds(pl.multiple_of(other * span, LANES), span)]
        out[step, :, pl.ds(span, LANES)] = block[:, pl.ds(CORES * span, LANES)]


def cross_first(blocks, after):
    span = (blocks[0].shape[1] - LANES) // CORES
    return pl.pallas_call(
        functools.partial(cross_first_kernel, len(blocks)),
        out_shape=jax.ShapeDtypeStruct((len(blocks), ROWS, span + LANES), BF16),
        in_specs=[VMEM] * len(blocks) + [ANY] * len(after),
        out_specs=VMEM,
        name="cross_first",
        **params(8),
    )(*blocks, *after)


def cross_later_kernel(mem, cols, low, width, img, out, data, sems):
    groups = data.shape[0] // ROWS
    places = mem // CORES
    here = lax.axis_index("mem") // CORES
    other = 1 - lax.rem(lax.axis_index("mem"), CORES)
    copies = []
    for step in range(places):
        dest = partner(here, step, places) * CORES + other
        start = pl.multiple_of(dest * cols + low, LANES)
        copies.append((img.at[:, pl.ds(start, width)], data.at[:, pl.ds(step * width, width)]))
    for step, copy in enumerate(run(copies, sems)):
        copy.wait()
        for g in range(groups):
            out[step, :, pl.ds(g * width, width)] = data[
                pl.ds(g * ROWS, ROWS), pl.ds(step * width, width)
            ]


def cross_later(images, cols, low, high):
    mem = lax.axis_size("mem")
    count = images.shape[0]
    width = (high - low) * LANES
    return pl.pallas_call(
        functools.partial(cross_later_kernel, mem, cols, low * LANES, width),
        out_shape=jax.ShapeDtypeStruct((mem // CORES, ROWS, count // ROWS * width), BF16),
        in_specs=[HBM],
        out_specs=VMEM,
        scratch_shapes=[
            pltpu.VMEM((count, mem // CORES * width), BF16),
            pltpu.SemaphoreType.DMA((mem // CORES,)),
        ],
        name="cross_later",
        **params(8),
    )(images)


def pack_later_kernel(mem, cols, low, width, img, crossed, after, *refs):
    places = mem // CORES
    outs, (data, sems) = refs[:places], refs[places:]
    groups = data.shape[0] // ROWS
    me = lax.axis_index("mem")
    here, core = me // CORES, lax.rem(me, CORES)
    copies = []
    for step in range(places):
        dest = partner(here, step, places) * CORES + core
        start = pl.multiple_of(dest * cols + low, LANES)
        copies.append((img.at[:, pl.ds(start, width)], data.at[:, pl.ds(step * width, width)]))
    copies = run(copies, sems)
    for step in range(places):
        outs[step][:, pl.ds(groups * width, groups * width)] = crossed[step]
    for step, copy in enumerate(copies):
        copy.wait()
        for g in range(groups):
            outs[step][:, pl.ds(g * width, width)] = data[
                pl.ds(g * ROWS, ROWS), pl.ds(step * width, width)
            ]


def pack_later(images, crossed, after, cols, low, high):
    mem = lax.axis_size("mem")
    places = mem // CORES
    count = images.shape[0]
    width = (high - low) * LANES
    shape = jax.ShapeDtypeStruct((ROWS, CORES * (count // ROWS) * width), BF16)
    return pl.pallas_call(
        functools.partial(pack_later_kernel, mem, cols, low * LANES, width),
        out_shape=[shape] * places,
        in_specs=[HBM, VMEM, ANY],
        out_specs=[VMEM] * places,
        scratch_shapes=[
            pltpu.VMEM((count, places * width), BF16),
            pltpu.SemaphoreType.DMA((places,)),
        ],
        name="pack_later",
        **params(8),
    )(images, crossed, after)


def table_kernel(turns, table, pieces, weights, ctf, square, sem):
    cols = ctf.shape[1]
    start = 0
    if table.shape[1] != cols:
        start = pl.multiple_of(lax.axis_index("mem") * cols, LANES)
    copy = pltpu.make_async_copy(table.at[:, pl.ds(start, cols)], ctf, sem)
    copy.start()
    copy.wait()
    value = ctf[...]
    high = value.astype(BF16).astype(F32)
    mid = (value - high).astype(BF16).astype(F32)
    low = value - high - mid
    stacked = jnp.concatenate([high, mid, low], axis=0).astype(BF16)
    eye = identity()
    pick = (
        lax.broadcasted_iota(jnp.int32, (PIECES * BINS, LANES), 0) % BINS
        == lax.broadcasted_iota(jnp.int32, (PIECES * BINS, LANES), 1) % BINS
    ).astype(BF16)
    for tile in range(cols // LANES):
        rows = pl.ds(tile * LANES, LANES)
        flipped = lax.dot_general(
            eye, stacked[:, tile * LANES : (tile + 1) * LANES], NT, preferred_element_type=F32
        ).astype(BF16)
        pieces[rows, :] = flipped
        spread = jnp.dot(flipped, pick, preferred_element_type=F32)
        square[rows, :] = spread * spread
    turn = lax.broadcasted_iota(jnp.int32, (1, LANES), 1) // BINS
    levels = max(NEAR - 1, 1).bit_length()

    def one(q, carry):
        rows = pl.ds(pl.multiple_of(q * ANGLES, 2 * ROWS), ANGLES)
        block = square[rows, :]
        for level in range(levels):
            chosen = (turn >> level & 1) == 1
            block = jnp.where(chosen, turned(block, SHIFT << level), block)
        high, low = split(block)
        weights[rows, pl.ds(0, LANES)] = high
        weights[rows, pl.ds(LANES, LANES)] = low
        return carry

    lax.fori_loop(0, turns, one, 0, unroll=2)


def tables(table, cols, turns):
    return pl.pallas_call(
        functools.partial(table_kernel, turns),
        out_shape=[
            jax.ShapeDtypeStruct((cols, PIECES * BINS), BF16),
            jax.ShapeDtypeStruct((turns * ANGLES, 2 * LANES), BF16),
        ],
        in_specs=[HBM],
        out_specs=[VMEM, VMEM],
        scratch_shapes=[
            pltpu.VMEM((BINS, cols), F32),
            pltpu.VMEM((cols, LANES), F32),
            pltpu.SemaphoreType.DMA,
        ],
        name="tables",
        **params(8),
    )(table)


def tag_spots(lanes, span):
    wide = span // LANES * LANES
    parts = -(-lanes // wide)
    spots = []
    for kind in range(3):
        for part in range(parts):
            spots.append((kind, CPG + kind * parts + part, part * wide, min(wide, lanes - part * wide)))
    return spots


def sum_rows(lanes, span):
    last = tag_spots(lanes, span)[-1][1] + 1
    return -(-last // ROWS) * ROWS


def read_tags(ref, lanes):
    kinds = [[], [], []]
    for kind, row, _, width in tag_spots(lanes, ref.shape[1]):
        kinds[kind].append(ref[pl.ds(row, 1), pl.ds(0, width)])
    return [jnp.concatenate(kind, axis=1) if len(kind) > 1 else kind[0] for kind in kinds]


def numer_kernel(mem, count, first, rows, base, tiles, segments, pieces, *refs):
    refs = list(refs)
    grp = lax.axis_size("grp")
    lanes = mem * count
    groups = count // ROWS
    places = mem // CORES
    core = lax.rem(lax.axis_index("mem"), CORES)
    own = lax.axis_index("grp")
    if not first:
        tags = refs.pop(0)
    for chunk, wide, src, dst, width in segments:
        across = pl.ds(dst * LANES, width * LANES)
        msgs, refs = refs[:places], refs[places:]
        if chunk == 0:
            crossed = refs.pop(0)
            past = groups * wide * LANES
        for step in range(places):
            for g in range(groups):
                low = (g * wide + src) * LANES
                if chunk == 0:
                    kept = pl.multiple_of(core * (groups * wide * LANES) + low, LANES)
                    near = msgs[step][:, pl.ds(kept, width * LANES)]
                    far = crossed[step, :, pl.ds(low, width * LANES)]
                else:
                    near = msgs[step][:, pl.ds(low, width * LANES)]
                    far = msgs[step][:, pl.ds(groups * wide * LANES + low, width * LANES)]
                refs[-3][pl.ds(step * count + g * ROWS, ROWS), across] = near
                refs[-3][pl.ds((places + step) * count + g * ROWS, ROWS), across] = far
    if first:
        tags = refs.pop(0)
        per_tile = LANES // count
        for tile in range(lanes // LANES):
            total = jnp.zeros((ROWS, LANES), F32)
            for slot in range(tile * per_tile, (tile + 1) * per_tile):
                if slot < places:
                    total += msgs[slot][:, pl.ds(CORES * past, LANES)].astype(F32)
                else:
                    total += crossed[slot - places, :, pl.ds(past, LANES)].astype(F32)
            tags[:, pl.ds(tile * LANES, LANES)] = total
    sums = refs[:grp]
    data, product, parts = refs[grp:]
    label = tags[...].astype(jnp.int32)
    key = label[0:1] * CPAD + label[1:2]
    spot = label[2:3]
    turn = label[3:4]
    pick = (
        lax.broadcasted_iota(jnp.int32, (PIECES * BINS, lanes), 0) % BINS == spot
    ).astype(BF16)
    klass = lax.broadcasted_iota(jnp.int32, (CPAD, lanes), 0)
    member = []
    for step in range(grp):
        one = (klass + CPAD * partner(own, step, grp) == key).astype(BF16)
        member.append(jnp.concatenate([one, one], axis=1))
    eye = identity()
    for tile in range(tiles):
        across = pl.ds(tile * LANES, LANES)
        flipped = lax.dot_general(eye, data[:, across], NT, preferred_element_type=F32)
        ctf = jnp.dot(
            pieces[pl.ds((base + tile) * LANES, LANES), :], pick, preferred_element_type=F32
        )
        product[across, :] = flipped * ctf
    offset = rows[0] * ANGLES - base * LANES

    def rotate(q, carry):
        for tile in range(lanes // LANES):
            block = product[
                pl.ds(pl.multiple_of(offset + q * ANGLES, ROWS), ANGLES),
                pl.ds(tile * LANES, LANES),
            ]
            bits = turn[:, tile * LANES : (tile + 1) * LANES]
            for level in range(LEVELS):
                chosen = (bits >> level & 1) == 1
                block = jnp.where(chosen, turned(block, SHIFT << level), block)
            high, low = split(block)
            where = pl.ds(pl.multiple_of(q * ANGLES, 2 * ROWS), ANGLES)
            parts[where, pl.ds(tile * LANES, LANES)] = high
            parts[where, pl.ds(lanes + tile * LANES, LANES)] = low
        return carry

    lax.fori_loop(0, rows[1] - rows[0], rotate, 0)
    result = lax.dot_general(
        jnp.concatenate(member, axis=0), parts[...], NT, preferred_element_type=F32
    )
    for step in range(grp):
        sums[step][pl.ds(0, CPAD)] = result[step * CPAD : (step + 1) * CPAD]
        if first:
            target = partner(own, step, grp)
            local = jnp.where(label[0:1] == target, label[1:2], -1)
            kinds = [kind.astype(F32) for kind in (local, spot, turn)]
            for kind, row, low, width in tag_spots(lanes, sums[step].shape[1]):
                sums[step][pl.ds(row, 1), pl.ds(0, width)] = kinds[kind][:, low : low + width]


def numerators(count, pieces, tags, arrived, chunk, edges, rows):
    mem, grp = lax.axis_size("mem"), lax.axis_size("grp")
    first = chunk == 0
    here = (rows[chunk], rows[chunk + 1])
    base = here[0] * ANGLES // LANES
    stop = min(-(-here[1] * ANGLES // LANES), edges[-1])
    segments, msgs = [], []
    for c in range(chunk + 1):
        low, high = max(edges[c], base), min(edges[c + 1], stop)
        if low < high:
            segments.append((c, edges[c + 1] - edges[c], low - edges[c], low - base, high - low))
            msgs += arrived[c]
    lanes = mem * count
    span = (here[1] - here[0]) * ANGLES
    tiles = stop - base
    shapes = [jax.ShapeDtypeStruct((ROWS, lanes), F32)] if first else []
    tall = sum_rows(lanes, span) if first else CPAD
    shapes += [jax.ShapeDtypeStruct((tall, span), F32)] * grp
    operands = [pieces] + ([] if first else [tags]) + msgs
    outs = pl.pallas_call(
        functools.partial(numer_kernel, mem, count, first, here, base, tiles, tuple(segments)),
        out_shape=shapes,
        in_specs=[VMEM] * len(operands),
        out_specs=[VMEM] * len(shapes),
        scratch_shapes=[
            pltpu.VMEM((lanes, tiles * LANES), BF16),
            pltpu.VMEM((tiles * LANES, lanes), F32),
            pltpu.VMEM((span, 2 * lanes), BF16),
        ],
        name="numerators",
        **params(16),
    )(*operands)
    if first:
        return outs[0], outs[1:]
    return tags, outs


def denom_kernel(lanes, weights, *refs):
    sums, (denom, spread) = refs[:-2], refs[-2:]
    span = weights.shape[0]
    klass = lax.broadcasted_iota(jnp.int32, (CPAD, lanes), 0)
    pair = lax.broadcasted_iota(jnp.int32, (PAIRS, lanes), 0)
    count = jnp.zeros((CPAD, PAIRS), F32)
    for ref in sums:
        local, spot, turn = [label.astype(jnp.int32) for label in read_tags(ref, lanes)]
        member = (klass == local).astype(BF16)
        which = (pair == turn * BINS + spot).astype(BF16)
        count += lax.dot_general(member, which, NT, preferred_element_type=F32)
    high, low = split(count)
    left = jnp.concatenate(
        [jnp.concatenate([high, high], axis=1), jnp.concatenate([low, low], axis=1)], axis=0
    )

    def turn_far(q, carry):
        rows = pl.ds(pl.multiple_of(q * ANGLES, 2 * ROWS), ANGLES)
        block = weights[rows, :]
        for tile in range(PAIRS // LANES):
            far = turned(block, SHIFT * NEAR * tile)
            spread[rows, pl.ds(tile * LANES, LANES)] = far[:, :LANES]
            spread[rows, pl.ds(PAIRS + tile * LANES, LANES)] = far[:, LANES:]
        return carry

    lax.fori_loop(0, span // ANGLES, turn_far, 0)
    both = lax.dot_general(left, spread[...], NT, preferred_element_type=F32)
    denom[...] = both[:CPAD] + both[CPAD:]


def denominators(weights, sums, lanes):
    span = weights.shape[0]
    return pl.pallas_call(
        functools.partial(denom_kernel, lanes),
        out_shape=jax.ShapeDtypeStruct((CPAD, span), F32),
        in_specs=[VMEM] * (1 + len(sums)),
        out_specs=VMEM,
        scratch_shapes=[pltpu.VMEM((span, 2 * PAIRS), BF16)],
        name="denominators",
        **params(20),
    )(weights, *sums)


def average_kernel(grp, rows, denom, *refs):
    sums, out = refs[:-1], refs[-1]
    for chunk in range(len(rows) - 1):
        across = pl.ds(rows[chunk] * ANGLES, (rows[chunk + 1] - rows[chunk]) * ANGLES)
        total = sums[chunk * grp][:CPG]
        for step in range(1, grp):
            total += sums[chunk * grp + step][:CPG]
        out[:, across] = total / (denom[:CPG, across] + wiener_term)


def averages(denom, sums, grp, rows):
    span = denom.shape[1]
    return pl.pallas_call(
        functools.partial(average_kernel, grp, rows),
        out_shape=jax.ShapeDtypeStruct((CPG, span), F32),
        in_specs=[VMEM] * (1 + len(sums)),
        out_specs=VMEM,
        name="averages",
        **params(8),
    )(denom, *sums)


def plan(span):
    turns = span // ANGLES
    tiles = -(-span // LANES)
    edges = [0, tiles // 2, tiles] if tiles % 2 == 0 else [0, tiles]
    rows = [min(edge * LANES // ANGLES, turns) for edge in edges]
    return tuple(edges), tuple(rows)


def on_device(images, classes, rotations, bins, ctf_table):
    mem, grp = lax.axis_size("mem"), lax.axis_size("grp")
    count = images.shape[0]
    span = images.shape[1] // mem
    edges, rows = plan(span)
    cols = edges[-1] * LANES
    places = mem // CORES
    table = ctf_table
    if cols != span:
        images = jnp.pad(images.reshape(count, mem, span), ((0, 0), (0, 0), (0, cols - span)))
        images = images.reshape(count, mem * cols)
        table = lax.dynamic_slice_in_dim(ctf_table, lax.axis_index("mem") * span, span, 1)
        table = jnp.pad(table, ((0, 0), (0, cols - span)))
    pieces, weights = tables(table, cols, span // ANGLES)
    steps = pack_first(images, classes, rotations, bins, cols, edges)
    here = {step: send(steps[step], "mem", step, CORES) for step in range(places - 1, 0, -1)}
    here[0] = steps[0]
    first = [here[step] for step in range(places)]
    after, arrived, ties = first[-1], [], [pieces]
    for low, high in zip(edges[1:], edges[2:]):
        crossed = swap(cross_later(images, cols, low, high), "mem")
        steps = pack_later(images, crossed, after, cols, low, high)
        here = {step: send(steps[step], "mem", step, CORES) for step in range(places - 1, 0, -1)}
        here[0] = steps[0]
        after = here[places - 1]
        ties.append(steps[0])
        arrived.append([here[step] for step in range(places)])
    arrived = [first + [swap(cross_first(first, ties[:2]), "mem")]] + arrived
    tags, sums = None, []
    for chunk in range(len(edges) - 1):
        tags, here = numerators(count, pieces, tags, arrived, chunk, edges, rows)
        sums += [here[0]] + [send(here[step], "grp", step) for step in range(1, grp)]
    denom = denominators(weights, sums[:grp], mem * count)
    return averages(denom, sums, grp, rows)


def solution(mesh):
    in_specs = (
        P(("grp", "mem"), None),
        P(("grp", "mem")),
        P(("grp", "mem")),
        P(("grp", "mem")),
        P(),
    )
    out_specs = P("grp", "mem")
    return jax.shard_map(
        on_device, mesh=mesh, in_specs=in_specs, out_specs=out_specs, check_vma=False
    )
```

time: 112 us -> 56.1 us (0.50)
  Pallas kernels: 64.1 us -> 9.69 us
  starting transfers between devices: 31 us -> 18.7 us
  waiting for transfers between devices: 14 us -> 24.8 us
    pallas_call x4 -> x7, Pallas kernels: 52.8 us -> 7.56 us  [the longest x1 3.53 us: denominators(): pl.pallas_call(functools.partial(denom_kernel, lanes), out_shape=jax.Shap...]
    ppermute x23 -> x14, starting transfers between devices: 31 us -> 18.7 us  [the longest x12 18.1 us: send(): return lax.ppermute(value, axis, pairs)]
    ppermute x23 -> x14, waiting for transfers between devices: 14 us -> 24.8 us  [the longest x12 23.2 us: send(): return lax.ppermute(value, axis, pairs)]
    pallas_call x1, Pallas kernels: 8.59 us -> 1.17 us  [tables(): pl.pallas_call(functools.partial(table_kernel, turns), out_shape=[jax.Sha...]
    pallas_call x1, Pallas kernels: 2.7 us -> 0.96 us  [averages(): pl.pallas_call(functools.partial(average_kernel, grp, rows), out_shape=ja...]
  transfers between devices with their start and end apart: 23 -> 14, of which waited for: 5 -> 9; matrix products, arithmetic and copies ran while one was open for 1% -> 1% of each run, Pallas kernels for 19% -> 13%
where the time goes in v2:
time: 56.1 us; the launch traced here: 55.2 us
  waiting for transfers between devices  24.8 us (44%)
  starting transfers between devices  18.7 us (33%)
  Pallas kernels  9.69 us (17%)
  local copies, waits for them, and re-layouts  1.28 us (2%)
  other arithmetic  0.73 us (1%)
    ppermute x12, waiting for transfers between devices, send(): return lax.ppermute(value, axis, pairs)  23.2 us
    ppermute x12, starting transfers between devices, send(): return lax.ppermute(value, axis, pairs)  18.1 us
    pallas_call x1, Pallas kernels, denominators(): pl.pallas_call(functools.partial(denom_kernel, lanes), out_shape=jax.Shap...  3.53 us
    pallas_call x2, Pallas kernels, numerators(): pl.pallas_call(functools.partial(numer_kernel, mem, count, first, here, b...  3.24 us
    ppermute x2, waiting for transfers between devices, swap(): lax.ppermute(value, axis, [(i, i ^ 1) for i in range(lax.axis_size(axis))])  1.58 us
    unnamed x6, local copies, waits for them, and re-layouts  1.28 us
    pallas_call x1, Pallas kernels, tables(): pl.pallas_call(functools.partial(table_kernel, turns), out_shape=[jax.Sha...  1.17 us
  transfers between devices with their start and end apart: 14, of which 9 were waited for; matrix products, arithmetic and copies ran while one was open for 1% of the time, Pallas kernels for 13%

profile of v2, /device:TPU:0, one launch (start us, length us, event | category | flops | bytes accessed | tf_op | source)
XLA Modules:
  0.0 55.2 jit_solution(13118644133569700281)
XLA Ops:
  0.0 1.3 %copy-done = bf16[32,18432]{1,0:T(8,128)(2,1)S(1)} copy-done((bf16[32,18432]{1,0:T(8,128)(2,1)S(1)}, bf16[32,18432]{1,0:T(8,128)(2,1)}, u32[]{:S(2)}) %copy-start) | copy-done | bytes 1179672
  1.3 0.1 cross_later.1
  1.4 0.5 collective-permute-start.3
  1.9 0.7 %pad_add_fusion.labels = s32[3,32]{1,0:T(4,128)S(1)} fusion(s32[1,32]{1,0:T(1,128)} %bitcast.3, s32[1,32]{1,0:T(1,128)} %bitcast.4, s32[1,32]{1,0:T(1,128)} %bitcast.5), kind=kLoop, calls=%fused_computation | loop fusion | flops 192 | bytes 768 | tf_op jit(solution)/shard_map/stack | solution.py:156
  2.7 0.4 pack_first.1
  3.1 5.0 %collective-permute-start.2 = (bf16[8,9344]{1,0:T(8,128)(2,1)S(1)}, bf16[8,9344]{1,0:T(8,128)(2,1)S(1)}, u32[]{:S(2)}, u32[]{:S(2)}) collective-permute-start(bf16[8,9344]{1,0:T(8,128)(2,1)S(1)} %get-tuple-element.29), channel_id=1, source_target_pairs={{0,6},{1,7},{2,4},{3,5},{4,2},{5,3},{6,0},{7,1},{8,14},{9,15},{10,... | collective-permute-start | bytes 448520 | tf_op jit(solution)/shard_map/ppermute | solution.py:48
  8.1 0.0 collective-permute-start
  8.1 0.6 %collective-permute-start.1 = (bf16[8,9344]{1,0:T(8,128)(2,1)S(1)}, bf16[8,9344]{1,0:T(8,128)(2,1)S(1)}, u32[]{:S(2)}, u32[]{:S(2)}) collective-permute-start(bf16[8,9344]{1,0:T(8,128)(2,1)S(1)} %get-tuple-element.28), channel_id=1, source_target_pairs={{0,4},{1,5},{2,6},{3,7},{4,0},{5,1},{6,2},{7,3},{8,12},{9,13},{10,... | collective-permute-start | bytes 448520 | tf_op jit(solution)/shard_map/ppermute | solution.py:48
  8.7 1.2 %tables.1 = (bf16[2304,48]{1,0:T(8,128)(2,1)S(1)}, bf16[2304,256]{1,0:T(8,128)(2,1)S(1)}) custom-call(f32[16,18432]{1,0:T(8,128)S(1)} %copy-done.2), custom_call_target="tpu_custom_call" | custom-call | flops 1048576 | bytes 65536 | tf_op jit(solution)/shard_map/tables/pallas_call | solution.py:302
  9.9 2.9 %collective-permute-done.2.after.refs_3_ = bf16[8,9344]{1,0:T(8,128)(2,1)S(1)} collective-permute-done((bf16[8,9344]{1,0:T(8,128)(2,1)S(1)}, bf16[8,9344]{1,0:T(8,128)(2,1)S(1)}, u32[]{:S(2)}, u32[]{:S(2)}) %collective-permute-start.2) | collective-permute-done | bytes 149536 | tf_op jit(solution)/shard_map/ppermute | solution.py:48
  12.8 0.2 pack_later.1
  13.0 3.6 %collective-permute-done.refs_1_ = bf16[8,9344]{1,0:T(8,128)(2,1)S(1)} collective-permute-done((bf16[8,9344]{1,0:T(8,128)(2,1)S(1)}, bf16[8,9344]{1,0:T(8,128)(2,1)S(1)}, u32[]{:S(2)}, u32[]{:S(2)}) %collective-permute-start) | collective-permute-done | bytes 149536 | tf_op jit(solution)/shard_map/ppermute | solution.py:48
  16.6 4.5 %collective-permute-done.1.refs_2_ = bf16[8,9344]{1,0:T(8,128)(2,1)S(1)} collective-permute-done((bf16[8,9344]{1,0:T(8,128)(2,1)S(1)}, bf16[8,9344]{1,0:T(8,128)(2,1)S(1)}, u32[]{:S(2)}, u32[]{:S(2)}) %collective-permute-start.1) | collective-permute-done | bytes 149536 | tf_op jit(solution)/shard_map/ppermute | solution.py:48
  21.1 0.1 collective-permute-start.4
  21.2 1.6 %collective-permute-done.4.refs_4_ = bf16[4,8,4736]{2,1,0:T(8,128)(2,1)S(1)} collective-permute-done((bf16[4,8,4736]{2,1,0:T(8,128)(2,1)S(1)}, bf16[4,8,4736]{2,1,0:T(8,128)(2,1)S(1)}, u32[]{:S(2)}, u32[]{:S(2)}) %collective-permute-start.4) | collective-permute-done | bytes 303136 | tf_op jit(solution)/shard_map/ppermute | solution.py:52
  22.8 1.6 %numerators.2 = (f32[8,256]{1,0:T(8,128)S(1)}, f32[56,1152]{1,0:T(8,128)S(1)}, f32[56,1152]{1,0:T(8,128)S(1)}, f32[56,1152]{1,0:T(8,128)S(1)}, f32[56,1152]{1,0:T(8,128)S(1)}) custom-call(bf16[2304,48]{1,0:T(8,128)(2,1)S(1)} %get-tuple-element.25.refs_4_.pieces, bf16[8,9344]{1,0:T(8,128)(2,1)S(1)} %get-tuple-element.26.refs_0_, ...), custom_call_target="tpu_custom_call" | custom-call | flops 1048576 | bytes 65536 | tf_op jit(solution)/shard_map/numerators/pallas_call | solution.py:454
  24.4 1.6 %collective-permute-start.5 = (f32[56,1152]{1,0:T(8,128)S(1)}, f32[56,1152]{1,0:T(8,128)S(1)}, u32[]{:S(2)}, u32[]{:S(2)}) collective-permute-start(f32[56,1152]{1,0:T(8,128)S(1)} %get-tuple-element.32), channel_id=1, source_target_pairs={{0,8},{8,0},{16,24},{24,16},{1,9},{9,1},{17,25},{25,17},{2,10},{10... | collective-permute-start | bytes 774152 | tf_op jit(solution)/shard_map/ppermute | solution.py:48
  26.0 3.0 %collective-permute-start.9 = (bf16[8,9216]{1,0:T(8,128)(2,1)S(1)}, bf16[8,9216]{1,0:T(8,128)(2,1)S(1)}, u32[]{:S(2)}, u32[]{:S(2)}) collective-permute-start(bf16[8,9216]{1,0:T(8,128)(2,1)S(1)} %get-tuple-element.37), channel_id=1, source_target_pairs={{0,4},{1,5},{2,6},{3,7},{4,0},{5,1},{6,2},{7,3},{8,12},{9,13},{10,... | collective-permute-start | bytes 442376 | tf_op jit(solution)/shard_map/ppermute | solution.py:48
  29.0 1.4 %collective-permute-start.10 = (bf16[8,9216]{1,0:T(8,128)(2,1)S(1)}, bf16[8,9216]{1,0:T(8,128)(2,1)S(1)}, u32[]{:S(2)}, u32[]{:S(2)}) collective-permute-start(bf16[8,9216]{1,0:T(8,128)(2,1)S(1)} %get-tuple-element.38), channel_id=1, source_target_pairs={{0,6},{1,7},{2,4},{3,5},{4,2},{5,3},{6,0},{7,1},{8,14},{9,15},{10,... | collective-permute-start | bytes 442376 | tf_op jit(solution)/shard_map/ppermute | solution.py:48
  30.4 1.5 %collective-permute-start.6 = (f32[56,1152]{1,0:T(8,128)S(1)}, f32[56,1152]{1,0:T(8,128)S(1)}, u32[]{:S(2)}, u32[]{:S(2)}) collective-permute-start(f32[56,1152]{1,0:T(8,128)S(1)} %get-tuple-element.33), channel_id=1, source_target_pairs={{0,16},{8,24},{16,0},{24,8},{1,17},{9,25},{17,1},{25,9},{2,18},{10... | collective-permute-start | bytes 774152 | tf_op jit(solution)/shard_map/ppermute | solution.py:48
  31.9 2.2 %collective-permute-done.8.refs_2_ = bf16[8,9216]{1,0:T(8,128)(2,1)S(1)} collective-permute-done((bf16[8,9216]{1,0:T(8,128)(2,1)S(1)}, bf16[8,9216]{1,0:T(8,128)(2,1)S(1)}, u32[]{:S(2)}, u32[]{:S(2)}) %collective-permute-start.8) | collective-permute-done | bytes 147488 | tf_op jit(solution)/shard_map/ppermute | solution.py:48
  34.1 1.5 %collective-permute-start.7 = (f32[56,1152]{1,0:T(8,128)S(1)}, f32[56,1152]{1,0:T(8,128)S(1)}, u32[]{:S(2)}, u32[]{:S(2)}) collective-permute-start(f32[56,1152]{1,0:T(8,128)S(1)} %get-tuple-element.34), channel_id=1, source_target_pairs={{0,24},{8,16},{16,8},{24,0},{1,25},{9,17},{17,9},{25,1},{2,26},{10... | collective-permute-start | bytes 774152 | tf_op jit(solution)/shard_map/ppermute | solution.py:48
  35.6 4.5 %collective-permute-done.9.refs_3_ = bf16[8,9216]{1,0:T(8,128)(2,1)S(1)} collective-permute-done((bf16[8,9216]{1,0:T(8,128)(2,1)S(1)}, bf16[8,9216]{1,0:T(8,128)(2,1)S(1)}, u32[]{:S(2)}, u32[]{:S(2)}) %collective-permute-start.9) | collective-permute-done | bytes 147488 | tf_op jit(solution)/shard_map/ppermute | solution.py:48
  40.0 1.6 %numerators.3 = (f32[56,1152]{1,0:T(8,128)S(1)}, f32[56,1152]{1,0:T(8,128)S(1)}, f32[56,1152]{1,0:T(8,128)S(1)}, f32[56,1152]{1,0:T(8,128)S(1)}) custom-call(bf16[2304,48]{1,0:T(8,128)(2,1)S(1)} %get-tuple-element.25.refs_4_.pieces, f32[8,256]{1,0:T(8,128)S(1)} %get-tuple-element.35.refs_0_, bf16[8,9216]{1,0:T(8,128)(2,1)S(1)} %get-tuple-element.30.refs_5_.refs_1_, ...), custom_call_target="tpu_custom_call" | custom-call | flops 1048576 | bytes 65536 | tf_op jit(solution)/shard_map/numerators/pallas_call | solution.py:454
  41.7 0.6 %collective-permute-start.11 = (f32[56,1152]{1,0:T(8,128)S(1)}, f32[56,1152]{1,0:T(8,128)S(1)}, u32[]{:S(2)}, u32[]{:S(2)}) collective-permute-start(f32[56,1152]{1,0:T(8,128)S(1)} %get-tuple-element.40), channel_id=1, source_target_pairs={{0,8},{8,0},{16,24},{24,16},{1,9},{9,1},{17,25},{25,17},{2,10},{10... | collective-permute-start | bytes 774152 | tf_op jit(solution)/shard_map/ppermute | solution.py:48
  42.3 1.5 %collective-permute-start.12 = (f32[56,1152]{1,0:T(8,128)S(1)}, f32[56,1152]{1,0:T(8,128)S(1)}, u32[]{:S(2)}, u32[]{:S(2)}) collective-permute-start(f32[56,1152]{1,0:T(8,128)S(1)} %get-tuple-element.41), channel_id=1, source_target_pairs={{0,16},{8,24},{16,0},{24,8},{1,17},{9,25},{17,1},{25,9},{2,18},{10... | collective-permute-start | bytes 774152 | tf_op jit(solution)/shard_map/ppermute | solution.py:48
  43.8 1.4 %collective-permute-start.13 = (f32[56,1152]{1,0:T(8,128)S(1)}, f32[56,1152]{1,0:T(8,128)S(1)}, u32[]{:S(2)}, u32[]{:S(2)}) collective-permute-start(f32[56,1152]{1,0:T(8,128)S(1)} %get-tuple-element.42), channel_id=1, source_target_pairs={{0,24},{8,16},{16,8},{24,0},{1,25},{9,17},{17,9},{25,1},{2,26},{10... | collective-permute-start | bytes 774152 | tf_op jit(solution)/shard_map/ppermute | solution.py:48
  45.2 3.5 %denominators.1.denom = f32[56,2304]{1,0:T(8,128)S(1)} custom-call(bf16[2304,256]{1,0:T(8,128)(2,1)S(1)} %get-tuple-element.24.weights, f32[56,1152]{1,0:T(8,128)S(1)} %get-tuple-element.31.refs_0_, f32[56,1152]{1,0:T(8,128)S(1)} %collective-permute-done.5.refs_1_, f32[56,1152]{1,0:T(8,128)S(1)} %collective-permute-done.6.refs_2_, ...), custom_call_target="tpu_custom_call" | custom-call | flops 1048576 | bytes 65536 | tf_op jit(solution)/shard_map/denominators/pallas_call | solution.py:504
  48.8 1.8 %collective-permute-done.11.refs_5_ = f32[56,1152]{1,0:T(8,128)S(1)} collective-permute-done((f32[56,1152]{1,0:T(8,128)S(1)}, f32[56,1152]{1,0:T(8,128)S(1)}, u32[]{:S(2)}, u32[]{:S(2)}) %collective-permute-start.11) | collective-permute-done | bytes 258080 | tf_op jit(solution)/shard_map/ppermute | solution.py:48
  50.5 2.6 %collective-permute-done.12.refs_6_ = f32[56,1152]{1,0:T(8,128)S(1)} collective-permute-done((f32[56,1152]{1,0:T(8,128)S(1)}, f32[56,1152]{1,0:T(8,128)S(1)}, u32[]{:S(2)}, u32[]{:S(2)}) %collective-permute-start.12) | collective-permute-done | bytes 258080 | tf_op jit(solution)/shard_map/ppermute | solution.py:48
  53.1 1.1 %collective-permute-done.13.refs_7_ = f32[56,1152]{1,0:T(8,128)S(1)} collective-permute-done((f32[56,1152]{1,0:T(8,128)S(1)}, f32[56,1152]{1,0:T(8,128)S(1)}, u32[]{:S(2)}, u32[]{:S(2)}) %collective-permute-start.13) | collective-permute-done | bytes 258080 | tf_op jit(solution)/shard_map/ppermute | solution.py:48
  54.2 1.0 %averages.1 = f32[50,2304]{1,0:T(8,128)} custom-call(f32[56,2304]{1,0:T(8,128)S(1)} %denominators.1.denom, f32[56,1152]{1,0:T(8,128)S(1)} %get-tuple-element.31.refs_0_, f32[56,1152]{1,0:T(8,128)S(1)} %collective-permute-done.5.refs_1_, f32[56,1152]{1,0:T(8,128)S(1)} %collective-permute-done.6.refs_2_, f32[56,1152]{1,0:T(8,128)S(1)} %collective-permute-done.7.refs_3_, ...), custom_call_target="tpu_custom_call" | custom-call | flops 1048576 | bytes 65536 | tf_op jit(solution)/shard_map/averages/pallas_call | solution.py:527
  (12 shorter events, 0.0 us)
Async XLA Ops:
  0.0 1.3 %copy-start = (bf16[32,18432]{1,0:T(8,128)(2,1)S(1)}, bf16[32,18432]{1,0:T(8,128)(2,1)}, u32[]{:S(2)}) copy-start(bf16[32,18432]{1,0:T(8,128)(2,1)} %img.5) | copy-start | bytes 3538948
  1.3 1.4 %copy-start.1 = (bf16[32,18432]{1,0:T(8,128)(2,1)S(1)}, bf16[32,18432]{1,0:T(8,128)(2,1)}, u32[]{:S(2)}) copy-start(bf16[32,18432]{1,0:T(8,128)(2,1)} %img.5) | copy-start | bytes 3538948
  1.3 7.5 %copy-start.2 = (f32[16,18432]{1,0:T(8,128)S(1)}, f32[16,18432]{1,0:T(8,128)}, u32[]{:S(2)}) copy-start(f32[16,18432]{1,0:T(8,128)} %table.1) | copy-start | bytes 3538948
  1.4 11.4 %collective-permute-start.3 = (bf16[4,8,4608]{2,1,0:T(8,128)(2,1)S(1)}, bf16[4,8,4608]{2,1,0:T(8,128)(2,1)S(1)}, u32[]{:S(2)}, u32[]{:S(2)}) collective-permute-start(bf16[4,8,4608]{2,1,0:T(8,128)(2,1)S(1)} %cross_later.1), channel_id=1, source_target_pairs={{0,1},{1,0},{2,3},{3,2},{4,5},{5,4},{6,7},{7,6},{8,9},{9,8},{10,11... | collective-permute-start | bytes 884744 | tf_op jit(solution)/shard_map/ppermute | solution.py:52
  3.1 9.7 %collective-permute-start.2 = (bf16[8,9344]{1,0:T(8,128)(2,1)S(1)}, bf16[8,9344]{1,0:T(8,128)(2,1)S(1)}, u32[]{:S(2)}, u32[]{:S(2)}) collective-permute-start(bf16[8,9344]{1,0:T(8,128)(2,1)S(1)} %get-tuple-element.29), channel_id=1, source_target_pairs={{0,6},{1,7},{2,4},{3,5},{4,2},{5,3},{6,0},{7,1},{8,14},{9,15},{10,... | collective-permute-start | bytes 448520 | tf_op jit(solution)/shard_map/ppermute | solution.py:48
  8.1 8.5 %collective-permute-start = (bf16[8,9344]{1,0:T(8,128)(2,1)S(1)}, bf16[8,9344]{1,0:T(8,128)(2,1)S(1)}, u32[]{:S(2)}, u32[]{:S(2)}) collective-permute-start(bf16[8,9344]{1,0:T(8,128)(2,1)S(1)} %get-tuple-element.27), channel_id=1, source_target_pairs={{0,2},{1,3},{2,0},{3,1},{4,6},{5,7},{6,4},{7,5},{8,10},{9,11},{10,... | collective-permute-start | bytes 448520 | tf_op jit(solution)/shard_map/ppermute | solution.py:48
  8.1 13.0 %collective-permute-start.1 = (bf16[8,9344]{1,0:T(8,128)(2,1)S(1)}, bf16[8,9344]{1,0:T(8,128)(2,1)S(1)}, u32[]{:S(2)}, u32[]{:S(2)}) collective-permute-start(bf16[8,9344]{1,0:T(8,128)(2,1)S(1)} %get-tuple-element.28), channel_id=1, source_target_pairs={{0,4},{1,5},{2,6},{3,7},{4,0},{5,1},{6,2},{7,3},{8,12},{9,13},{10,... | collective-permute-start | bytes 448520 | tf_op jit(solution)/shard_map/ppermute | solution.py:48
  21.1 1.7 %collective-permute-start.4 = (bf16[4,8,4736]{2,1,0:T(8,128)(2,1)S(1)}, bf16[4,8,4736]{2,1,0:T(8,128)(2,1)S(1)}, u32[]{:S(2)}, u32[]{:S(2)}) collective-permute-start(bf16[4,8,4736]{2,1,0:T(8,128)(2,1)S(1)} %cross_first.1), channel_id=1, source_target_pairs={{0,1},{1,0},{2,3},{3,2},{4,5},{5,4},{6,7},{7,6},{8,9},{9,8},{10,11... | collective-permute-start | bytes 909320 | tf_op jit(solution)/shard_map/ppermute | solution.py:52
  24.4 19.4 %collective-permute-start.5 = (f32[56,1152]{1,0:T(8,128)S(1)}, f32[56,1152]{1,0:T(8,128)S(1)}, u32[]{:S(2)}, u32[]{:S(2)}) collective-permute-start(f32[56,1152]{1,0:T(8,128)S(1)} %get-tuple-element.32), channel_id=1, source_target_pairs={{0,8},{8,0},{16,24},{24,16},{1,9},{9,1},{17,25},{25,17},{2,10},{10... | collective-permute-start | bytes 774152 | tf_op jit(solution)/shard_map/ppermute | solution.py:48
  26.0 8.1 %collective-permute-start.8 = (bf16[8,9216]{1,0:T(8,128)(2,1)S(1)}, bf16[8,9216]{1,0:T(8,128)(2,1)S(1)}, u32[]{:S(2)}, u32[]{:S(2)}) collective-permute-start(bf16[8,9216]{1,0:T(8,128)(2,1)S(1)} %get-tuple-element.36), channel_id=1, source_target_pairs={{0,2},{1,3},{2,0},{3,1},{4,6},{5,7},{6,4},{7,5},{8,10},{9,11},{10,... | collective-permute-start | bytes 442376 | tf_op jit(solution)/shard_map/ppermute | solution.py:48
  26.0 14.1 %collective-permute-start.9 = (bf16[8,9216]{1,0:T(8,128)(2,1)S(1)}, bf16[8,9216]{1,0:T(8,128)(2,1)S(1)}, u32[]{:S(2)}, u32[]{:S(2)}) collective-permute-start(bf16[8,9216]{1,0:T(8,128)(2,1)S(1)} %get-tuple-element.37), channel_id=1, source_target_pairs={{0,4},{1,5},{2,6},{3,7},{4,0},{5,1},{6,2},{7,3},{8,12},{9,13},{10,... | collective-permute-start | bytes 442376 | tf_op jit(solution)/shard_map/ppermute | solution.py:48
  29.0 11.0 %collective-permute-start.10 = (bf16[8,9216]{1,0:T(8,128)(2,1)S(1)}, bf16[8,9216]{1,0:T(8,128)(2,1)S(1)}, u32[]{:S(2)}, u32[]{:S(2)}) collective-permute-start(bf16[8,9216]{1,0:T(8,128)(2,1)S(1)} %get-tuple-element.38), channel_id=1, source_target_pairs={{0,6},{1,7},{2,4},{3,5},{4,2},{5,3},{6,0},{7,1},{8,14},{9,15},{10,... | collective-permute-start | bytes 442376 | tf_op jit(solution)/shard_map/ppermute | solution.py:48
  30.4 14.9 %collective-permute-start.6 = (f32[56,1152]{1,0:T(8,128)S(1)}, f32[56,1152]{1,0:T(8,128)S(1)}, u32[]{:S(2)}, u32[]{:S(2)}) collective-permute-start(f32[56,1152]{1,0:T(8,128)S(1)} %get-tuple-element.33), channel_id=1, source_target_pairs={{0,16},{8,24},{16,0},{24,8},{1,17},{9,25},{17,1},{25,9},{2,18},{10... | collective-permute-start | bytes 774152 | tf_op jit(solution)/shard_map/ppermute | solution.py:48
  34.1 11.1 %collective-permute-start.7 = (f32[56,1152]{1,0:T(8,128)S(1)}, f32[56,1152]{1,0:T(8,128)S(1)}, u32[]{:S(2)}, u32[]{:S(2)}) collective-permute-start(f32[56,1152]{1,0:T(8,128)S(1)} %get-tuple-element.34), channel_id=1, source_target_pairs={{0,24},{8,16},{16,8},{24,0},{1,25},{9,17},{17,9},{25,1},{2,26},{10... | collective-permute-start | bytes 774152 | tf_op jit(solution)/shard_map/ppermute | solution.py:48
  41.7 8.9 %collective-permute-start.11 = (f32[56,1152]{1,0:T(8,128)S(1)}, f32[56,1152]{1,0:T(8,128)S(1)}, u32[]{:S(2)}, u32[]{:S(2)}) collective-permute-start(f32[56,1152]{1,0:T(8,128)S(1)} %get-tuple-element.40), channel_id=1, source_target_pairs={{0,8},{8,0},{16,24},{24,16},{1,9},{9,1},{17,25},{25,17},{2,10},{10... | collective-permute-start | bytes 774152 | tf_op jit(solution)/shard_map/ppermute | solution.py:48
  42.3 10.9 %collective-permute-start.12 = (f32[56,1152]{1,0:T(8,128)S(1)}, f32[56,1152]{1,0:T(8,128)S(1)}, u32[]{:S(2)}, u32[]{:S(2)}) collective-permute-start(f32[56,1152]{1,0:T(8,128)S(1)} %get-tuple-element.41), channel_id=1, source_target_pairs={{0,16},{8,24},{16,0},{24,8},{1,17},{9,25},{17,1},{25,9},{2,18},{10... | collective-permute-start | bytes 774152 | tf_op jit(solution)/shard_map/ppermute | solution.py:48
  43.8 10.5 %collective-permute-start.13 = (f32[56,1152]{1,0:T(8,128)S(1)}, f32[56,1152]{1,0:T(8,128)S(1)}, u32[]{:S(2)}, u32[]{:S(2)}) collective-permute-start(f32[56,1152]{1,0:T(8,128)S(1)} %get-tuple-element.42), channel_id=1, source_target_pairs={{0,24},{8,16},{16,8},{24,0},{1,25},{9,17},{17,9},{25,1},{2,26},{10... | collective-permute-start | bytes 774152 | tf_op jit(solution)/shard_map/ppermute | solution.py:48

commit v3 on v2

--- a/solution.py
+++ b/solution.py
@@ -26,6 +26,7 @@
 
 F32 = jnp.float32
 BF16 = jnp.bfloat16
+HALF = jnp.float16
 NT = (((1,), (1,)), ((), ()))
 ANY = pl.BlockSpec(memory_space=pl.ANY)
 HBM = pl.BlockSpec(memory_space=pltpu.HBM)
@@ -38,18 +39,14 @@
     return lax.rem(index + step, size) if not isinstance(index, int) else (index + step) % size
 
 
-def send(value, axis, step, cores=1):
+def send(value, axis, step, cores=1, cross=0):
     size = lax.axis_size(axis) // cores
     pairs = [
-        (i * cores + core, partner(i, step, size) * cores + core)
+        (i * cores + core, partner(i, step, size) * cores + (core ^ cross))
         for i in range(size)
         for core in range(cores)
     ]
     return lax.ppermute(value, axis, pairs)
-
-
-def swap(value, axis):
-    return lax.ppermute(value, axis, [(i, i ^ 1) for i in range(lax.axis_size(axis))])
 
 
 def identity():
@@ -80,28 +77,12 @@
     )
 
 
-def run(copies, sems):
-    copies = [
-        pltpu.make_async_copy(src, dst, sems.at[spot]) for spot, (src, dst) in enumerate(copies)
-    ]
-    for copy in copies:
-        copy.start()
-    return copies
-
-
-def pack_first_kernel(mem, cols, width, img, labels, *refs):
+def pack_kernel(mem, cols, edges, img, labels, *outs):
     places = mem // CORES
-    outs, (data, sems) = refs[:places], refs[places:]
-    count = data.shape[0]
+    count = img.shape[0]
     groups = count // ROWS
     here = lax.axis_index("mem") // CORES
-    copies = run(
-        [
-            (img.at[:, pl.ds(dest * cols, width)], data.at[:, pl.ds(dest * width, width)])
-            for dest in range(mem)
-        ],
-        sems,
-    )
+    core = lax.rem(lax.axis_index("mem"), CORES)
     label = labels[0:1]
     owner = jnp.zeros_like(label)
     for g in range(1, lax.axis_size("grp")):
@@ -122,41 +103,67 @@
     ).astype(BF16)
     tags = jnp.dot(stack.astype(F32).astype(BF16), spread, preferred_element_type=F32)
     place = lax.broadcasted_iota(jnp.int32, (ROWS, LANES), 1) // count
+    first = (edges[1] - edges[0]) * LANES
     for step in range(places):
+        there = partner(here, step, places) * CORES
+        for target in range(CORES):
+            start = pl.multiple_of((there + target) * cols + edges[0] * LANES, LANES)
+            for g in range(groups):
+                outs[step][:, pl.ds((target * groups + g) * first, first)] = img[
+                    pl.ds(g * ROWS, ROWS), pl.ds(start, first)
+                ]
         mine = jnp.where(place == step % (LANES // count), tags, 0.0)
-        outs[step][:, pl.ds(CORES * groups * width, LANES)] = mine.astype(BF16)
-    for copy in copies:
-        copy.wait()
-    for step in range(places):
-        dest = partner(here, step, places) * CORES
-        for core in range(CORES):
-            start = pl.multiple_of((dest + core) * width, LANES)
+        outs[step][:, pl.ds(CORES * groups * first, LANES)] = mine.astype(BF16)
+        if len(edges) == 2:
+            continue
+        width = (edges[2] - edges[1]) * LANES
+        for cross in range(CORES):
+            start = pl.multiple_of((there + (core ^ cross)) * cols + edges[1] * LANES, LANES)
             for g in range(groups):
-                outs[step][:, pl.ds((core * groups + g) * width, width)] = data[
+                outs[places + cross][step, :, pl.ds(g * width, width)] = img[
                     pl.ds(g * ROWS, ROWS), pl.ds(start, width)
                 ]
 
 
-def pack_first(images, classes, rotations, bins, cols, edges):
+def pack(images, labels, cols, edges):
     mem = lax.axis_size("mem")
-    count = images.shape[0]
-    width = edges[1] * LANES
-    shape = jax.ShapeDtypeStruct((ROWS, CORES * (count // ROWS) * width + LANES), BF16)
+    groups = images.shape[0] // ROWS
+    wide = [groups * (high - low) * LANES for low, high in zip(edges, edges[1:])]
+    shapes = [jax.ShapeDtypeStruct((ROWS, CORES * wide[0] + LANES), BF16)] * (mem // CORES)
+    for width in wide[1:]:
+        shapes += [jax.ShapeDtypeStruct((mem // CORES, ROWS, width), BF16)] * CORES
+    outs = pl.pallas_call(
+        functools.partial(pack_kernel, mem, cols, edges),
+        out_shape=shapes,
+        in_specs=[VMEM] * 2,
+        out_specs=[VMEM] * len(shapes),
+        name="pack",
+        **params(8),
+    )(images, labels)
+    return outs[: mem // CORES], outs[mem // CORES :]
+
+
+def join_kernel(kept, crossed, *refs):
+    places, _, span = kept.shape
+    outs = refs[-places:]
+    for step in range(places):
+        outs[step][:, pl.ds(0, span)] = kept[step]
+        outs[step][:, pl.ds(span, span)] = crossed[step]
+
+
+def join(kept, crossed, after):
+    places, _, span = kept.shape
     return pl.pallas_call(
-        functools.partial(pack_first_kernel, mem, cols, width),
-        out_shape=[shape] * (mem // CORES),
-        in_specs=[HBM, VMEM],
-        out_specs=[VMEM] * (mem // CORES),
-        scratch_shapes=[
-            pltpu.VMEM((count, mem * width), BF16),
-            pltpu.SemaphoreType.DMA((mem,)),
-        ],
-        name="pack_first",
+        join_kernel,
+        out_shape=[jax.ShapeDtypeStruct((ROWS, CORES * span), BF16)] * places,
+        in_specs=[VMEM] * 2 + [ANY] * len(after),
+        out_specs=[VMEM] * places,
+        name="join",
         **params(8),
-    )(images, jnp.stack([classes, bins, rotations]))
-
-
-def cross_first_kernel(places, *refs):
+    )(kept, crossed, *after)
+
+
+def cross_kernel(places, *refs):
     blocks, out = refs[:places], refs[-1]
     other = 1 - lax.rem(lax.axis_index("mem"), CORES)
     span = (blocks[0].shape[1] - LANES) // CORES
@@ -165,94 +172,16 @@
         out[step, :, pl.ds(span, LANES)] = block[:, pl.ds(CORES * span, LANES)]
 
 
-def cross_first(blocks, after):
+def cross(blocks, after):
     span = (blocks[0].shape[1] - LANES) // CORES
     return pl.pallas_call(
-        functools.partial(cross_first_kernel, len(blocks)),
+        functools.partial(cross_kernel, len(blocks)),
         out_shape=jax.ShapeDtypeStruct((len(blocks), ROWS, span + LANES), BF16),
         in_specs=[VMEM] * len(blocks) + [ANY] * len(after),
         out_specs=VMEM,
-        name="cross_first",
+        name="cross",
         **params(8),
     )(*blocks, *after)
-
-
-def cross_later_kernel(mem, cols, low, width, img, out, data, sems):
-    groups = data.shape[0] // ROWS
-    places = mem // CORES
-    here = lax.axis_index("mem") // CORES
-    other = 1 - lax.rem(lax.axis_index("mem"), CORES)
-    copies = []
-    for step in range(places):
-        dest = partner(here, step, places) * CORES + other
-        start = pl.multiple_of(dest * cols + low, LANES)
-        copies.append((img.at[:, pl.ds(start, width)], data.at[:, pl.ds(step * width, width)]))
-    for step, copy in enumerate(run(copies, sems)):
-        copy.wait()
-        for g in range(groups):
-            out[step, :, pl.ds(g * width, width)] = data[
-                pl.ds(g * ROWS, ROWS), pl.ds(step * width, width)
-            ]
-
-
-def cross_later(images, cols, low, high):
-    mem = lax.axis_size("mem")
-    count = images.shape[0]
-    width = (high - low) * LANES
-    return pl.pallas_call(
-        functools.partial(cross_later_kernel, mem, cols, low * LANES, width),
-        out_shape=jax.ShapeDtypeStruct((mem // CORES, ROWS, count // ROWS * width), BF16),
-        in_specs=[HBM],
-        out_specs=VMEM,
-        scratch_shapes=[
-            pltpu.VMEM((count, mem // CORES * width), BF16),
-            pltpu.SemaphoreType.DMA((mem // CORES,)),
-        ],
-        name="cross_later",
-        **params(8),
-    )(images)
-
-
-def pack_later_kernel(mem, cols, low, width, img, crossed, after, *refs):
-    places = mem // CORES
-    outs, (data, sems) = refs[:places], refs[places:]
-    groups = data.shape[0] // ROWS
-    me = lax.axis_index("mem")
-    here, core = me // CORES, lax.rem(me, CORES)
-    copies = []
-    for step in range(places):
-        dest = partner(here, step, places) * CORES + core
-        start = pl.multiple_of(dest * cols + low, LANES)
-        copies.append((img.at[:, pl.ds(start, width)], data.at[:, pl.ds(step * width, width)]))
-    copies = run(copies, sems)
-    for step in range(places):
-        outs[step][:, pl.ds(groups * width, groups * width)] = crossed[step]
-    for step, copy in enumerate(copies):
-        copy.wait()
-        for g in range(groups):
-            outs[step][:, pl.ds(g * width, width)] = data[
-                pl.ds(g * ROWS, ROWS), pl.ds(step * width, width)
-            ]
-
-
-def pack_later(images, crossed, after, cols, low, high):
-    mem = lax.axis_size("mem")
-    places = mem // CORES
-    count = images.shape[0]
-    width = (high - low) * LANES
-    shape = jax.ShapeDtypeStruct((ROWS, CORES * (count // ROWS) * width), BF16)
-    return pl.pallas_call(
-        functools.partial(pack_later_kernel, mem, cols, low * LANES, width),
-        out_shape=[shape] * places,
-        in_specs=[HBM, VMEM, ANY],
-        out_specs=[VMEM] * places,
-        scratch_shapes=[
-            pltpu.VMEM((count, places * width), BF16),
-            pltpu.SemaphoreType.DMA((places,)),
-        ],
-        name="pack_later",
-        **params(8),
-    )(images, crossed, after)
 
 
 def table_kernel(turns, table, pieces, weights, ctf, square, sem):
@@ -332,10 +261,15 @@
     return -(-last // ROWS) * ROWS
 
 
+def tag_block(message, lanes):
+    low = CPG // ROWS * ROWS
+    return message[low:].astype(F32)
+
+
 def read_tags(ref, lanes):
     kinds = [[], [], []]
     for kind, row, _, width in tag_spots(lanes, ref.shape[1]):
-        kinds[kind].append(ref[pl.ds(row, 1), pl.ds(0, width)])
+        kinds[kind].append(ref[pl.ds(row - CPG // ROWS * ROWS, 1), pl.ds(0, width)])
     return [jnp.concatenate(kind, axis=1) if len(kind) > 1 else kind[0] for kind in kinds]
 
 
@@ -470,12 +404,12 @@
 
 
 def denom_kernel(lanes, weights, *refs):
-    sums, (denom, spread) = refs[:-2], refs[-2:]
+    blocks, (denom, spread) = refs[:-2], refs[-2:]
     span = weights.shape[0]
     klass = lax.broadcasted_iota(jnp.int32, (CPAD, lanes), 0)
     pair = lax.broadcasted_iota(jnp.int32, (PAIRS, lanes), 0)
     count = jnp.zeros((CPAD, PAIRS), F32)
-    for ref in sums:
+    for ref in blocks:
         local, spot, turn = [label.astype(jnp.int32) for label in read_tags(ref, lanes)]
         member = (klass == local).astype(BF16)
         which = (pair == turn * BINS + spot).astype(BF16)
@@ -499,33 +433,30 @@
     denom[...] = both[:CPAD] + both[CPAD:]
 
 
-def denominators(weights, sums, lanes):
+def denominators(weights, blocks, lanes):
     span = weights.shape[0]
     return pl.pallas_call(
         functools.partial(denom_kernel, lanes),
         out_shape=jax.ShapeDtypeStruct((CPAD, span), F32),
-        in_specs=[VMEM] * (1 + len(sums)),
+        in_specs=[VMEM] * (1 + len(blocks)),
         out_specs=VMEM,
         scratch_shapes=[pltpu.VMEM((span, 2 * PAIRS), BF16)],
         name="denominators",
         **params(20),
-    )(weights, *sums)
-
-
-def average_kernel(grp, rows, denom, *refs):
+    )(weights, *blocks)
+
+
+def average_kernel(rows, denom, *refs):
     sums, out = refs[:-1], refs[-1]
     for chunk in range(len(rows) - 1):
         across = pl.ds(rows[chunk] * ANGLES, (rows[chunk + 1] - rows[chunk]) * ANGLES)
-        total = sums[chunk * grp][:CPG]
-        for step in range(1, grp):
-            total += sums[chunk * grp + step][:CPG]
-        out[:, across] = total / (denom[:CPG, across] + wiener_term)
-
-
-def averages(denom, sums, grp, rows):
+        out[:, across] = sums[chunk][:CPG] / (denom[:CPG, across] + wiener_term)
+
+
+def averages(denom, sums, rows):
     span = denom.shape[1]
     return pl.pallas_call(
-        functools.partial(average_kernel, grp, rows),
+        functools.partial(average_kernel, rows),
         out_shape=jax.ShapeDtypeStruct((CPG, span), F32),
         in_specs=[VMEM] * (1 + len(sums)),
         out_specs=VMEM,
@@ -556,26 +487,31 @@
         table = lax.dynamic_slice_in_dim(ctf_table, lax.axis_index("mem") * span, span, 1)
         table = jnp.pad(table, ((0, 0), (0, cols - span)))
     pieces, weights = tables(table, cols, span // ANGLES)
-    steps = pack_first(images, classes, rotations, bins, cols, edges)
-    here = {step: send(steps[step], "mem", step, CORES) for step in range(places - 1, 0, -1)}
-    here[0] = steps[0]
+    firsts, seconds = pack(images, jnp.stack([classes, bins, rotations]), cols, edges)
+    others = range(places - 1, 0, -1)
+    here = {step: send(firsts[step], "mem", step, CORES) for step in others}
+    here[0] = firsts[0]
     first = [here[step] for step in range(places)]
-    after, arrived, ties = first[-1], [], [pieces]
-    for low, high in zip(edges[1:], edges[2:]):
-        crossed = swap(cross_later(images, cols, low, high), "mem")
-        steps = pack_later(images, crossed, after, cols, low, high)
-        here = {step: send(steps[step], "mem", step, CORES) for step in range(places - 1, 0, -1)}
-        here[0] = steps[0]
-        after = here[places - 1]
-        ties.append(steps[0])
-        arrived.append([here[step] for step in range(places)])
-    arrived = [first + [swap(cross_first(first, ties[:2]), "mem")]] + arrived
-    tags, sums = None, []
+    arrived, after = [], [pieces]
+    if seconds:
+        kept, crossed = seconds[0], send(seconds[1], "mem", 0, CORES, 1)
+        msgs = join(kept, crossed, [first[-1], pieces])
+        here = {step: send(msgs[step], "mem", step, CORES) for step in others}
+        here[0] = msgs[0]
+        arrived, after = [[here[step] for step in range(places)]], [msgs[0]]
+    arrived = [first + [send(cross(first, after), "mem", 0, CORES, 1)]] + arrived
+    tags, sums, blocks = None, [], []
     for chunk in range(len(edges) - 1):
         tags, here = numerators(count, pieces, tags, arrived, chunk, edges, rows)
-        sums += [here[0]] + [send(here[step], "grp", step) for step in range(1, grp)]
-    denom = denominators(weights, sums[:grp], mem * count)
-    return averages(denom, sums, grp, rows)
+        others = [send(here[step].astype(HALF), "grp", step) for step in range(1, grp)]
+        if chunk == 0:
+            blocks = [tag_block(part, mem * count) for part in [here[0]] + others]
+        total = here[0]
+        for part in others:
+            total = total + part.astype(F32)
+        sums.append(total)
+    denom = denominators(weights, blocks, mem * count)
+    return averages(denom, sums, rows)
 
 
 def solution(mesh):

time: 56.1 us -> 46.6 us (0.83)
  waiting for transfers between devices: 24.8 us -> 15.1 us
  starting transfers between devices: 18.7 us -> 19.4 us
  Pallas kernels: 9.69 us -> 9.02 us
    ppermute x12 -> x14, waiting for transfers between devices: 23.2 us -> 15.1 us  [send(): return lax.ppermute(value, axis, pairs)]
    ppermute x2 -> x0, waiting for transfers between devices: 1.58 us -> none  [swap(): lax.ppermute(value, axis, [(i, i ^ 1) for i in range(lax.axis_size(axis))])]
    ppermute x12 -> x14, starting transfers between devices: 18.1 us -> 19.4 us  [send(): return lax.ppermute(value, axis, pairs)]
    pallas_call x5 -> x4, Pallas kernels: 1.74 us -> 1.07 us  [the longest x1 0.88 us: averages(): pl.pallas_call(functools.partial(average_kernel, rows), out_shape=jax.Sha...]
    ppermute x2 -> x0, starting transfers between devices: 0.59 us -> none  [swap(): lax.ppermute(value, axis, [(i, i ^ 1) for i in range(lax.axis_size(axis))])]
    unnamed x6 -> x4, local copies, waits for them, and re-layouts: 1.28 us -> 1.27 us
  transfers between devices with their start and end apart: 14 -> 14, of which waited for: 9 -> 6; matrix products, arithmetic and copies ran while one was open for 1% -> 0% of each run, Pallas kernels for 13% -> 17%
where the time goes in v3:
time: 46.6 us; the launch traced here: 45.8 us
  starting transfers between devices  19.4 us (42%)
  waiting for transfers between devices  15.1 us (32%)
  Pallas kernels  9.02 us (19%)
  local copies, waits for them, and re-layouts  1.28 us (3%)
  other arithmetic  0.97 us (2%)
    ppermute x14, starting transfers between devices, send(): return lax.ppermute(value, axis, pairs)  19.4 us
    ppermute x14, waiting for transfers between devices, send(): return lax.ppermute(value, axis, pairs)  15.1 us
    pallas_call x1, Pallas kernels, denominators(): pl.pallas_call(functools.partial(denom_kernel, lanes), out_shape=jax.Shap...  3.53 us
    pallas_call x2, Pallas kernels, numerators(): pl.pallas_call(functools.partial(numer_kernel, mem, count, first, here, b...  3.25 us
    unnamed x4, local copies, waits for them, and re-layouts  1.27 us
    pallas_call x1, Pallas kernels, tables(): pl.pallas_call(functools.partial(table_kernel, turns), out_shape=[jax.Sha...  1.17 us
  transfers between devices with their start and end apart: 14, of which 6 were waited for; matrix products, arithmetic and copies ran while one was open for 0% of the time, Pallas kernels for 17%

profile of v3, /device:TPU:0, one launch (start us, length us, event | category | flops | bytes accessed | tf_op | source)
XLA Modules:
  0.0 45.8 jit_solution(7934998336600958619)
XLA Ops:
  0.0 0.7 %pad_add_fusion.labels = s32[3,32]{1,0:T(4,128)S(1)} fusion(s32[1,32]{1,0:T(1,128)} %bitcast.3, s32[1,32]{1,0:T(1,128)} %bitcast.4, s32[1,32]{1,0:T(1,128)} %bitcast.5), kind=kLoop, calls=%fused_computation.5 | loop fusion | flops 192 | bytes 768 | tf_op jit(solution)/shard_map/stack | solution.py:490
  0.7 1.3 %copy-done = bf16[32,18432]{1,0:T(8,128)(2,1)S(1)} copy-done((bf16[32,18432]{1,0:T(8,128)(2,1)S(1)}, bf16[32,18432]{1,0:T(8,128)(2,1)}, u32[]{:S(2)}) %copy-start) | copy-done | bytes 1179672
  2.0 0.1 pack.1
  2.1 0.5 %collective-permute-start.3 = (bf16[4,8,4608]{2,1,0:T(8,128)(2,1)S(1)}, bf16[4,8,4608]{2,1,0:T(8,128)(2,1)S(1)}, u32[]{:S(2)}, u32[]{:S(2)}) collective-permute-start(bf16[4,8,4608]{2,1,0:T(8,128)(2,1)S(1)} %get-tuple-element.33), channel_id=1, source_target_pairs={{0,1},{1,0},{2,3},{3,2},{4,5},{5,4},{6,7},{7,6},{8,9},{9,8},{10,11... | collective-permute-start | bytes 884744 | tf_op jit(solution)/shard_map/ppermute | solution.py:49
  2.6 4.7 %collective-permute-start.2 = (bf16[8,9344]{1,0:T(8,128)(2,1)S(1)}, bf16[8,9344]{1,0:T(8,128)(2,1)S(1)}, u32[]{:S(2)}, u32[]{:S(2)}) collective-permute-start(bf16[8,9344]{1,0:T(8,128)(2,1)S(1)} %get-tuple-element.31), channel_id=1, source_target_pairs={{0,6},{1,7},{2,4},{3,5},{4,2},{5,3},{6,0},{7,1},{8,14},{9,15},{10,... | collective-permute-start | bytes 448520 | tf_op jit(solution)/shard_map/ppermute | solution.py:49
  7.3 0.6 %collective-permute-start.1 = (bf16[8,9344]{1,0:T(8,128)(2,1)S(1)}, bf16[8,9344]{1,0:T(8,128)(2,1)S(1)}, u32[]{:S(2)}, u32[]{:S(2)}) collective-permute-start(bf16[8,9344]{1,0:T(8,128)(2,1)S(1)} %get-tuple-element.30), channel_id=1, source_target_pairs={{0,4},{1,5},{2,6},{3,7},{4,0},{5,1},{6,2},{7,3},{8,12},{9,13},{10,... | collective-permute-start | bytes 448520 | tf_op jit(solution)/shard_map/ppermute | solution.py:49
  7.9 1.2 %tables.1 = (bf16[2304,48]{1,0:T(8,128)(2,1)S(1)}, bf16[2304,256]{1,0:T(8,128)(2,1)S(1)}) custom-call(f32[16,18432]{1,0:T(8,128)S(1)} %copy-done.1), custom_call_target="tpu_custom_call" | custom-call | flops 1048576 | bytes 65536 | tf_op jit(solution)/shard_map/tables/pallas_call | solution.py:231
  9.1 3.0 %collective-permute-done.2.refs_0_.refs_3_ = bf16[8,9344]{1,0:T(8,128)(2,1)S(1)} collective-permute-done((bf16[8,9344]{1,0:T(8,128)(2,1)S(1)}, bf16[8,9344]{1,0:T(8,128)(2,1)S(1)}, u32[]{:S(2)}, u32[]{:S(2)}) %collective-permute-start.2) | collective-permute-done | bytes 149536 | tf_op jit(solution)/shard_map/ppermute | solution.py:49
  12.1 0.0 collective-permute-done.3.crossed
  12.1 3.9 %collective-permute-done.refs_1_ = bf16[8,9344]{1,0:T(8,128)(2,1)S(1)} collective-permute-done((bf16[8,9344]{1,0:T(8,128)(2,1)S(1)}, bf16[8,9344]{1,0:T(8,128)(2,1)S(1)}, u32[]{:S(2)}, u32[]{:S(2)}) %collective-permute-start) | collective-permute-done | bytes 149536 | tf_op jit(solution)/shard_map/ppermute | solution.py:49
  16.0 4.5 %collective-permute-done.1.refs_2_ = bf16[8,9344]{1,0:T(8,128)(2,1)S(1)} collective-permute-done((bf16[8,9344]{1,0:T(8,128)(2,1)S(1)}, bf16[8,9344]{1,0:T(8,128)(2,1)S(1)}, u32[]{:S(2)}, u32[]{:S(2)}) %collective-permute-start.1) | collective-permute-done | bytes 149536 | tf_op jit(solution)/shard_map/ppermute | solution.py:49
  20.6 0.1 collective-permute-start.4
  20.6 0.1 collective-permute-start.8
  20.7 3.0 %collective-permute-start.9 = (bf16[8,9216]{1,0:T(8,128)(2,1)S(1)}, bf16[8,9216]{1,0:T(8,128)(2,1)S(1)}, u32[]{:S(2)}, u32[]{:S(2)}) collective-permute-start(bf16[8,9216]{1,0:T(8,128)(2,1)S(1)} %get-tuple-element.41), channel_id=1, source_target_pairs={{0,4},{1,5},{2,6},{3,7},{4,0},{5,1},{6,2},{7,3},{8,12},{9,13},{10,... | collective-permute-start | bytes 442376 | tf_op jit(solution)/shard_map/ppermute | solution.py:49
  23.7 1.3 %collective-permute-start.10 = (bf16[8,9216]{1,0:T(8,128)(2,1)S(1)}, bf16[8,9216]{1,0:T(8,128)(2,1)S(1)}, u32[]{:S(2)}, u32[]{:S(2)}) collective-permute-start(bf16[8,9216]{1,0:T(8,128)(2,1)S(1)} %get-tuple-element.42), channel_id=1, source_target_pairs={{0,6},{1,7},{2,4},{3,5},{4,2},{5,3},{6,0},{7,1},{8,14},{9,15},{10,... | collective-permute-start | bytes 442376 | tf_op jit(solution)/shard_map/ppermute | solution.py:49
  25.1 0.0 collective-permute-done.4.refs_4_
  25.1 1.6 %numerators.2 = (f32[8,256]{1,0:T(8,128)S(1)}, f32[56,1152]{1,0:T(8,128)S(1)}, f32[56,1152]{1,0:T(8,128)S(1)}, f32[56,1152]{1,0:T(8,128)S(1)}, f32[56,1152]{1,0:T(8,128)S(1)}) custom-call(bf16[2304,48]{1,0:T(8,128)(2,1)S(1)} %get-tuple-element.27.refs_1_.pieces, bf16[8,9344]{1,0:T(8,128)(2,1)S(1)} %get-tuple-element.28.refs_0_, ...), custom_call_target="tpu_custom_call" | custom-call | flops 1048576 | bytes 65536 | tf_op jit(solution)/shard_map/numerators/pallas_call | solution.py:388
  26.8 1.6 %collective-permute-start.5 = (f16[56,1152]{1,0:T(8,128)(2,1)S(1)}, f16[56,1152]{1,0:T(8,128)(2,1)S(1)}, u32[]{:S(2)}, u32[]{:S(2)}) collective-permute-start(f16[56,1152]{1,0:T(8,128)(2,1)S(1)} %convert_element_type.45), channel_id=1, source_target_pairs={{0,8},{8,0},{16,24},{24,16},{1,9},{9,1},{17,25},{25,17},{2,10},{10... | collective-permute-start | bytes 387080 | tf_op jit(solution)/shard_map/ppermute | solution.py:49
  28.3 1.6 %collective-permute-start.6 = (f16[56,1152]{1,0:T(8,128)(2,1)S(1)}, f16[56,1152]{1,0:T(8,128)(2,1)S(1)}, u32[]{:S(2)}, u32[]{:S(2)}) collective-permute-start(f16[56,1152]{1,0:T(8,128)(2,1)S(1)} %convert_element_type.47), channel_id=1, source_target_pairs={{0,16},{8,24},{16,0},{24,8},{1,17},{9,25},{17,1},{25,9},{2,18},{10... | collective-permute-start | bytes 387080 | tf_op jit(solution)/shard_map/ppermute | solution.py:49
  30.0 2.2 %collective-permute-start.7 = (f16[56,1152]{1,0:T(8,128)(2,1)S(1)}, f16[56,1152]{1,0:T(8,128)(2,1)S(1)}, u32[]{:S(2)}, u32[]{:S(2)}) collective-permute-start(f16[56,1152]{1,0:T(8,128)(2,1)S(1)} %convert_element_type.49), channel_id=1, source_target_pairs={{0,24},{8,16},{16,8},{24,0},{1,25},{9,17},{17,9},{25,1},{2,26},{10... | collective-permute-start | bytes 387080 | tf_op jit(solution)/shard_map/ppermute | solution.py:49
  32.2 2.6 %collective-permute-done.9.refs_3_ = bf16[8,9216]{1,0:T(8,128)(2,1)S(1)} collective-permute-done((bf16[8,9216]{1,0:T(8,128)(2,1)S(1)}, bf16[8,9216]{1,0:T(8,128)(2,1)S(1)}, u32[]{:S(2)}, u32[]{:S(2)}) %collective-permute-start.9) | collective-permute-done | bytes 147488 | tf_op jit(solution)/shard_map/ppermute | solution.py:49
  34.7 1.6 %numerators.3 = (f32[56,1152]{1,0:T(8,128)S(1)}, f32[56,1152]{1,0:T(8,128)S(1)}, f32[56,1152]{1,0:T(8,128)S(1)}, f32[56,1152]{1,0:T(8,128)S(1)}) custom-call(bf16[2304,48]{1,0:T(8,128)(2,1)S(1)} %get-tuple-element.27.refs_1_.pieces, f32[8,256]{1,0:T(8,128)S(1)} %get-tuple-element.39.refs_0_, bf16[8,9216]{1,0:T(8,128)(2,1)S(1)} %get-tuple-element.34.refs_4_.refs_1_, ...), custom_call_target="tpu_custom_call" | custom-call | flops 1048576 | bytes 65536 | tf_op jit(solution)/shard_map/numerators/pallas_call | solution.py:388
  36.4 2.5 %collective-permute-start.13 = (f16[56,1152]{1,0:T(8,128)(2,1)S(1)}, f16[56,1152]{1,0:T(8,128)(2,1)S(1)}, u32[]{:S(2)}, u32[]{:S(2)}) collective-permute-start(f16[56,1152]{1,0:T(8,128)(2,1)S(1)} %convert_element_type.58), channel_id=1, source_target_pairs={{0,24},{8,16},{16,8},{24,0},{1,25},{9,17},{17,9},{25,1},{2,26},{10... | collective-permute-start | bytes 387080 | tf_op jit(solution)/shard_map/ppermute | solution.py:49
  38.9 0.6 %collective-permute-start.12 = (f16[56,1152]{1,0:T(8,128)(2,1)S(1)}, f16[56,1152]{1,0:T(8,128)(2,1)S(1)}, u32[]{:S(2)}, u32[]{:S(2)}) collective-permute-start(f16[56,1152]{1,0:T(8,128)(2,1)S(1)} %convert_element_type.56), channel_id=1, source_target_pairs={{0,16},{8,24},{16,0},{24,8},{1,17},{9,25},{17,1},{25,9},{2,18},{10... | collective-permute-start | bytes 387080 | tf_op jit(solution)/shard_map/ppermute | solution.py:49
  39.5 0.6 %collective-permute-start.11 = (f16[56,1152]{1,0:T(8,128)(2,1)S(1)}, f16[56,1152]{1,0:T(8,128)(2,1)S(1)}, u32[]{:S(2)}, u32[]{:S(2)}) collective-permute-start(f16[56,1152]{1,0:T(8,128)(2,1)S(1)} %convert_element_type.54), channel_id=1, source_target_pairs={{0,8},{8,0},{16,24},{24,16},{1,9},{9,1},{17,25},{25,17},{2,10},{10... | collective-permute-start | bytes 387080 | tf_op jit(solution)/shard_map/ppermute | solution.py:49
  40.1 0.0 collective-permute-done.6
  40.2 0.1 convert_add_fusion.1.refs_0_
  40.3 3.5 %denominators.1.denom = f32[56,2304]{1,0:T(8,128)S(1)} custom-call(bf16[2304,256]{1,0:T(8,128)(2,1)S(1)} %get-tuple-element.26.weights, f32[8,1152]{1,0:T(8,128)S(1)} %slice.12.refs_0_, f32[8,1152]{1,0:T(8,128)S(1)} %slice_convert_fusion.2.refs_1_, f32[8,1152]{1,0:T(8,128)S(1)} %slice_convert_fusion.1.refs_2_, f32[8,1152]{1,0:T(8,128)S(1)} %slice_convert_fusion.refs_3_), custom_call_target="tpu_custom_call" | custom-call | flops 1048576 | bytes 65536 | tf_op jit(solution)/shard_map/denominators/pallas_call | solution.py:438
  43.8 0.8 %collective-permute-done.12 = f16[56,1152]{1,0:T(8,128)(2,1)S(1)} collective-permute-done((f16[56,1152]{1,0:T(8,128)(2,1)S(1)}, f16[56,1152]{1,0:T(8,128)(2,1)S(1)}, u32[]{:S(2)}, u32[]{:S(2)}) %collective-permute-start.12) | collective-permute-done | bytes 129056 | tf_op jit(solution)/shard_map/ppermute | solution.py:49
  44.6 0.3 collective-permute-done.11
  44.9 0.1 convert_add_fusion.refs_1_
  45.0 0.9 %averages.1 = f32[50,2304]{1,0:T(8,128)} custom-call(f32[56,2304]{1,0:T(8,128)S(1)} %denominators.1.denom, f32[56,1152]{1,0:T(8,128)S(1)} %convert_add_fusion.1.refs_0_, f32[56,1152]{1,0:T(8,128)S(1)} %convert_add_fusion.refs_1_), custom_call_target="tpu_custom_call" | custom-call | flops 1048576 | bytes 65536 | tf_op jit(solution)/shard_map/averages/pallas_call | solution.py:458
  (21 shorter events, 0.2 us)
Async XLA Ops:
  0.7 1.3 %copy-start = (bf16[32,18432]{1,0:T(8,128)(2,1)S(1)}, bf16[32,18432]{1,0:T(8,128)(2,1)}, u32[]{:S(2)}) copy-start(bf16[32,18432]{1,0:T(8,128)(2,1)} %img.1) | copy-start | bytes 3538948
  2.0 5.9 %copy-start.1 = (f32[16,18432]{1,0:T(8,128)S(1)}, f32[16,18432]{1,0:T(8,128)}, u32[]{:S(2)}) copy-start(f32[16,18432]{1,0:T(8,128)} %table.1) | copy-start | bytes 3538948
  2.1 10.0 %collective-permute-start.3 = (bf16[4,8,4608]{2,1,0:T(8,128)(2,1)S(1)}, bf16[4,8,4608]{2,1,0:T(8,128)(2,1)S(1)}, u32[]{:S(2)}, u32[]{:S(2)}) collective-permute-start(bf16[4,8,4608]{2,1,0:T(8,128)(2,1)S(1)} %get-tuple-element.33), channel_id=1, source_target_pairs={{0,1},{1,0},{2,3},{3,2},{4,5},{5,4},{6,7},{7,6},{8,9},{9,8},{10,11... | collective-permute-start | bytes 884744 | tf_op jit(solution)/shard_map/ppermute | solution.py:49
  2.6 9.5 %collective-permute-start.2 = (bf16[8,9344]{1,0:T(8,128)(2,1)S(1)}, bf16[8,9344]{1,0:T(8,128)(2,1)S(1)}, u32[]{:S(2)}, u32[]{:S(2)}) collective-permute-start(bf16[8,9344]{1,0:T(8,128)(2,1)S(1)} %get-tuple-element.31), channel_id=1, source_target_pairs={{0,6},{1,7},{2,4},{3,5},{4,2},{5,3},{6,0},{7,1},{8,14},{9,15},{10,... | collective-permute-start | bytes 448520 | tf_op jit(solution)/shard_map/ppermute | solution.py:49
  7.3 8.8 %collective-permute-start = (bf16[8,9344]{1,0:T(8,128)(2,1)S(1)}, bf16[8,9344]{1,0:T(8,128)(2,1)S(1)}, u32[]{:S(2)}, u32[]{:S(2)}) collective-permute-start(bf16[8,9344]{1,0:T(8,128)(2,1)S(1)} %get-tuple-element.29), channel_id=1, source_target_pairs={{0,2},{1,3},{2,0},{3,1},{4,6},{5,7},{6,4},{7,5},{8,10},{9,11},{10,... | collective-permute-start | bytes 448520 | tf_op jit(solution)/shard_map/ppermute | solution.py:49
  7.3 13.3 %collective-permute-start.1 = (bf16[8,9344]{1,0:T(8,128)(2,1)S(1)}, bf16[8,9344]{1,0:T(8,128)(2,1)S(1)}, u32[]{:S(2)}, u32[]{:S(2)}) collective-permute-start(bf16[8,9344]{1,0:T(8,128)(2,1)S(1)} %get-tuple-element.30), channel_id=1, source_target_pairs={{0,4},{1,5},{2,6},{3,7},{4,0},{5,1},{6,2},{7,3},{8,12},{9,13},{10,... | collective-permute-start | bytes 448520 | tf_op jit(solution)/shard_map/ppermute | solution.py:49
  20.6 4.5 %collective-permute-start.4 = (bf16[4,8,4736]{2,1,0:T(8,128)(2,1)S(1)}, bf16[4,8,4736]{2,1,0:T(8,128)(2,1)S(1)}, u32[]{:S(2)}, u32[]{:S(2)}) collective-permute-start(bf16[4,8,4736]{2,1,0:T(8,128)(2,1)S(1)} %cross.1), channel_id=1, source_target_pairs={{0,1},{1,0},{2,3},{3,2},{4,5},{5,4},{6,7},{7,6},{8,9},{9,8},{10,11... | collective-permute-start | bytes 909320 | tf_op jit(solution)/shard_map/ppermute | solution.py:49
  20.6 9.3 %collective-permute-start.8 = (bf16[8,9216]{1,0:T(8,128)(2,1)S(1)}, bf16[8,9216]{1,0:T(8,128)(2,1)S(1)}, u32[]{:S(2)}, u32[]{:S(2)}) collective-permute-start(bf16[8,9216]{1,0:T(8,128)(2,1)S(1)} %get-tuple-element.40), channel_id=1, source_target_pairs={{0,2},{1,3},{2,0},{3,1},{4,6},{5,7},{6,4},{7,5},{8,10},{9,11},{10,... | collective-permute-start | bytes 442376 | tf_op jit(solution)/shard_map/ppermute | solution.py:49
  20.7 14.0 %collective-permute-start.9 = (bf16[8,9216]{1,0:T(8,128)(2,1)S(1)}, bf16[8,9216]{1,0:T(8,128)(2,1)S(1)}, u32[]{:S(2)}, u32[]{:S(2)}) collective-permute-start(bf16[8,9216]{1,0:T(8,128)(2,1)S(1)} %get-tuple-element.41), channel_id=1, source_target_pairs={{0,4},{1,5},{2,6},{3,7},{4,0},{5,1},{6,2},{7,3},{8,12},{9,13},{10,... | collective-permute-start | bytes 442376 | tf_op jit(solution)/shard_map/ppermute | solution.py:49
  23.7 11.0 %collective-permute-start.10 = (bf16[8,9216]{1,0:T(8,128)(2,1)S(1)}, bf16[8,9216]{1,0:T(8,128)(2,1)S(1)}, u32[]{:S(2)}, u32[]{:S(2)}) collective-permute-start(bf16[8,9216]{1,0:T(8,128)(2,1)S(1)} %get-tuple-element.42), channel_id=1, source_target_pairs={{0,6},{1,7},{2,4},{3,5},{4,2},{5,3},{6,0},{7,1},{8,14},{9,15},{10,... | collective-permute-start | bytes 442376 | tf_op jit(solution)/shard_map/ppermute | solution.py:49
  26.8 12.8 %collective-permute-start.5 = (f16[56,1152]{1,0:T(8,128)(2,1)S(1)}, f16[56,1152]{1,0:T(8,128)(2,1)S(1)}, u32[]{:S(2)}, u32[]{:S(2)}) collective-permute-start(f16[56,1152]{1,0:T(8,128)(2,1)S(1)} %convert_element_type.45), channel_id=1, source_target_pairs={{0,8},{8,0},{16,24},{24,16},{1,9},{9,1},{17,25},{25,17},{2,10},{10... | collective-permute-start | bytes 387080 | tf_op jit(solution)/shard_map/ppermute | solution.py:49
  28.3 11.8 %collective-permute-start.6 = (f16[56,1152]{1,0:T(8,128)(2,1)S(1)}, f16[56,1152]{1,0:T(8,128)(2,1)S(1)}, u32[]{:S(2)}, u32[]{:S(2)}) collective-permute-start(f16[56,1152]{1,0:T(8,128)(2,1)S(1)} %convert_element_type.47), channel_id=1, source_target_pairs={{0,16},{8,24},{16,0},{24,8},{1,17},{9,25},{17,1},{25,9},{2,18},{10... | collective-permute-start | bytes 387080 | tf_op jit(solution)/shard_map/ppermute | solution.py:49
  30.0 10.2 %collective-permute-start.7 = (f16[56,1152]{1,0:T(8,128)(2,1)S(1)}, f16[56,1152]{1,0:T(8,128)(2,1)S(1)}, u32[]{:S(2)}, u32[]{:S(2)}) collective-permute-start(f16[56,1152]{1,0:T(8,128)(2,1)S(1)} %convert_element_type.49), channel_id=1, source_target_pairs={{0,24},{8,16},{16,8},{24,0},{1,25},{9,17},{17,9},{25,1},{2,26},{10... | collective-permute-start | bytes 387080 | tf_op jit(solution)/shard_map/ppermute | solution.py:49
  36.4 7.4 %collective-permute-start.13 = (f16[56,1152]{1,0:T(8,128)(2,1)S(1)}, f16[56,1152]{1,0:T(8,128)(2,1)S(1)}, u32[]{:S(2)}, u32[]{:S(2)}) collective-permute-start(f16[56,1152]{1,0:T(8,128)(2,1)S(1)} %convert_element_type.58), channel_id=1, source_target_pairs={{0,24},{8,16},{16,8},{24,0},{1,25},{9,17},{17,9},{25,1},{2,26},{10... | collective-permute-start | bytes 387080 | tf_op jit(solution)/shard_map/ppermute | solution.py:49
  38.9 5.6 %collective-permute-start.12 = (f16[56,1152]{1,0:T(8,128)(2,1)S(1)}, f16[56,1152]{1,0:T(8,128)(2,1)S(1)}, u32[]{:S(2)}, u32[]{:S(2)}) collective-permute-start(f16[56,1152]{1,0:T(8,128)(2,1)S(1)} %convert_element_type.56), channel_id=1, source_target_pairs={{0,16},{8,24},{16,0},{24,8},{1,17},{9,25},{17,1},{25,9},{2,18},{10... | collective-permute-start | bytes 387080 | tf_op jit(solution)/shard_map/ppermute | solution.py:49
  39.5 5.3 %collective-permute-start.11 = (f16[56,1152]{1,0:T(8,128)(2,1)S(1)}, f16[56,1152]{1,0:T(8,128)(2,1)S(1)}, u32[]{:S(2)}, u32[]{:S(2)}) collective-permute-start(f16[56,1152]{1,0:T(8,128)(2,1)S(1)} %convert_element_type.54), channel_id=1, source_target_pairs={{0,8},{8,0},{16,24},{24,16},{1,9},{9,1},{17,25},{25,17},{2,10},{10... | collective-permute-start | bytes 387080 | tf_op jit(solution)/shard_map/ppermute | solution.py:49

commit v4 on v3

--- a/solution.py
+++ b/solution.py
@@ -246,31 +246,28 @@
     )(table)
 
 
-def tag_spots(lanes, span):
-    wide = span // LANES * LANES
-    parts = -(-lanes // wide)
-    spots = []
-    for kind in range(3):
-        for part in range(parts):
-            spots.append((kind, CPG + kind * parts + part, part * wide, min(wide, lanes - part * wide)))
-    return spots
-
-
-def sum_rows(lanes, span):
-    last = tag_spots(lanes, span)[-1][1] + 1
-    return -(-last // ROWS) * ROWS
-
-
-def tag_block(message, lanes):
-    low = CPG // ROWS * ROWS
+def stacked(span):
+    return [(low // LANES, min(LANES, span - low)) for low in range(0, span, LANES)]
+
+
+def sum_rows(span, lanes):
+    used = CPG * len(stacked(span)) + 3 * lanes // LANES
+    return -(-used // ROWS) * ROWS
+
+
+def tag_block(message, span):
+    low = CPG * len(stacked(span)) // ROWS * ROWS
     return message[low:].astype(F32)
 
 
-def read_tags(ref, lanes):
-    kinds = [[], [], []]
-    for kind, row, _, width in tag_spots(lanes, ref.shape[1]):
-        kinds[kind].append(ref[pl.ds(row - CPG // ROWS * ROWS, 1), pl.ds(0, width)])
-    return [jnp.concatenate(kind, axis=1) if len(kind) > 1 else kind[0] for kind in kinds]
+def read_tags(ref, span, lanes):
+    rows = CPG * len(stacked(span))
+    parts = lanes // LANES
+    low = rows - rows // ROWS * ROWS
+    return [
+        jnp.concatenate([ref[pl.ds(low + kind * parts + part, 1), :] for part in range(parts)], axis=1)
+        for kind in range(3)
+    ]
 
 
 def numer_kernel(mem, count, first, rows, base, tiles, segments, pieces, *refs):
@@ -357,13 +354,19 @@
         jnp.concatenate(member, axis=0), parts[...], NT, preferred_element_type=F32
     )
     for step in range(grp):
-        sums[step][pl.ds(0, CPAD)] = result[step * CPAD : (step + 1) * CPAD]
+        for tile, width in stacked(result.shape[1]):
+            here = (pl.ds(tile * CPG, CPG), pl.ds(0, width))
+            value = result[step * CPAD : step * CPAD + CPG, tile * LANES : tile * LANES + width]
+            sums[step][here] = value
         if first:
             target = partner(own, step, grp)
             local = jnp.where(label[0:1] == target, label[1:2], -1)
-            kinds = [kind.astype(F32) for kind in (local, spot, turn)]
-            for kind, row, low, width in tag_spots(lanes, sums[step].shape[1]):
-                sums[step][pl.ds(row, 1), pl.ds(0, width)] = kinds[kind][:, low : low + width]
+            row = CPG * len(stacked(result.shape[1]))
+            for kind in (local, spot, turn):
+                for tile in range(lanes // LANES):
+                    value = kind[:, tile * LANES : (tile + 1) * LANES].astype(F32)
+                    sums[step][pl.ds(row, 1), :] = value
+                    row += 1
 
 
 def numerators(count, pieces, tags, arrived, chunk, edges, rows):
@@ -382,8 +385,8 @@
     span = (here[1] - here[0]) * ANGLES
     tiles = stop - base
     shapes = [jax.ShapeDtypeStruct((ROWS, lanes), F32)] if first else []
-    tall = sum_rows(lanes, span) if first else CPAD
-    shapes += [jax.ShapeDtypeStruct((tall, span), F32)] * grp
+    tall = sum_rows(span, lanes if first else 0)
+    shapes += [jax.ShapeDtypeStruct((tall, LANES), F32)] * grp
     operands = [pieces] + ([] if first else [tags]) + msgs
     outs = pl.pallas_call(
         functools.partial(numer_kernel, mem, count, first, here, base, tiles, tuple(segments)),
@@ -403,14 +406,14 @@
     return tags, outs
 
 
-def denom_kernel(lanes, weights, *refs):
+def denom_kernel(first, lanes, weights, *refs):
     blocks, (denom, spread) = refs[:-2], refs[-2:]
     span = weights.shape[0]
     klass = lax.broadcasted_iota(jnp.int32, (CPAD, lanes), 0)
     pair = lax.broadcasted_iota(jnp.int32, (PAIRS, lanes), 0)
     count = jnp.zeros((CPAD, PAIRS), F32)
     for ref in blocks:
-        local, spot, turn = [label.astype(jnp.int32) for label in read_tags(ref, lanes)]
+        local, spot, turn = [label.astype(jnp.int32) for label in read_tags(ref, first, lanes)]
         member = (klass == local).astype(BF16)
         which = (pair == turn * BINS + spot).astype(BF16)
         count += lax.dot_general(member, which, NT, preferred_element_type=F32)
@@ -433,10 +436,10 @@
     denom[...] = both[:CPAD] + both[CPAD:]
 
 
-def denominators(weights, blocks, lanes):
+def denominators(weights, blocks, first, lanes):
     span = weights.shape[0]
     return pl.pallas_call(
-        functools.partial(denom_kernel, lanes),
+        functools.partial(denom_kernel, first, lanes),
         out_shape=jax.ShapeDtypeStruct((CPAD, span), F32),
         in_specs=[VMEM] * (1 + len(blocks)),
         out_specs=VMEM,
@@ -449,8 +452,10 @@
 def average_kernel(rows, denom, *refs):
     sums, out = refs[:-1], refs[-1]
     for chunk in range(len(rows) - 1):
-        across = pl.ds(rows[chunk] * ANGLES, (rows[chunk + 1] - rows[chunk]) * ANGLES)
-        out[:, across] = sums[chunk][:CPG] / (denom[:CPG, across] + wiener_term)
+        for tile, width in stacked((rows[chunk + 1] - rows[chunk]) * ANGLES):
+            across = pl.ds(rows[chunk] * ANGLES + tile * LANES, width)
+            total = sums[chunk][pl.ds(tile * CPG, CPG), pl.ds(0, width)]
+            out[:, across] = total / (denom[:CPG, across] + wiener_term)
 
 
 def averages(denom, sums, rows):
@@ -505,12 +510,12 @@
         tags, here = numerators(count, pieces, tags, arrived, chunk, edges, rows)
         others = [send(here[step].astype(HALF), "grp", step) for step in range(1, grp)]
         if chunk == 0:
-            blocks = [tag_block(part, mem * count) for part in [here[0]] + others]
+            blocks = [tag_block(part, rows[1] * ANGLES) for part in [here[0]] + others]
         total = here[0]
         for part in others:
             total = total + part.astype(F32)
         sums.append(total)
-    denom = denominators(weights, blocks, mem * count)
+    denom = denominators(weights, blocks, rows[1] * ANGLES, mem * count)
     return averages(denom, sums, rows)
 
 

time: 46.6 us -> 46.1 us (0.989)
  transfers between devices with their start and end apart: 14 -> 14, of which waited for: 6 -> 6; matrix products, arithmetic and copies ran while one was open for 0% -> 0% of each run, Pallas kernels for 17% -> 18%
where the time goes in v4:
time: 46.1 us; the launch traced here: 45.4 us
  starting transfers between devices  19.4 us (42%)
  waiting for transfers between devices  14.7 us (32%)
  Pallas kernels  9.04 us (20%)
  local copies, waits for them, and re-layouts  1.27 us (3%)
  other arithmetic  0.97 us (2%)
    ppermute x14, starting transfers between devices, send(): return lax.ppermute(value, axis, pairs)  19.4 us
    ppermute x14, waiting for transfers between devices, send(): return lax.ppermute(value, axis, pairs)  14.7 us
    pallas_call x1, Pallas kernels, denominators(): pl.pallas_call(functools.partial(denom_kernel, first, lanes), out_shape=j...  3.53 us
    pallas_call x2, Pallas kernels, numerators(): pl.pallas_call(functools.partial(numer_kernel, mem, count, first, here, b...  3.25 us
    unnamed x4, local copies, waits for them, and re-layouts  1.27 us
    pallas_call x1, Pallas kernels, tables(): pl.pallas_call(functools.partial(table_kernel, turns), out_shape=[jax.Sha...  1.17 us
  transfers between devices with their start and end apart: 14, of which 6 were waited for; matrix products, arithmetic and copies ran while one was open for 0% of the time, Pallas kernels for 18%

profile of v4, /device:TPU:0, one launch (start us, length us, event | category | flops | bytes accessed | tf_op | source)
XLA Modules:
  0.0 45.4 jit_solution(3986176906107929890)
XLA Ops:
  0.0 0.7 %pad_add_fusion.labels = s32[3,32]{1,0:T(4,128)S(1)} fusion(s32[1,32]{1,0:T(1,128)} %bitcast.3, s32[1,32]{1,0:T(1,128)} %bitcast.4, s32[1,32]{1,0:T(1,128)} %bitcast.5), kind=kLoop, calls=%fused_computation.5 | loop fusion | flops 192 | bytes 768 | tf_op jit(solution)/shard_map/stack | solution.py:495
  0.7 1.3 %copy-done = bf16[32,18432]{1,0:T(8,128)(2,1)S(1)} copy-done((bf16[32,18432]{1,0:T(8,128)(2,1)S(1)}, bf16[32,18432]{1,0:T(8,128)(2,1)}, u32[]{:S(2)}) %copy-start) | copy-done | bytes 1179672
  2.0 0.1 pack.1
  2.1 0.5 %collective-permute-start.3 = (bf16[4,8,4608]{2,1,0:T(8,128)(2,1)S(1)}, bf16[4,8,4608]{2,1,0:T(8,128)(2,1)S(1)}, u32[]{:S(2)}, u32[]{:S(2)}) collective-permute-start(bf16[4,8,4608]{2,1,0:T(8,128)(2,1)S(1)} %get-tuple-element.33), channel_id=1, source_target_pairs={{0,1},{1,0},{2,3},{3,2},{4,5},{5,4},{6,7},{7,6},{8,9},{9,8},{10,11... | collective-permute-start | bytes 884744 | tf_op jit(solution)/shard_map/ppermute | solution.py:49
  2.6 4.7 %collective-permute-start.2 = (bf16[8,9344]{1,0:T(8,128)(2,1)S(1)}, bf16[8,9344]{1,0:T(8,128)(2,1)S(1)}, u32[]{:S(2)}, u32[]{:S(2)}) collective-permute-start(bf16[8,9344]{1,0:T(8,128)(2,1)S(1)} %get-tuple-element.31), channel_id=1, source_target_pairs={{0,6},{1,7},{2,4},{3,5},{4,2},{5,3},{6,0},{7,1},{8,14},{9,15},{10,... | collective-permute-start | bytes 448520 | tf_op jit(solution)/shard_map/ppermute | solution.py:49
  7.3 0.0 collective-permute-start
  7.3 0.6 %collective-permute-start.1 = (bf16[8,9344]{1,0:T(8,128)(2,1)S(1)}, bf16[8,9344]{1,0:T(8,128)(2,1)S(1)}, u32[]{:S(2)}, u32[]{:S(2)}) collective-permute-start(bf16[8,9344]{1,0:T(8,128)(2,1)S(1)} %get-tuple-element.30), channel_id=1, source_target_pairs={{0,4},{1,5},{2,6},{3,7},{4,0},{5,1},{6,2},{7,3},{8,12},{9,13},{10,... | collective-permute-start | bytes 448520 | tf_op jit(solution)/shard_map/ppermute | solution.py:49
  7.9 1.2 %tables.1 = (bf16[2304,48]{1,0:T(8,128)(2,1)S(1)}, bf16[2304,256]{1,0:T(8,128)(2,1)S(1)}) custom-call(f32[16,18432]{1,0:T(8,128)S(1)} %copy-done.1), custom_call_target="tpu_custom_call" | custom-call | flops 1048576 | bytes 65536 | tf_op jit(solution)/shard_map/tables/pallas_call | solution.py:231
  9.1 3.0 %collective-permute-done.2.refs_0_.refs_3_ = bf16[8,9344]{1,0:T(8,128)(2,1)S(1)} collective-permute-done((bf16[8,9344]{1,0:T(8,128)(2,1)S(1)}, bf16[8,9344]{1,0:T(8,128)(2,1)S(1)}, u32[]{:S(2)}, u32[]{:S(2)}) %collective-permute-start.2) | collective-permute-done | bytes 149536 | tf_op jit(solution)/shard_map/ppermute | solution.py:49
  12.1 0.0 collective-permute-done.3.crossed
  12.1 3.9 %collective-permute-done.refs_1_ = bf16[8,9344]{1,0:T(8,128)(2,1)S(1)} collective-permute-done((bf16[8,9344]{1,0:T(8,128)(2,1)S(1)}, bf16[8,9344]{1,0:T(8,128)(2,1)S(1)}, u32[]{:S(2)}, u32[]{:S(2)}) %collective-permute-start) | collective-permute-done | bytes 149536 | tf_op jit(solution)/shard_map/ppermute | solution.py:49
  16.0 4.5 %collective-permute-done.1.refs_2_ = bf16[8,9344]{1,0:T(8,128)(2,1)S(1)} collective-permute-done((bf16[8,9344]{1,0:T(8,128)(2,1)S(1)}, bf16[8,9344]{1,0:T(8,128)(2,1)S(1)}, u32[]{:S(2)}, u32[]{:S(2)}) %collective-permute-start.1) | collective-permute-done | bytes 149536 | tf_op jit(solution)/shard_map/ppermute | solution.py:49
  20.6 0.1 collective-permute-start.4
  20.6 0.1 collective-permute-start.8
  20.7 3.0 %collective-permute-start.9 = (bf16[8,9216]{1,0:T(8,128)(2,1)S(1)}, bf16[8,9216]{1,0:T(8,128)(2,1)S(1)}, u32[]{:S(2)}, u32[]{:S(2)}) collective-permute-start(bf16[8,9216]{1,0:T(8,128)(2,1)S(1)} %get-tuple-element.41), channel_id=1, source_target_pairs={{0,4},{1,5},{2,6},{3,7},{4,0},{5,1},{6,2},{7,3},{8,12},{9,13},{10,... | collective-permute-start | bytes 442376 | tf_op jit(solution)/shard_map/ppermute | solution.py:49
  23.7 1.3 %collective-permute-start.10 = (bf16[8,9216]{1,0:T(8,128)(2,1)S(1)}, bf16[8,9216]{1,0:T(8,128)(2,1)S(1)}, u32[]{:S(2)}, u32[]{:S(2)}) collective-permute-start(bf16[8,9216]{1,0:T(8,128)(2,1)S(1)} %get-tuple-element.42), channel_id=1, source_target_pairs={{0,6},{1,7},{2,4},{3,5},{4,2},{5,3},{6,0},{7,1},{8,14},{9,15},{10,... | collective-permute-start | bytes 442376 | tf_op jit(solution)/shard_map/ppermute | solution.py:49
  25.1 1.6 %numerators.2 = (f32[8,256]{1,0:T(8,128)S(1)}, f32[456,128]{1,0:T(8,128)S(1)}, f32[456,128]{1,0:T(8,128)S(1)}, f32[456,128]{1,0:T(8,128)S(1)}, f32[456,128]{1,0:T(8,128)S(1)}) custom-call(bf16[2304,48]{1,0:T(8,128)(2,1)S(1)} %get-tuple-element.27.refs_1_.pieces, bf16[8,9344]{1,0:T(8,128)(2,1)S(1)} %get-tuple-element.28.refs_0_, ...), custom_call_target="tpu_custom_call" | custom-call | flops 1048576 | bytes 65536 | tf_op jit(solution)/shard_map/numerators/pallas_call | solution.py:391
  26.8 1.6 %collective-permute-start.5 = (f16[456,128]{1,0:T(8,128)(2,1)S(1)}, f16[456,128]{1,0:T(8,128)(2,1)S(1)}, u32[]{:S(2)}, u32[]{:S(2)}) collective-permute-start(f16[456,128]{1,0:T(8,128)(2,1)S(1)} %convert_element_type.45), channel_id=1, source_target_pairs={{0,8},{8,0},{16,24},{24,16},{1,9},{9,1},{17,25},{25,17},{2,10},{10... | collective-permute-start | bytes 350216 | tf_op jit(solution)/shard_map/ppermute | solution.py:49
  28.4 1.6 %collective-permute-start.6 = (f16[456,128]{1,0:T(8,128)(2,1)S(1)}, f16[456,128]{1,0:T(8,128)(2,1)S(1)}, u32[]{:S(2)}, u32[]{:S(2)}) collective-permute-start(f16[456,128]{1,0:T(8,128)(2,1)S(1)} %convert_element_type.47), channel_id=1, source_target_pairs={{0,16},{8,24},{16,0},{24,8},{1,17},{9,25},{17,1},{25,9},{2,18},{10... | collective-permute-start | bytes 350216 | tf_op jit(solution)/shard_map/ppermute | solution.py:49
  30.0 2.2 %collective-permute-start.7 = (f16[456,128]{1,0:T(8,128)(2,1)S(1)}, f16[456,128]{1,0:T(8,128)(2,1)S(1)}, u32[]{:S(2)}, u32[]{:S(2)}) collective-permute-start(f16[456,128]{1,0:T(8,128)(2,1)S(1)} %convert_element_type.49), channel_id=1, source_target_pairs={{0,24},{8,16},{16,8},{24,0},{1,25},{9,17},{17,9},{25,1},{2,26},{10... | collective-permute-start | bytes 350216 | tf_op jit(solution)/shard_map/ppermute | solution.py:49
  32.2 2.6 %collective-permute-done.9.refs_3_ = bf16[8,9216]{1,0:T(8,128)(2,1)S(1)} collective-permute-done((bf16[8,9216]{1,0:T(8,128)(2,1)S(1)}, bf16[8,9216]{1,0:T(8,128)(2,1)S(1)}, u32[]{:S(2)}, u32[]{:S(2)}) %collective-permute-start.9) | collective-permute-done | bytes 147488 | tf_op jit(solution)/shard_map/ppermute | solution.py:49
  34.7 1.6 %numerators.3 = (f32[456,128]{1,0:T(8,128)S(1)}, f32[456,128]{1,0:T(8,128)S(1)}, f32[456,128]{1,0:T(8,128)S(1)}, f32[456,128]{1,0:T(8,128)S(1)}) custom-call(bf16[2304,48]{1,0:T(8,128)(2,1)S(1)} %get-tuple-element.27.refs_1_.pieces, f32[8,256]{1,0:T(8,128)S(1)} %get-tuple-element.39.refs_0_, bf16[8,9216]{1,0:T(8,128)(2,1)S(1)} %get-tuple-element.34.refs_4_.refs_1_, ...), custom_call_target="tpu_custom_call" | custom-call | flops 1048576 | bytes 65536 | tf_op jit(solution)/shard_map/numerators/pallas_call | solution.py:391
  36.4 2.5 %collective-permute-start.13 = (f16[456,128]{1,0:T(8,128)(2,1)S(1)}, f16[456,128]{1,0:T(8,128)(2,1)S(1)}, u32[]{:S(2)}, u32[]{:S(2)}) collective-permute-start(f16[456,128]{1,0:T(8,128)(2,1)S(1)} %convert_element_type.58), channel_id=1, source_target_pairs={{0,24},{8,16},{16,8},{24,0},{1,25},{9,17},{17,9},{25,1},{2,26},{10... | collective-permute-start | bytes 350216 | tf_op jit(solution)/shard_map/ppermute | solution.py:49
  38.9 0.6 %collective-permute-start.12 = (f16[456,128]{1,0:T(8,128)(2,1)S(1)}, f16[456,128]{1,0:T(8,128)(2,1)S(1)}, u32[]{:S(2)}, u32[]{:S(2)}) collective-permute-start(f16[456,128]{1,0:T(8,128)(2,1)S(1)} %convert_element_type.56), channel_id=1, source_target_pairs={{0,16},{8,24},{16,0},{24,8},{1,17},{9,25},{17,1},{25,9},{2,18},{10... | collective-permute-start | bytes 350216 | tf_op jit(solution)/shard_map/ppermute | solution.py:49
  39.5 0.0 collective-permute-done.5
  39.5 0.6 %collective-permute-start.11 = (f16[456,128]{1,0:T(8,128)(2,1)S(1)}, f16[456,128]{1,0:T(8,128)(2,1)S(1)}, u32[]{:S(2)}, u32[]{:S(2)}) collective-permute-start(f16[456,128]{1,0:T(8,128)(2,1)S(1)} %convert_element_type.54), channel_id=1, source_target_pairs={{0,8},{8,0},{16,24},{24,16},{1,9},{9,1},{17,25},{25,17},{2,10},{10... | collective-permute-start | bytes 350216 | tf_op jit(solution)/shard_map/ppermute | solution.py:49
  40.2 0.1 convert_add_fusion.1.refs_0_
  40.2 3.5 %denominators.1.denom = f32[56,2304]{1,0:T(8,128)S(1)} custom-call(bf16[2304,256]{1,0:T(8,128)(2,1)S(1)} %get-tuple-element.26.weights, f32[8,128]{1,0:T(8,128)S(1)} %slice.12.refs_0_, f32[8,128]{1,0:T(8,128)S(1)} %slice_convert_fusion.2.refs_1_, f32[8,128]{1,0:T(8,128)S(1)} %slice_convert_fusion.1.refs_2_, f32[8,128]{1,0:T(8,128)S(1)} %slice_convert_fusion.refs_3_), custom_call_target="tpu_custom_call" | custom-call | flops 1048576 | bytes 65536 | tf_op jit(solution)/shard_map/denominators/pallas_call | solution.py:441
  43.8 0.4 collective-permute-done.12
  44.2 0.3 collective-permute-done.11
  44.5 0.1 convert_add_fusion.refs_1_
  44.6 0.9 %averages.1 = f32[50,2304]{1,0:T(8,128)} custom-call(f32[56,2304]{1,0:T(8,128)S(1)} %denominators.1.denom, f32[456,128]{1,0:T(8,128)S(1)} %convert_add_fusion.1.refs_0_, f32[456,128]{1,0:T(8,128)S(1)} %convert_add_fusion.refs_1_), custom_call_target="tpu_custom_call" | custom-call | flops 1048576 | bytes 65536 | tf_op jit(solution)/shard_map/averages/pallas_call | solution.py:463
  (21 shorter events, 0.2 us)
Async XLA Ops:
  0.7 1.3 %copy-start = (bf16[32,18432]{1,0:T(8,128)(2,1)S(1)}, bf16[32,18432]{1,0:T(8,128)(2,1)}, u32[]{:S(2)}) copy-start(bf16[32,18432]{1,0:T(8,128)(2,1)} %img.1) | copy-start | bytes 3538948
  2.0 5.9 %copy-start.1 = (f32[16,18432]{1,0:T(8,128)S(1)}, f32[16,18432]{1,0:T(8,128)}, u32[]{:S(2)}) copy-start(f32[16,18432]{1,0:T(8,128)} %table.1) | copy-start | bytes 3538948
  2.1 10.0 %collective-permute-start.3 = (bf16[4,8,4608]{2,1,0:T(8,128)(2,1)S(1)}, bf16[4,8,4608]{2,1,0:T(8,128)(2,1)S(1)}, u32[]{:S(2)}, u32[]{:S(2)}) collective-permute-start(bf16[4,8,4608]{2,1,0:T(8,128)(2,1)S(1)} %get-tuple-element.33), channel_id=1, source_target_pairs={{0,1},{1,0},{2,3},{3,2},{4,5},{5,4},{6,7},{7,6},{8,9},{9,8},{10,11... | collective-permute-start | bytes 884744 | tf_op jit(solution)/shard_map/ppermute | solution.py:49
  2.6 9.5 %collective-permute-start.2 = (bf16[8,9344]{1,0:T(8,128)(2,1)S(1)}, bf16[8,9344]{1,0:T(8,128)(2,1)S(1)}, u32[]{:S(2)}, u32[]{:S(2)}) collective-permute-start(bf16[8,9344]{1,0:T(8,128)(2,1)S(1)} %get-tuple-element.31), channel_id=1, source_target_pairs={{0,6},{1,7},{2,4},{3,5},{4,2},{5,3},{6,0},{7,1},{8,14},{9,15},{10,... | collective-permute-start | bytes 448520 | tf_op jit(solution)/shard_map/ppermute | solution.py:49
  7.3 8.8 %collective-permute-start = (bf16[8,9344]{1,0:T(8,128)(2,1)S(1)}, bf16[8,9344]{1,0:T(8,128)(2,1)S(1)}, u32[]{:S(2)}, u32[]{:S(2)}) collective-permute-start(bf16[8,9344]{1,0:T(8,128)(2,1)S(1)} %get-tuple-element.29), channel_id=1, source_target_pairs={{0,2},{1,3},{2,0},{3,1},{4,6},{5,7},{6,4},{7,5},{8,10},{9,11},{10,... | collective-permute-start | bytes 448520 | tf_op jit(solution)/shard_map/ppermute | solution.py:49
  7.3 13.3 %collective-permute-start.1 = (bf16[8,9344]{1,0:T(8,128)(2,1)S(1)}, bf16[8,9344]{1,0:T(8,128)(2,1)S(1)}, u32[]{:S(2)}, u32[]{:S(2)}) collective-permute-start(bf16[8,9344]{1,0:T(8,128)(2,1)S(1)} %get-tuple-element.30), channel_id=1, source_target_pairs={{0,4},{1,5},{2,6},{3,7},{4,0},{5,1},{6,2},{7,3},{8,12},{9,13},{10,... | collective-permute-start | bytes 448520 | tf_op jit(solution)/shard_map/ppermute | solution.py:49
  20.6 4.5 %collective-permute-start.4 = (bf16[4,8,4736]{2,1,0:T(8,128)(2,1)S(1)}, bf16[4,8,4736]{2,1,0:T(8,128)(2,1)S(1)}, u32[]{:S(2)}, u32[]{:S(2)}) collective-permute-start(bf16[4,8,4736]{2,1,0:T(8,128)(2,1)S(1)} %cross.1), channel_id=1, source_target_pairs={{0,1},{1,0},{2,3},{3,2},{4,5},{5,4},{6,7},{7,6},{8,9},{9,8},{10,11... | collective-permute-start | bytes 909320 | tf_op jit(solution)/shard_map/ppermute | solution.py:49
  20.6 9.3 %collective-permute-start.8 = (bf16[8,9216]{1,0:T(8,128)(2,1)S(1)}, bf16[8,9216]{1,0:T(8,128)(2,1)S(1)}, u32[]{:S(2)}, u32[]{:S(2)}) collective-permute-start(bf16[8,9216]{1,0:T(8,128)(2,1)S(1)} %get-tuple-element.40), channel_id=1, source_target_pairs={{0,2},{1,3},{2,0},{3,1},{4,6},{5,7},{6,4},{7,5},{8,10},{9,11},{10,... | collective-permute-start | bytes 442376 | tf_op jit(solution)/shard_map/ppermute | solution.py:49
  20.7 14.0 %collective-permute-start.9 = (bf16[8,9216]{1,0:T(8,128)(2,1)S(1)}, bf16[8,9216]{1,0:T(8,128)(2,1)S(1)}, u32[]{:S(2)}, u32[]{:S(2)}) collective-permute-start(bf16[8,9216]{1,0:T(8,128)(2,1)S(1)} %get-tuple-element.41), channel_id=1, source_target_pairs={{0,4},{1,5},{2,6},{3,7},{4,0},{5,1},{6,2},{7,3},{8,12},{9,13},{10,... | collective-permute-start | bytes 442376 | tf_op jit(solution)/shard_map/ppermute | solution.py:49
  23.7 11.0 %collective-permute-start.10 = (bf16[8,9216]{1,0:T(8,128)(2,1)S(1)}, bf16[8,9216]{1,0:T(8,128)(2,1)S(1)}, u32[]{:S(2)}, u32[]{:S(2)}) collective-permute-start(bf16[8,9216]{1,0:T(8,128)(2,1)S(1)} %get-tuple-element.42), channel_id=1, source_target_pairs={{0,6},{1,7},{2,4},{3,5},{4,2},{5,3},{6,0},{7,1},{8,14},{9,15},{10,... | collective-permute-start | bytes 442376 | tf_op jit(solution)/shard_map/ppermute | solution.py:49
  26.8 12.8 %collective-permute-start.5 = (f16[456,128]{1,0:T(8,128)(2,1)S(1)}, f16[456,128]{1,0:T(8,128)(2,1)S(1)}, u32[]{:S(2)}, u32[]{:S(2)}) collective-permute-start(f16[456,128]{1,0:T(8,128)(2,1)S(1)} %convert_element_type.45), channel_id=1, source_target_pairs={{0,8},{8,0},{16,24},{24,16},{1,9},{9,1},{17,25},{25,17},{2,10},{10... | collective-permute-start | bytes 350216 | tf_op jit(solution)/shard_map/ppermute | solution.py:49
  28.4 11.8 %collective-permute-start.6 = (f16[456,128]{1,0:T(8,128)(2,1)S(1)}, f16[456,128]{1,0:T(8,128)(2,1)S(1)}, u32[]{:S(2)}, u32[]{:S(2)}) collective-permute-start(f16[456,128]{1,0:T(8,128)(2,1)S(1)} %convert_element_type.47), channel_id=1, source_target_pairs={{0,16},{8,24},{16,0},{24,8},{1,17},{9,25},{17,1},{25,9},{2,18},{10... | collective-permute-start | bytes 350216 | tf_op jit(solution)/shard_map/ppermute | solution.py:49
  30.0 10.2 %collective-permute-start.7 = (f16[456,128]{1,0:T(8,128)(2,1)S(1)}, f16[456,128]{1,0:T(8,128)(2,1)S(1)}, u32[]{:S(2)}, u32[]{:S(2)}) collective-permute-start(f16[456,128]{1,0:T(8,128)(2,1)S(1)} %convert_element_type.49), channel_id=1, source_target_pairs={{0,24},{8,16},{16,8},{24,0},{1,25},{9,17},{17,9},{25,1},{2,26},{10... | collective-permute-start | bytes 350216 | tf_op jit(solution)/shard_map/ppermute | solution.py:49
  36.4 7.4 %collective-permute-start.13 = (f16[456,128]{1,0:T(8,128)(2,1)S(1)}, f16[456,128]{1,0:T(8,128)(2,1)S(1)}, u32[]{:S(2)}, u32[]{:S(2)}) collective-permute-start(f16[456,128]{1,0:T(8,128)(2,1)S(1)} %convert_element_type.58), channel_id=1, source_target_pairs={{0,24},{8,16},{16,8},{24,0},{1,25},{9,17},{17,9},{25,1},{2,26},{10... | collective-permute-start | bytes 350216 | tf_op jit(solution)/shard_map/ppermute | solution.py:49
  38.9 5.2 %collective-permute-start.12 = (f16[456,128]{1,0:T(8,128)(2,1)S(1)}, f16[456,128]{1,0:T(8,128)(2,1)S(1)}, u32[]{:S(2)}, u32[]{:S(2)}) collective-permute-start(f16[456,128]{1,0:T(8,128)(2,1)S(1)} %convert_element_type.56), channel_id=1, source_target_pairs={{0,16},{8,24},{16,0},{24,8},{1,17},{9,25},{17,1},{25,9},{2,18},{10... | collective-permute-start | bytes 350216 | tf_op jit(solution)/shard_map/ppermute | solution.py:49
  39.5 4.9 %collective-permute-start.11 = (f16[456,128]{1,0:T(8,128)(2,1)S(1)}, f16[456,128]{1,0:T(8,128)(2,1)S(1)}, u32[]{:S(2)}, u32[]{:S(2)}) collective-permute-start(f16[456,128]{1,0:T(8,128)(2,1)S(1)} %convert_element_type.54), channel_id=1, source_target_pairs={{0,8},{8,0},{16,24},{24,16},{1,9},{9,1},{17,25},{25,17},{2,10},{10... | collective-permute-start | bytes 350216 | tf_op jit(solution)/shard_map/ppermute | solution.py:49

commit v5 on v4

--- a/solution.py
+++ b/solution.py
@@ -87,7 +87,7 @@
     owner = jnp.zeros_like(label)
     for g in range(1, lax.axis_size("grp")):
         owner += (label >= g * CPG).astype(jnp.int32)
-    row = lax.broadcasted_iota(jnp.int32, (ROWS, count), 0)
+    row = lax.broadcasted_iota(jnp.int32, (ROWS, count), 0) % (ROWS // CORES)
     stack = jnp.where(
         row == 0,
         owner,
@@ -103,6 +103,7 @@
     ).astype(BF16)
     tags = jnp.dot(stack.astype(F32).astype(BF16), spread, preferred_element_type=F32)
     place = lax.broadcasted_iota(jnp.int32, (ROWS, LANES), 1) // count
+    lower = lax.broadcasted_iota(jnp.int32, (ROWS, LANES), 0) // (ROWS // CORES)
     first = (edges[1] - edges[0]) * LANES
     for step in range(places):
         there = partner(here, step, places) * CORES
@@ -112,7 +113,8 @@
                 outs[step][:, pl.ds((target * groups + g) * first, first)] = img[
                     pl.ds(g * ROWS, ROWS), pl.ds(start, first)
                 ]
-        mine = jnp.where(place == step % (LANES // count), tags, 0.0)
+        slot = (step * CORES + lower) % (LANES // count)
+        mine = jnp.where(place == slot, tags, 0.0)
         outs[step][:, pl.ds(CORES * groups * first, LANES)] = mine.astype(BF16)
         if len(edges) == 2:
             continue
@@ -270,10 +272,10 @@
     ]
 
 
-def numer_kernel(mem, count, first, rows, base, tiles, segments, pieces, *refs):
+def numer_kernel(mem, count, first, rows, base, tiles, segments, steps, added, pieces, *refs):
     refs = list(refs)
     grp = lax.axis_size("grp")
-    lanes = mem * count
+    lanes = (steps[1] - steps[0]) * CORES * count
     groups = count // ROWS
     places = mem // CORES
     core = lax.rem(lax.axis_index("mem"), CORES)
@@ -282,11 +284,12 @@
         tags = refs.pop(0)
     for chunk, wide, src, dst, width in segments:
         across = pl.ds(dst * LANES, width * LANES)
-        msgs, refs = refs[:places], refs[places:]
+        taken = places if chunk == 0 else steps[1] - steps[0]
+        msgs, refs = refs[:taken], refs[taken:]
         if chunk == 0:
             crossed = refs.pop(0)
             past = groups * wide * LANES
-        for step in range(places):
+        for step in range(*steps):
             for g in range(groups):
                 low = (g * wide + src) * LANES
                 if chunk == 0:
@@ -294,24 +297,29 @@
                     near = msgs[step][:, pl.ds(kept, width * LANES)]
                     far = crossed[step, :, pl.ds(low, width * LANES)]
                 else:
-                    near = msgs[step][:, pl.ds(low, width * LANES)]
-                    far = msgs[step][:, pl.ds(groups * wide * LANES + low, width * LANES)]
-                refs[-3][pl.ds(step * count + g * ROWS, ROWS), across] = near
-                refs[-3][pl.ds((places + step) * count + g * ROWS, ROWS), across] = far
+                    msg = msgs[step - steps[0]]
+                    near = msg[:, pl.ds(low, width * LANES)]
+                    far = msg[:, pl.ds(groups * wide * LANES + low, width * LANES)]
+                at = (step - steps[0]) * CORES * count + g * ROWS
+                refs[-3][pl.ds(at, ROWS), across] = near
+                refs[-3][pl.ds(at + count, ROWS), across] = far
+    partial = refs[:added]
+    refs = refs[added:]
     if first:
         tags = refs.pop(0)
         per_tile = LANES // count
+        half = ROWS // CORES
         for tile in range(lanes // LANES):
             total = jnp.zeros((ROWS, LANES), F32)
-            for slot in range(tile * per_tile, (tile + 1) * per_tile):
-                if slot < places:
-                    total += msgs[slot][:, pl.ds(CORES * past, LANES)].astype(F32)
-                else:
-                    total += crossed[slot - places, :, pl.ds(past, LANES)].astype(F32)
+            for slot in range(tile * per_tile, (tile + 1) * per_tile, CORES):
+                step = slot // CORES
+                near = msgs[step][:, pl.ds(CORES * past, LANES)].astype(F32)
+                far = crossed[step, :, pl.ds(past, LANES)].astype(F32)
+                total += jnp.concatenate([near[:half] + far[half:], near[half:]], axis=0)
             tags[:, pl.ds(tile * LANES, LANES)] = total
     sums = refs[:grp]
     data, product, parts = refs[grp:]
-    label = tags[...].astype(jnp.int32)
+    label = tags[:, pl.ds(steps[0] * CORES * count, lanes)].astype(jnp.int32)
     key = label[0:1] * CPAD + label[1:2]
     spot = label[2:3]
     turn = label[3:4]
@@ -357,7 +365,7 @@
         for tile, width in stacked(result.shape[1]):
             here = (pl.ds(tile * CPG, CPG), pl.ds(0, width))
             value = result[step * CPAD : step * CPAD + CPG, tile * LANES : tile * LANES + width]
-            sums[step][here] = value
+            sums[step][here] = value + partial[step][here] if partial else value
         if first:
             target = partner(own, step, grp)
             local = jnp.where(label[0:1] == target, label[1:2], -1)
@@ -369,7 +377,7 @@
                     row += 1
 
 
-def numerators(count, pieces, tags, arrived, chunk, edges, rows):
+def numerators(count, pieces, tags, arrived, chunk, edges, rows, steps, partial=()):
     mem, grp = lax.axis_size("mem"), lax.axis_size("grp")
     first = chunk == 0
     here = (rows[chunk], rows[chunk + 1])
@@ -380,16 +388,18 @@
         low, high = max(edges[c], base), min(edges[c + 1], stop)
         if low < high:
             segments.append((c, edges[c + 1] - edges[c], low - edges[c], low - base, high - low))
-            msgs += arrived[c]
-    lanes = mem * count
+            msgs += arrived[c] if c == 0 else arrived[c][slice(*steps)]
+    lanes = (steps[1] - steps[0]) * CORES * count
     span = (here[1] - here[0]) * ANGLES
     tiles = stop - base
     shapes = [jax.ShapeDtypeStruct((ROWS, lanes), F32)] if first else []
     tall = sum_rows(span, lanes if first else 0)
     shapes += [jax.ShapeDtypeStruct((tall, LANES), F32)] * grp
-    operands = [pieces] + ([] if first else [tags]) + msgs
+    operands = [pieces] + ([] if first else [tags]) + msgs + list(partial)
     outs = pl.pallas_call(
-        functools.partial(numer_kernel, mem, count, first, here, base, tiles, tuple(segments)),
+        functools.partial(
+            numer_kernel, mem, count, first, here, base, tiles, tuple(segments), steps, len(partial)
+        ),
         out_shape=shapes,
         in_specs=[VMEM] * len(operands),
         out_specs=[VMEM] * len(shapes),
@@ -507,7 +517,12 @@
     arrived = [first + [send(cross(first, after), "mem", 0, CORES, 1)]] + arrived
     tags, sums, blocks = None, [], []
     for chunk in range(len(edges) - 1):
-        tags, here = numerators(count, pieces, tags, arrived, chunk, edges, rows)
+        cuts = [0, places]
+        if chunk > 0 and places // 2 * CORES * count % LANES == 0:
+            cuts = [0, places // 2, places]
+        here = ()
+        for steps in zip(cuts, cuts[1:]):
+            tags, here = numerators(count, pieces, tags, arrived, chunk, edges, rows, steps, here)
         others = [send(here[step].astype(HALF), "grp", step) for step in range(1, grp)]
         if chunk == 0:
             blocks = [tag_block(part, rows[1] * ANGLES) for part in [here[0]] + others]

time: 46.1 us -> 45.6 us (0.989)
  starting transfers between devices: 19.4 us -> 18.3 us
  Pallas kernels: 9.04 us -> 9.52 us
    ppermute x14, starting transfers between devices: 19.4 us -> 18.3 us  [send(): return lax.ppermute(value, axis, pairs)]
    pallas_call x2 -> x3, Pallas kernels: 3.25 us -> 3.74 us  [numerators(): pl.pallas_call(functools.partial(numer_kernel, mem, count, first, here, b...]
  transfers between devices with their start and end apart: 14 -> 14, of which waited for: 6 -> 6; matrix products, arithmetic and copies ran while one was open for 0% -> 0% of each run, Pallas kernels for 18% -> 19%
where the time goes in v5:
time: 45.6 us; the launch traced here: 44.7 us
  starting transfers between devices  18.3 us (40%)
  waiting for transfers between devices  14.6 us (32%)
  Pallas kernels  9.52 us (21%)
  local copies, waits for them, and re-layouts  1.28 us (3%)
  other arithmetic  0.95 us (2%)
    ppermute x14, starting transfers between devices, send(): return lax.ppermute(value, axis, pairs)  18.3 us
    ppermute x14, waiting for transfers between devices, send(): return lax.ppermute(value, axis, pairs)  14.6 us
    pallas_call x3, Pallas kernels, numerators(): pl.pallas_call(functools.partial(numer_kernel, mem, count, first, here, b...  3.74 us
    pallas_call x1, Pallas kernels, denominators(): pl.pallas_call(functools.partial(denom_kernel, first, lanes), out_shape=j...  3.53 us
    unnamed x4, local copies, waits for them, and re-layouts  1.27 us
    pallas_call x1, Pallas kernels, tables(): pl.pallas_call(functools.partial(table_kernel, turns), out_shape=[jax.Sha...  1.17 us
  transfers between devices with their start and end apart: 14, of which 6 were waited for; matrix products, arithmetic and copies ran while one was open for 0% of the time, Pallas kernels for 19%

profile of v5, /device:TPU:0, one launch (start us, length us, event | category | flops | bytes accessed | tf_op | source)
XLA Modules:
  0.0 44.7 jit_solution(14808587214800979980)
XLA Ops:
  0.0 0.7 %pad_add_fusion.labels = s32[3,32]{1,0:T(4,128)S(1)} fusion(s32[1,32]{1,0:T(1,128)} %bitcast.3, s32[1,32]{1,0:T(1,128)} %bitcast.4, s32[1,32]{1,0:T(1,128)} %bitcast.5), kind=kLoop, calls=%fused_computation.5 | loop fusion | flops 192 | bytes 768 | tf_op jit(solution)/shard_map/stack | solution.py:505
  0.7 1.3 %copy-done = bf16[32,18432]{1,0:T(8,128)(2,1)S(1)} copy-done((bf16[32,18432]{1,0:T(8,128)(2,1)S(1)}, bf16[32,18432]{1,0:T(8,128)(2,1)}, u32[]{:S(2)}) %copy-start) | copy-done | bytes 1179672
  2.0 0.1 pack.1
  2.1 0.5 %collective-permute-start.3 = (bf16[4,8,4608]{2,1,0:T(8,128)(2,1)S(1)}, bf16[4,8,4608]{2,1,0:T(8,128)(2,1)S(1)}, u32[]{:S(2)}, u32[]{:S(2)}) collective-permute-start(bf16[4,8,4608]{2,1,0:T(8,128)(2,1)S(1)} %get-tuple-element.37), channel_id=1, source_target_pairs={{0,1},{1,0},{2,3},{3,2},{4,5},{5,4},{6,7},{7,6},{8,9},{9,8},{10,11... | collective-permute-start | bytes 884744 | tf_op jit(solution)/shard_map/ppermute | solution.py:49
  2.6 4.7 %collective-permute-start.2 = (bf16[8,9344]{1,0:T(8,128)(2,1)S(1)}, bf16[8,9344]{1,0:T(8,128)(2,1)S(1)}, u32[]{:S(2)}, u32[]{:S(2)}) collective-permute-start(bf16[8,9344]{1,0:T(8,128)(2,1)S(1)} %get-tuple-element.35), channel_id=1, source_target_pairs={{0,6},{1,7},{2,4},{3,5},{4,2},{5,3},{6,0},{7,1},{8,14},{9,15},{10,... | collective-permute-start | bytes 448520 | tf_op jit(solution)/shard_map/ppermute | solution.py:49
  7.3 0.6 %collective-permute-start.1 = (bf16[8,9344]{1,0:T(8,128)(2,1)S(1)}, bf16[8,9344]{1,0:T(8,128)(2,1)S(1)}, u32[]{:S(2)}, u32[]{:S(2)}) collective-permute-start(bf16[8,9344]{1,0:T(8,128)(2,1)S(1)} %get-tuple-element.34), channel_id=1, source_target_pairs={{0,4},{1,5},{2,6},{3,7},{4,0},{5,1},{6,2},{7,3},{8,12},{9,13},{10,... | collective-permute-start | bytes 448520 | tf_op jit(solution)/shard_map/ppermute | solution.py:49
  7.9 1.2 %tables.1 = (bf16[2304,48]{1,0:T(8,128)(2,1)S(1)}, bf16[2304,256]{1,0:T(8,128)(2,1)S(1)}) custom-call(f32[16,18432]{1,0:T(8,128)S(1)} %copy-done.1), custom_call_target="tpu_custom_call" | custom-call | flops 1048576 | bytes 65536 | tf_op jit(solution)/shard_map/tables/pallas_call | solution.py:233
  9.1 3.0 %collective-permute-done.2.refs_0_.refs_3_ = bf16[8,9344]{1,0:T(8,128)(2,1)S(1)} collective-permute-done((bf16[8,9344]{1,0:T(8,128)(2,1)S(1)}, bf16[8,9344]{1,0:T(8,128)(2,1)S(1)}, u32[]{:S(2)}, u32[]{:S(2)}) %collective-permute-start.2) | collective-permute-done | bytes 149536 | tf_op jit(solution)/shard_map/ppermute | solution.py:49
  12.1 0.0 collective-permute-done.3.crossed
  12.1 3.9 %collective-permute-done.refs_1_ = bf16[8,9344]{1,0:T(8,128)(2,1)S(1)} collective-permute-done((bf16[8,9344]{1,0:T(8,128)(2,1)S(1)}, bf16[8,9344]{1,0:T(8,128)(2,1)S(1)}, u32[]{:S(2)}, u32[]{:S(2)}) %collective-permute-start) | collective-permute-done | bytes 149536 | tf_op jit(solution)/shard_map/ppermute | solution.py:49
  16.0 4.5 %collective-permute-done.1.refs_2_ = bf16[8,9344]{1,0:T(8,128)(2,1)S(1)} collective-permute-done((bf16[8,9344]{1,0:T(8,128)(2,1)S(1)}, bf16[8,9344]{1,0:T(8,128)(2,1)S(1)}, u32[]{:S(2)}, u32[]{:S(2)}) %collective-permute-start.1) | collective-permute-done | bytes 149536 | tf_op jit(solution)/shard_map/ppermute | solution.py:49
  20.6 0.1 collective-permute-start.4
  20.6 0.1 collective-permute-start.10
  20.7 3.0 %collective-permute-start.8 = (bf16[8,9216]{1,0:T(8,128)(2,1)S(1)}, bf16[8,9216]{1,0:T(8,128)(2,1)S(1)}, u32[]{:S(2)}, u32[]{:S(2)}) collective-permute-start(bf16[8,9216]{1,0:T(8,128)(2,1)S(1)} %get-tuple-element.44), channel_id=1, source_target_pairs={{0,4},{1,5},{2,6},{3,7},{4,0},{5,1},{6,2},{7,3},{8,12},{9,13},{10,... | collective-permute-start | bytes 442376 | tf_op jit(solution)/shard_map/ppermute | solution.py:49
  23.7 1.3 %collective-permute-start.9 = (bf16[8,9216]{1,0:T(8,128)(2,1)S(1)}, bf16[8,9216]{1,0:T(8,128)(2,1)S(1)}, u32[]{:S(2)}, u32[]{:S(2)}) collective-permute-start(bf16[8,9216]{1,0:T(8,128)(2,1)S(1)} %get-tuple-element.45), channel_id=1, source_target_pairs={{0,6},{1,7},{2,4},{3,5},{4,2},{5,3},{6,0},{7,1},{8,14},{9,15},{10,... | collective-permute-start | bytes 442376 | tf_op jit(solution)/shard_map/ppermute | solution.py:49
  25.1 1.6 %numerators.3 = (f32[8,256]{1,0:T(8,128)S(1)}, f32[456,128]{1,0:T(8,128)S(1)}, f32[456,128]{1,0:T(8,128)S(1)}, f32[456,128]{1,0:T(8,128)S(1)}, f32[456,128]{1,0:T(8,128)S(1)}) custom-call(bf16[2304,48]{1,0:T(8,128)(2,1)S(1)} %get-tuple-element.31.refs_1_.pieces, bf16[8,9344]{1,0:T(8,128)(2,1)S(1)} %get-tuple-element.32.refs_0_, ...), custom_call_target="tpu_custom_call" | custom-call | flops 1048576 | bytes 65536 | tf_op jit(solution)/shard_map/numerators/pallas_call | solution.py:399
  26.8 2.5 %collective-permute-start.7 = (f16[456,128]{1,0:T(8,128)(2,1)S(1)}, f16[456,128]{1,0:T(8,128)(2,1)S(1)}, u32[]{:S(2)}, u32[]{:S(2)}) collective-permute-start(f16[456,128]{1,0:T(8,128)(2,1)S(1)} %convert_element_type.49), channel_id=1, source_target_pairs={{0,24},{8,16},{16,8},{24,0},{1,25},{9,17},{17,9},{25,1},{2,26},{10... | collective-permute-start | bytes 350216 | tf_op jit(solution)/shard_map/ppermute | solution.py:49
  29.3 0.6 %collective-permute-start.6 = (f16[456,128]{1,0:T(8,128)(2,1)S(1)}, f16[456,128]{1,0:T(8,128)(2,1)S(1)}, u32[]{:S(2)}, u32[]{:S(2)}) collective-permute-start(f16[456,128]{1,0:T(8,128)(2,1)S(1)} %convert_element_type.47), channel_id=1, source_target_pairs={{0,16},{8,24},{16,0},{24,8},{1,17},{9,25},{17,1},{25,9},{2,18},{10... | collective-permute-start | bytes 350216 | tf_op jit(solution)/shard_map/ppermute | solution.py:49
  29.9 0.0 collective-permute-done.10.refs_2_
  29.9 1.3 %collective-permute-start.5 = (f16[456,128]{1,0:T(8,128)(2,1)S(1)}, f16[456,128]{1,0:T(8,128)(2,1)S(1)}, u32[]{:S(2)}, u32[]{:S(2)}) collective-permute-start(f16[456,128]{1,0:T(8,128)(2,1)S(1)} %convert_element_type.45), channel_id=1, source_target_pairs={{0,8},{8,0},{16,24},{24,16},{1,9},{9,1},{17,25},{25,17},{2,10},{10... | collective-permute-start | bytes 350216 | tf_op jit(solution)/shard_map/ppermute | solution.py:49
  31.2 1.1 %numerators.4 = (f32[456,128]{1,0:T(8,128)S(1)}, f32[456,128]{1,0:T(8,128)S(1)}, f32[456,128]{1,0:T(8,128)S(1)}, f32[456,128]{1,0:T(8,128)S(1)}) custom-call(bf16[2304,48]{1,0:T(8,128)(2,1)S(1)} %get-tuple-element.31.refs_1_.pieces, f32[8,256]{1,0:T(8,128)S(1)} %get-tuple-element.43.refs_0_, bf16[8,9216]{1,0:T(8,128)(2,1)S(1)} %get-tuple-element.38.refs_4_.refs_1_, ...), custom_call_target="tpu_custom_call" | custom-call | flops 1048576 | bytes 65536 | tf_op jit(solution)/shard_map/numerators/pallas_call | solution.py:399
  32.3 2.5 %collective-permute-done.8.refs_1_ = bf16[8,9216]{1,0:T(8,128)(2,1)S(1)} collective-permute-done((bf16[8,9216]{1,0:T(8,128)(2,1)S(1)}, bf16[8,9216]{1,0:T(8,128)(2,1)S(1)}, u32[]{:S(2)}, u32[]{:S(2)}) %collective-permute-start.8) | collective-permute-done | bytes 147488 | tf_op jit(solution)/shard_map/ppermute | solution.py:49
  34.7 1.1 %numerators.5 = (f32[456,128]{1,0:T(8,128)S(1)}, f32[456,128]{1,0:T(8,128)S(1)}, f32[456,128]{1,0:T(8,128)S(1)}, f32[456,128]{1,0:T(8,128)S(1)}) custom-call(bf16[2304,48]{1,0:T(8,128)(2,1)S(1)} %get-tuple-element.31.refs_1_.pieces, f32[8,256]{1,0:T(8,128)S(1)} %get-tuple-element.43.refs_0_, bf16[8,9216]{1,0:T(8,128)(2,1)S(1)} %collective-permute-done.8.refs_1_, ...), custom_call_target="tpu_custom_call" | custom-call | flops 1048576 | bytes 65536 | tf_op jit(solution)/shard_map/numerators/pallas_call | solution.py:399
  35.9 2.5 %collective-permute-start.13 = (f16[456,128]{1,0:T(8,128)(2,1)S(1)}, f16[456,128]{1,0:T(8,128)(2,1)S(1)}, u32[]{:S(2)}, u32[]{:S(2)}) collective-permute-start(f16[456,128]{1,0:T(8,128)(2,1)S(1)} %convert_element_type.58), channel_id=1, source_target_pairs={{0,24},{8,16},{16,8},{24,0},{1,25},{9,17},{17,9},{25,1},{2,26},{10... | collective-permute-start | bytes 350216 | tf_op jit(solution)/shard_map/ppermute | solution.py:49
  38.4 0.5 %collective-permute-start.12 = (f16[456,128]{1,0:T(8,128)(2,1)S(1)}, f16[456,128]{1,0:T(8,128)(2,1)S(1)}, u32[]{:S(2)}, u32[]{:S(2)}) collective-permute-start(f16[456,128]{1,0:T(8,128)(2,1)S(1)} %convert_element_type.56), channel_id=1, source_target_pairs={{0,16},{8,24},{16,0},{24,8},{1,17},{9,25},{17,1},{25,9},{2,18},{10... | collective-permute-start | bytes 350216 | tf_op jit(solution)/shard_map/ppermute | solution.py:49
  38.9 0.5 %collective-permute-start.11 = (f16[456,128]{1,0:T(8,128)(2,1)S(1)}, f16[456,128]{1,0:T(8,128)(2,1)S(1)}, u32[]{:S(2)}, u32[]{:S(2)}) collective-permute-start(f16[456,128]{1,0:T(8,128)(2,1)S(1)} %convert_element_type.54), channel_id=1, source_target_pairs={{0,8},{8,0},{16,24},{24,16},{1,9},{9,1},{17,25},{25,17},{2,10},{10... | collective-permute-start | bytes 350216 | tf_op jit(solution)/shard_map/ppermute | solution.py:49
  39.5 0.1 convert_add_fusion.1.refs_0_
  39.6 3.5 %denominators.1.denom = f32[56,2304]{1,0:T(8,128)S(1)} custom-call(bf16[2304,256]{1,0:T(8,128)(2,1)S(1)} %get-tuple-element.30.weights, f32[8,128]{1,0:T(8,128)S(1)} %slice.12.refs_0_, f32[8,128]{1,0:T(8,128)S(1)} %slice_convert_fusion.2.refs_1_, f32[8,128]{1,0:T(8,128)S(1)} %slice_convert_fusion.1.refs_2_, f32[8,128]{1,0:T(8,128)S(1)} %slice_convert_fusion.refs_3_), custom_call_target="tpu_custom_call" | custom-call | flops 1048576 | bytes 65536 | tf_op jit(solution)/shard_map/denominators/pallas_call | solution.py:451
  43.1 0.5 %collective-permute-done.12 = f16[456,128]{1,0:T(8,128)(2,1)S(1)} collective-permute-done((f16[456,128]{1,0:T(8,128)(2,1)S(1)}, f16[456,128]{1,0:T(8,128)(2,1)S(1)}, u32[]{:S(2)}, u32[]{:S(2)}) %collective-permute-start.12) | collective-permute-done | bytes 116768 | tf_op jit(solution)/shard_map/ppermute | solution.py:49
  43.6 0.2 collective-permute-done.11
  43.8 0.1 convert_add_fusion.refs_1_
  43.9 0.9 %averages.1 = f32[50,2304]{1,0:T(8,128)} custom-call(f32[56,2304]{1,0:T(8,128)S(1)} %denominators.1.denom, f32[456,128]{1,0:T(8,128)S(1)} %convert_add_fusion.1.refs_0_, f32[456,128]{1,0:T(8,128)S(1)} %convert_add_fusion.refs_1_), custom_call_target="tpu_custom_call" | custom-call | flops 1048576 | bytes 65536 | tf_op jit(solution)/shard_map/averages/pallas_call | solution.py:473
  (22 shorter events, 0.2 us)
Async XLA Ops:
  0.7 1.3 %copy-start = (bf16[32,18432]{1,0:T(8,128)(2,1)S(1)}, bf16[32,18432]{1,0:T(8,128)(2,1)}, u32[]{:S(2)}) copy-start(bf16[32,18432]{1,0:T(8,128)(2,1)} %img.1) | copy-start | bytes 3538948
  2.0 5.9 %copy-start.1 = (f32[16,18432]{1,0:T(8,128)S(1)}, f32[16,18432]{1,0:T(8,128)}, u32[]{:S(2)}) copy-start(f32[16,18432]{1,0:T(8,128)} %table.1) | copy-start | bytes 3538948
  2.1 10.0 %collective-permute-start.3 = (bf16[4,8,4608]{2,1,0:T(8,128)(2,1)S(1)}, bf16[4,8,4608]{2,1,0:T(8,128)(2,1)S(1)}, u32[]{:S(2)}, u32[]{:S(2)}) collective-permute-start(bf16[4,8,4608]{2,1,0:T(8,128)(2,1)S(1)} %get-tuple-element.37), channel_id=1, source_target_pairs={{0,1},{1,0},{2,3},{3,2},{4,5},{5,4},{6,7},{7,6},{8,9},{9,8},{10,11... | collective-permute-start | bytes 884744 | tf_op jit(solution)/shard_map/ppermute | solution.py:49
  2.6 9.5 %collective-permute-start.2 = (bf16[8,9344]{1,0:T(8,128)(2,1)S(1)}, bf16[8,9344]{1,0:T(8,128)(2,1)S(1)}, u32[]{:S(2)}, u32[]{:S(2)}) collective-permute-start(bf16[8,9344]{1,0:T(8,128)(2,1)S(1)} %get-tuple-element.35), channel_id=1, source_target_pairs={{0,6},{1,7},{2,4},{3,5},{4,2},{5,3},{6,0},{7,1},{8,14},{9,15},{10,... | collective-permute-start | bytes 448520 | tf_op jit(solution)/shard_map/ppermute | solution.py:49
  7.3 8.8 %collective-permute-start = (bf16[8,9344]{1,0:T(8,128)(2,1)S(1)}, bf16[8,9344]{1,0:T(8,128)(2,1)S(1)}, u32[]{:S(2)}, u32[]{:S(2)}) collective-permute-start(bf16[8,9344]{1,0:T(8,128)(2,1)S(1)} %get-tuple-element.33), channel_id=1, source_target_pairs={{0,2},{1,3},{2,0},{3,1},{4,6},{5,7},{6,4},{7,5},{8,10},{9,11},{10,... | collective-permute-start | bytes 448520 | tf_op jit(solution)/shard_map/ppermute | solution.py:49
  7.3 13.3 %collective-permute-start.1 = (bf16[8,9344]{1,0:T(8,128)(2,1)S(1)}, bf16[8,9344]{1,0:T(8,128)(2,1)S(1)}, u32[]{:S(2)}, u32[]{:S(2)}) collective-permute-start(bf16[8,9344]{1,0:T(8,128)(2,1)S(1)} %get-tuple-element.34), channel_id=1, source_target_pairs={{0,4},{1,5},{2,6},{3,7},{4,0},{5,1},{6,2},{7,3},{8,12},{9,13},{10,... | collective-permute-start | bytes 448520 | tf_op jit(solution)/shard_map/ppermute | solution.py:49
  20.6 4.5 %collective-permute-start.4 = (bf16[4,8,4736]{2,1,0:T(8,128)(2,1)S(1)}, bf16[4,8,4736]{2,1,0:T(8,128)(2,1)S(1)}, u32[]{:S(2)}, u32[]{:S(2)}) collective-permute-start(bf16[4,8,4736]{2,1,0:T(8,128)(2,1)S(1)} %cross.1), channel_id=1, source_target_pairs={{0,1},{1,0},{2,3},{3,2},{4,5},{5,4},{6,7},{7,6},{8,9},{9,8},{10,11... | collective-permute-start | bytes 909320 | tf_op jit(solution)/shard_map/ppermute | solution.py:49
  20.6 9.3 %collective-permute-start.10 = (bf16[8,9216]{1,0:T(8,128)(2,1)S(1)}, bf16[8,9216]{1,0:T(8,128)(2,1)S(1)}, u32[]{:S(2)}, u32[]{:S(2)}) collective-permute-start(bf16[8,9216]{1,0:T(8,128)(2,1)S(1)} %get-tuple-element.46), channel_id=1, source_target_pairs={{0,2},{1,3},{2,0},{3,1},{4,6},{5,7},{6,4},{7,5},{8,10},{9,11},{10,... | collective-permute-start | bytes 442376 | tf_op jit(solution)/shard_map/ppermute | solution.py:49
  20.7 14.0 %collective-permute-start.8 = (bf16[8,9216]{1,0:T(8,128)(2,1)S(1)}, bf16[8,9216]{1,0:T(8,128)(2,1)S(1)}, u32[]{:S(2)}, u32[]{:S(2)}) collective-permute-start(bf16[8,9216]{1,0:T(8,128)(2,1)S(1)} %get-tuple-element.44), channel_id=1, source_target_pairs={{0,4},{1,5},{2,6},{3,7},{4,0},{5,1},{6,2},{7,3},{8,12},{9,13},{10,... | collective-permute-start | bytes 442376 | tf_op jit(solution)/shard_map/ppermute | solution.py:49
  23.7 11.0 %collective-permute-start.9 = (bf16[8,9216]{1,0:T(8,128)(2,1)S(1)}, bf16[8,9216]{1,0:T(8,128)(2,1)S(1)}, u32[]{:S(2)}, u32[]{:S(2)}) collective-permute-start(bf16[8,9216]{1,0:T(8,128)(2,1)S(1)} %get-tuple-element.45), channel_id=1, source_target_pairs={{0,6},{1,7},{2,4},{3,5},{4,2},{5,3},{6,0},{7,1},{8,14},{9,15},{10,... | collective-permute-start | bytes 442376 | tf_op jit(solution)/shard_map/ppermute | solution.py:49
  26.8 12.2 %collective-permute-start.7 = (f16[456,128]{1,0:T(8,128)(2,1)S(1)}, f16[456,128]{1,0:T(8,128)(2,1)S(1)}, u32[]{:S(2)}, u32[]{:S(2)}) collective-permute-start(f16[456,128]{1,0:T(8,128)(2,1)S(1)} %convert_element_type.49), channel_id=1, source_target_pairs={{0,24},{8,16},{16,8},{24,0},{1,25},{9,17},{17,9},{25,1},{2,26},{10... | collective-permute-start | bytes 350216 | tf_op jit(solution)/shard_map/ppermute | solution.py:49
  29.3 10.1 %collective-permute-start.6 = (f16[456,128]{1,0:T(8,128)(2,1)S(1)}, f16[456,128]{1,0:T(8,128)(2,1)S(1)}, u32[]{:S(2)}, u32[]{:S(2)}) collective-permute-start(f16[456,128]{1,0:T(8,128)(2,1)S(1)} %convert_element_type.47), channel_id=1, source_target_pairs={{0,16},{8,24},{16,0},{24,8},{1,17},{9,25},{17,1},{25,9},{2,18},{10... | collective-permute-start | bytes 350216 | tf_op jit(solution)/shard_map/ppermute | solution.py:49
  29.9 9.5 %collective-permute-start.5 = (f16[456,128]{1,0:T(8,128)(2,1)S(1)}, f16[456,128]{1,0:T(8,128)(2,1)S(1)}, u32[]{:S(2)}, u32[]{:S(2)}) collective-permute-start(f16[456,128]{1,0:T(8,128)(2,1)S(1)} %convert_element_type.45), channel_id=1, source_target_pairs={{0,8},{8,0},{16,24},{24,16},{1,9},{9,1},{17,25},{25,17},{2,10},{10... | collective-permute-start | bytes 350216 | tf_op jit(solution)/shard_map/ppermute | solution.py:49
  35.9 7.2 %collective-permute-start.13 = (f16[456,128]{1,0:T(8,128)(2,1)S(1)}, f16[456,128]{1,0:T(8,128)(2,1)S(1)}, u32[]{:S(2)}, u32[]{:S(2)}) collective-permute-start(f16[456,128]{1,0:T(8,128)(2,1)S(1)} %convert_element_type.58), channel_id=1, source_target_pairs={{0,24},{8,16},{16,8},{24,0},{1,25},{9,17},{17,9},{25,1},{2,26},{10... | collective-permute-start | bytes 350216 | tf_op jit(solution)/shard_map/ppermute | solution.py:49
  38.4 5.2 %collective-permute-start.12 = (f16[456,128]{1,0:T(8,128)(2,1)S(1)}, f16[456,128]{1,0:T(8,128)(2,1)S(1)}, u32[]{:S(2)}, u32[]{:S(2)}) collective-permute-start(f16[456,128]{1,0:T(8,128)(2,1)S(1)} %convert_element_type.56), channel_id=1, source_target_pairs={{0,16},{8,24},{16,0},{24,8},{1,17},{9,25},{17,1},{25,9},{2,18},{10... | collective-permute-start | bytes 350216 | tf_op jit(solution)/shard_map/ppermute | solution.py:49
  38.9 4.9 %collective-permute-start.11 = (f16[456,128]{1,0:T(8,128)(2,1)S(1)}, f16[456,128]{1,0:T(8,128)(2,1)S(1)}, u32[]{:S(2)}, u32[]{:S(2)}) collective-permute-start(f16[456,128]{1,0:T(8,128)(2,1)S(1)} %convert_element_type.54), channel_id=1, source_target_pairs={{0,8},{8,0},{16,24},{24,16},{1,9},{9,1},{17,25},{25,17},{2,10},{10... | collective-permute-start | bytes 350216 | tf_op jit(solution)/shard_map/ppermute | solution.py:49

commit v6 on v5

--- a/solution.py
+++ b/solution.py
@@ -357,7 +357,7 @@
             parts[where, pl.ds(lanes + tile * LANES, LANES)] = low
         return carry
 
-    lax.fori_loop(0, rows[1] - rows[0], rotate, 0)
+    lax.fori_loop(0, rows[1] - rows[0], rotate, 0, unroll=True)
     result = lax.dot_general(
         jnp.concatenate(member, axis=0), parts[...], NT, preferred_element_type=F32
     )
@@ -441,7 +441,7 @@
             spread[rows, pl.ds(PAIRS + tile * LANES, LANES)] = far[:, LANES:]
         return carry
 
-    lax.fori_loop(0, span // ANGLES, turn_far, 0)
+    lax.fori_loop(0, span // ANGLES, turn_far, 0, unroll=True)
     both = lax.dot_general(left, spread[...], NT, preferred_element_type=F32)
     denom[...] = both[:CPAD] + both[CPAD:]
 

time: 45.6 us -> 45.3 us (level)
  Pallas kernels: 9.52 us -> 7.67 us
  waiting for transfers between devices: 14.6 us -> 15.9 us
    ppermute x14, waiting for transfers between devices: 14.6 us -> 15.9 us  [send(): return lax.ppermute(value, axis, pairs)]
    pallas_call x3, Pallas kernels: 3.74 us -> 2.67 us  [numerators(): pl.pallas_call(functools.partial(numer_kernel, mem, count, first, here, b...]
    pallas_call x1, Pallas kernels: 3.53 us -> 2.74 us  [denominators(): pl.pallas_call(functools.partial(denom_kernel, first, lanes), out_shape=j...]
  transfers between devices with their start and end apart: 14 -> 14, of which waited for: 6 -> 8; matrix products, arithmetic and copies ran while one was open for 0% -> 0% of each run, Pallas kernels for 19% -> 15%
where the time goes in v6:
time: 45.3 us; the launch traced here: 44.4 us
  starting transfers between devices  18.5 us (41%)
  waiting for transfers between devices  15.9 us (35%)
  Pallas kernels  7.67 us (17%)
  local copies, waits for them, and re-layouts  1.28 us (3%)
  other arithmetic  0.95 us (2%)
    ppermute x14, starting transfers between devices, send(): return lax.ppermute(value, axis, pairs)  18.5 us
    ppermute x14, waiting for transfers between devices, send(): return lax.ppermute(value, axis, pairs)  15.9 us
    pallas_call x1, Pallas kernels, denominators(): pl.pallas_call(functools.partial(denom_kernel, first, lanes), out_shape=j...  2.74 us
    pallas_call x3, Pallas kernels, numerators(): pl.pallas_call(functools.partial(numer_kernel, mem, count, first, here, b...  2.67 us
    unnamed x4, local copies, waits for them, and re-layouts  1.27 us
    pallas_call x1, Pallas kernels, tables(): pl.pallas_call(functools.partial(table_kernel, turns), out_shape=[jax.Sha...  1.17 us
  transfers between devices with their start and end apart: 14, of which 8 were waited for; matrix products, arithmetic and copies ran while one was open for 0% of the time, Pallas kernels for 15%

profile of v6, /device:TPU:0, one launch (start us, length us, event | category | flops | bytes accessed | tf_op | source)
XLA Modules:
  0.0 44.4 jit_solution(8328268064646876085)
XLA Ops:
  0.0 0.7 %pad_add_fusion.labels = s32[3,32]{1,0:T(4,128)S(1)} fusion(s32[1,32]{1,0:T(1,128)} %bitcast.3, s32[1,32]{1,0:T(1,128)} %bitcast.4, s32[1,32]{1,0:T(1,128)} %bitcast.5), kind=kLoop, calls=%fused_computation.5 | loop fusion | flops 192 | bytes 768 | tf_op jit(solution)/shard_map/stack | solution.py:505
  0.7 1.3 %copy-done = bf16[32,18432]{1,0:T(8,128)(2,1)S(1)} copy-done((bf16[32,18432]{1,0:T(8,128)(2,1)S(1)}, bf16[32,18432]{1,0:T(8,128)(2,1)}, u32[]{:S(2)}) %copy-start) | copy-done | bytes 1179672
  2.0 0.1 pack.1
  2.1 0.5 %collective-permute-start.3 = (bf16[4,8,4608]{2,1,0:T(8,128)(2,1)S(1)}, bf16[4,8,4608]{2,1,0:T(8,128)(2,1)S(1)}, u32[]{:S(2)}, u32[]{:S(2)}) collective-permute-start(bf16[4,8,4608]{2,1,0:T(8,128)(2,1)S(1)} %get-tuple-element.37), channel_id=1, source_target_pairs={{0,1},{1,0},{2,3},{3,2},{4,5},{5,4},{6,7},{7,6},{8,9},{9,8},{10,11... | collective-permute-start | bytes 884744 | tf_op jit(solution)/shard_map/ppermute | solution.py:49
  2.6 4.7 %collective-permute-start.2 = (bf16[8,9344]{1,0:T(8,128)(2,1)S(1)}, bf16[8,9344]{1,0:T(8,128)(2,1)S(1)}, u32[]{:S(2)}, u32[]{:S(2)}) collective-permute-start(bf16[8,9344]{1,0:T(8,128)(2,1)S(1)} %get-tuple-element.35), channel_id=1, source_target_pairs={{0,6},{1,7},{2,4},{3,5},{4,2},{5,3},{6,0},{7,1},{8,14},{9,15},{10,... | collective-permute-start | bytes 448520 | tf_op jit(solution)/shard_map/ppermute | solution.py:49
  7.3 0.6 %collective-permute-start.1 = (bf16[8,9344]{1,0:T(8,128)(2,1)S(1)}, bf16[8,9344]{1,0:T(8,128)(2,1)S(1)}, u32[]{:S(2)}, u32[]{:S(2)}) collective-permute-start(bf16[8,9344]{1,0:T(8,128)(2,1)S(1)} %get-tuple-element.34), channel_id=1, source_target_pairs={{0,4},{1,5},{2,6},{3,7},{4,0},{5,1},{6,2},{7,3},{8,12},{9,13},{10,... | collective-permute-start | bytes 448520 | tf_op jit(solution)/shard_map/ppermute | solution.py:49
  7.9 1.2 %tables.1 = (bf16[2304,48]{1,0:T(8,128)(2,1)S(1)}, bf16[2304,256]{1,0:T(8,128)(2,1)S(1)}) custom-call(f32[16,18432]{1,0:T(8,128)S(1)} %copy-done.1), custom_call_target="tpu_custom_call" | custom-call | flops 1048576 | bytes 65536 | tf_op jit(solution)/shard_map/tables/pallas_call | solution.py:233
  9.1 3.0 %collective-permute-done.2.refs_0_.refs_3_ = bf16[8,9344]{1,0:T(8,128)(2,1)S(1)} collective-permute-done((bf16[8,9344]{1,0:T(8,128)(2,1)S(1)}, bf16[8,9344]{1,0:T(8,128)(2,1)S(1)}, u32[]{:S(2)}, u32[]{:S(2)}) %collective-permute-start.2) | collective-permute-done | bytes 149536 | tf_op jit(solution)/shard_map/ppermute | solution.py:49
  12.1 3.9 %collective-permute-done.refs_1_ = bf16[8,9344]{1,0:T(8,128)(2,1)S(1)} collective-permute-done((bf16[8,9344]{1,0:T(8,128)(2,1)S(1)}, bf16[8,9344]{1,0:T(8,128)(2,1)S(1)}, u32[]{:S(2)}, u32[]{:S(2)}) %collective-permute-start) | collective-permute-done | bytes 149536 | tf_op jit(solution)/shard_map/ppermute | solution.py:49
  16.0 4.5 %collective-permute-done.1.refs_2_ = bf16[8,9344]{1,0:T(8,128)(2,1)S(1)} collective-permute-done((bf16[8,9344]{1,0:T(8,128)(2,1)S(1)}, bf16[8,9344]{1,0:T(8,128)(2,1)S(1)}, u32[]{:S(2)}, u32[]{:S(2)}) %collective-permute-start.1) | collective-permute-done | bytes 149536 | tf_op jit(solution)/shard_map/ppermute | solution.py:49
  20.6 0.1 collective-permute-start.4
  20.6 0.1 collective-permute-start.10
  20.7 3.0 %collective-permute-start.8 = (bf16[8,9216]{1,0:T(8,128)(2,1)S(1)}, bf16[8,9216]{1,0:T(8,128)(2,1)S(1)}, u32[]{:S(2)}, u32[]{:S(2)}) collective-permute-start(bf16[8,9216]{1,0:T(8,128)(2,1)S(1)} %get-tuple-element.44), channel_id=1, source_target_pairs={{0,4},{1,5},{2,6},{3,7},{4,0},{5,1},{6,2},{7,3},{8,12},{9,13},{10,... | collective-permute-start | bytes 442376 | tf_op jit(solution)/shard_map/ppermute | solution.py:49
  23.7 1.3 %collective-permute-start.9 = (bf16[8,9216]{1,0:T(8,128)(2,1)S(1)}, bf16[8,9216]{1,0:T(8,128)(2,1)S(1)}, u32[]{:S(2)}, u32[]{:S(2)}) collective-permute-start(bf16[8,9216]{1,0:T(8,128)(2,1)S(1)} %get-tuple-element.45), channel_id=1, source_target_pairs={{0,6},{1,7},{2,4},{3,5},{4,2},{5,3},{6,0},{7,1},{8,14},{9,15},{10,... | collective-permute-start | bytes 442376 | tf_op jit(solution)/shard_map/ppermute | solution.py:49
  25.1 1.2 %numerators.3 = (f32[8,256]{1,0:T(8,128)S(1)}, f32[456,128]{1,0:T(8,128)S(1)}, f32[456,128]{1,0:T(8,128)S(1)}, f32[456,128]{1,0:T(8,128)S(1)}, f32[456,128]{1,0:T(8,128)S(1)}) custom-call(bf16[2304,48]{1,0:T(8,128)(2,1)S(1)} %get-tuple-element.31.refs_1_.pieces, bf16[8,9344]{1,0:T(8,128)(2,1)S(1)} %get-tuple-element.32.refs_0_, ...), custom_call_target="tpu_custom_call" | custom-call | flops 1048576 | bytes 65536 | tf_op jit(solution)/shard_map/numerators/pallas_call | solution.py:399
  26.3 2.5 %collective-permute-start.7 = (f16[456,128]{1,0:T(8,128)(2,1)S(1)}, f16[456,128]{1,0:T(8,128)(2,1)S(1)}, u32[]{:S(2)}, u32[]{:S(2)}) collective-permute-start(f16[456,128]{1,0:T(8,128)(2,1)S(1)} %convert_element_type.49), channel_id=1, source_target_pairs={{0,24},{8,16},{16,8},{24,0},{1,25},{9,17},{17,9},{25,1},{2,26},{10... | collective-permute-start | bytes 350216 | tf_op jit(solution)/shard_map/ppermute | solution.py:49
  28.9 0.6 %collective-permute-start.6 = (f16[456,128]{1,0:T(8,128)(2,1)S(1)}, f16[456,128]{1,0:T(8,128)(2,1)S(1)}, u32[]{:S(2)}, u32[]{:S(2)}) collective-permute-start(f16[456,128]{1,0:T(8,128)(2,1)S(1)} %convert_element_type.47), channel_id=1, source_target_pairs={{0,16},{8,24},{16,0},{24,8},{1,17},{9,25},{17,1},{25,9},{2,18},{10... | collective-permute-start | bytes 350216 | tf_op jit(solution)/shard_map/ppermute | solution.py:49
  29.5 0.3 collective-permute-done.10.refs_2_
  29.7 1.5 %collective-permute-start.5 = (f16[456,128]{1,0:T(8,128)(2,1)S(1)}, f16[456,128]{1,0:T(8,128)(2,1)S(1)}, u32[]{:S(2)}, u32[]{:S(2)}) collective-permute-start(f16[456,128]{1,0:T(8,128)(2,1)S(1)} %convert_element_type.45), channel_id=1, source_target_pairs={{0,8},{8,0},{16,24},{24,16},{1,9},{9,1},{17,25},{25,17},{2,10},{10... | collective-permute-start | bytes 350216 | tf_op jit(solution)/shard_map/ppermute | solution.py:49
  31.2 0.7 %numerators.4 = (f32[456,128]{1,0:T(8,128)S(1)}, f32[456,128]{1,0:T(8,128)S(1)}, f32[456,128]{1,0:T(8,128)S(1)}, f32[456,128]{1,0:T(8,128)S(1)}) custom-call(bf16[2304,48]{1,0:T(8,128)(2,1)S(1)} %get-tuple-element.31.refs_1_.pieces, f32[8,256]{1,0:T(8,128)S(1)} %get-tuple-element.43.refs_0_, bf16[8,9216]{1,0:T(8,128)(2,1)S(1)} %get-tuple-element.38.refs_4_.refs_1_, ...), custom_call_target="tpu_custom_call" | custom-call | flops 1048576 | bytes 65536 | tf_op jit(solution)/shard_map/numerators/pallas_call | solution.py:399
  32.0 2.8 %collective-permute-done.8.refs_1_ = bf16[8,9216]{1,0:T(8,128)(2,1)S(1)} collective-permute-done((bf16[8,9216]{1,0:T(8,128)(2,1)S(1)}, bf16[8,9216]{1,0:T(8,128)(2,1)S(1)}, u32[]{:S(2)}, u32[]{:S(2)}) %collective-permute-start.8) | collective-permute-done | bytes 147488 | tf_op jit(solution)/shard_map/ppermute | solution.py:49
  34.7 0.8 %numerators.5 = (f32[456,128]{1,0:T(8,128)S(1)}, f32[456,128]{1,0:T(8,128)S(1)}, f32[456,128]{1,0:T(8,128)S(1)}, f32[456,128]{1,0:T(8,128)S(1)}) custom-call(bf16[2304,48]{1,0:T(8,128)(2,1)S(1)} %get-tuple-element.31.refs_1_.pieces, f32[8,256]{1,0:T(8,128)S(1)} %get-tuple-element.43.refs_0_, bf16[8,9216]{1,0:T(8,128)(2,1)S(1)} %collective-permute-done.8.refs_1_, ...), custom_call_target="tpu_custom_call" | custom-call | flops 1048576 | bytes 65536 | tf_op jit(solution)/shard_map/numerators/pallas_call | solution.py:399
  35.6 2.5 %collective-permute-start.13 = (f16[456,128]{1,0:T(8,128)(2,1)S(1)}, f16[456,128]{1,0:T(8,128)(2,1)S(1)}, u32[]{:S(2)}, u32[]{:S(2)}) collective-permute-start(f16[456,128]{1,0:T(8,128)(2,1)S(1)} %convert_element_type.58), channel_id=1, source_target_pairs={{0,24},{8,16},{16,8},{24,0},{1,25},{9,17},{17,9},{25,1},{2,26},{10... | collective-permute-start | bytes 350216 | tf_op jit(solution)/shard_map/ppermute | solution.py:49
  38.1 0.5 %collective-permute-start.12 = (f16[456,128]{1,0:T(8,128)(2,1)S(1)}, f16[456,128]{1,0:T(8,128)(2,1)S(1)}, u32[]{:S(2)}, u32[]{:S(2)}) collective-permute-start(f16[456,128]{1,0:T(8,128)(2,1)S(1)} %convert_element_type.56), channel_id=1, source_target_pairs={{0,16},{8,24},{16,0},{24,8},{1,17},{9,25},{17,1},{25,9},{2,18},{10... | collective-permute-start | bytes 350216 | tf_op jit(solution)/shard_map/ppermute | solution.py:49
  38.6 0.5 %collective-permute-start.11 = (f16[456,128]{1,0:T(8,128)(2,1)S(1)}, f16[456,128]{1,0:T(8,128)(2,1)S(1)}, u32[]{:S(2)}, u32[]{:S(2)}) collective-permute-start(f16[456,128]{1,0:T(8,128)(2,1)S(1)} %convert_element_type.54), channel_id=1, source_target_pairs={{0,8},{8,0},{16,24},{24,16},{1,9},{9,1},{17,25},{25,17},{2,10},{10... | collective-permute-start | bytes 350216 | tf_op jit(solution)/shard_map/ppermute | solution.py:49
  39.2 0.1 convert_add_fusion.1.refs_0_
  39.2 2.7 %denominators.1.denom = f32[56,2304]{1,0:T(8,128)S(1)} custom-call(bf16[2304,256]{1,0:T(8,128)(2,1)S(1)} %get-tuple-element.30.weights, f32[8,128]{1,0:T(8,128)S(1)} %slice.12.refs_0_, f32[8,128]{1,0:T(8,128)S(1)} %slice_convert_fusion.2.refs_1_, f32[8,128]{1,0:T(8,128)S(1)} %slice_convert_fusion.1.refs_2_, f32[8,128]{1,0:T(8,128)S(1)} %slice_convert_fusion.refs_3_), custom_call_target="tpu_custom_call" | custom-call | flops 1048576 | bytes 65536 | tf_op jit(solution)/shard_map/denominators/pallas_call | solution.py:451
  42.0 0.1 collective-permute-done.13
  42.1 1.2 %collective-permute-done.12 = f16[456,128]{1,0:T(8,128)(2,1)S(1)} collective-permute-done((f16[456,128]{1,0:T(8,128)(2,1)S(1)}, f16[456,128]{1,0:T(8,128)(2,1)S(1)}, u32[]{:S(2)}, u32[]{:S(2)}) %collective-permute-start.12) | collective-permute-done | bytes 116768 | tf_op jit(solution)/shard_map/ppermute | solution.py:49
  43.3 0.2 collective-permute-done.11
  43.5 0.1 convert_add_fusion.refs_1_
  43.5 0.9 %averages.1 = f32[50,2304]{1,0:T(8,128)} custom-call(f32[56,2304]{1,0:T(8,128)S(1)} %denominators.1.denom, f32[456,128]{1,0:T(8,128)S(1)} %convert_add_fusion.1.refs_0_, f32[456,128]{1,0:T(8,128)S(1)} %convert_add_fusion.refs_1_), custom_call_target="tpu_custom_call" | custom-call | flops 1048576 | bytes 65536 | tf_op jit(solution)/shard_map/averages/pallas_call | solution.py:473
  (22 shorter events, 0.2 us)
Async XLA Ops:
  0.7 1.3 %copy-start = (bf16[32,18432]{1,0:T(8,128)(2,1)S(1)}, bf16[32,18432]{1,0:T(8,128)(2,1)}, u32[]{:S(2)}) copy-start(bf16[32,18432]{1,0:T(8,128)(2,1)} %img.1) | copy-start | bytes 3538948
  2.0 5.9 %copy-start.1 = (f32[16,18432]{1,0:T(8,128)S(1)}, f32[16,18432]{1,0:T(8,128)}, u32[]{:S(2)}) copy-start(f32[16,18432]{1,0:T(8,128)} %table.1) | copy-start | bytes 3538948
  2.1 10.0 %collective-permute-start.3 = (bf16[4,8,4608]{2,1,0:T(8,128)(2,1)S(1)}, bf16[4,8,4608]{2,1,0:T(8,128)(2,1)S(1)}, u32[]{:S(2)}, u32[]{:S(2)}) collective-permute-start(bf16[4,8,4608]{2,1,0:T(8,128)(2,1)S(1)} %get-tuple-element.37), channel_id=1, source_target_pairs={{0,1},{1,0},{2,3},{3,2},{4,5},{5,4},{6,7},{7,6},{8,9},{9,8},{10,11... | collective-permute-start | bytes 884744 | tf_op jit(solution)/shard_map/ppermute | solution.py:49
  2.6 9.5 %collective-permute-start.2 = (bf16[8,9344]{1,0:T(8,128)(2,1)S(1)}, bf16[8,9344]{1,0:T(8,128)(2,1)S(1)}, u32[]{:S(2)}, u32[]{:S(2)}) collective-permute-start(bf16[8,9344]{1,0:T(8,128)(2,1)S(1)} %get-tuple-element.35), channel_id=1, source_target_pairs={{0,6},{1,7},{2,4},{3,5},{4,2},{5,3},{6,0},{7,1},{8,14},{9,15},{10,... | collective-permute-start | bytes 448520 | tf_op jit(solution)/shard_map/ppermute | solution.py:49
  7.3 8.8 %collective-permute-start = (bf16[8,9344]{1,0:T(8,128)(2,1)S(1)}, bf16[8,9344]{1,0:T(8,128)(2,1)S(1)}, u32[]{:S(2)}, u32[]{:S(2)}) collective-permute-start(bf16[8,9344]{1,0:T(8,128)(2,1)S(1)} %get-tuple-element.33), channel_id=1, source_target_pairs={{0,2},{1,3},{2,0},{3,1},{4,6},{5,7},{6,4},{7,5},{8,10},{9,11},{10,... | collective-permute-start | bytes 448520 | tf_op jit(solution)/shard_map/ppermute | solution.py:49
  7.3 13.3 %collective-permute-start.1 = (bf16[8,9344]{1,0:T(8,128)(2,1)S(1)}, bf16[8,9344]{1,0:T(8,128)(2,1)S(1)}, u32[]{:S(2)}, u32[]{:S(2)}) collective-permute-start(bf16[8,9344]{1,0:T(8,128)(2,1)S(1)} %get-tuple-element.34), channel_id=1, source_target_pairs={{0,4},{1,5},{2,6},{3,7},{4,0},{5,1},{6,2},{7,3},{8,12},{9,13},{10,... | collective-permute-start | bytes 448520 | tf_op jit(solution)/shard_map/ppermute | solution.py:49
  20.6 4.5 %collective-permute-start.4 = (bf16[4,8,4736]{2,1,0:T(8,128)(2,1)S(1)}, bf16[4,8,4736]{2,1,0:T(8,128)(2,1)S(1)}, u32[]{:S(2)}, u32[]{:S(2)}) collective-permute-start(bf16[4,8,4736]{2,1,0:T(8,128)(2,1)S(1)} %cross.1), channel_id=1, source_target_pairs={{0,1},{1,0},{2,3},{3,2},{4,5},{5,4},{6,7},{7,6},{8,9},{9,8},{10,11... | collective-permute-start | bytes 909320 | tf_op jit(solution)/shard_map/ppermute | solution.py:49
  20.6 9.1 %collective-permute-start.10 = (bf16[8,9216]{1,0:T(8,128)(2,1)S(1)}, bf16[8,9216]{1,0:T(8,128)(2,1)S(1)}, u32[]{:S(2)}, u32[]{:S(2)}) collective-permute-start(bf16[8,9216]{1,0:T(8,128)(2,1)S(1)} %get-tuple-element.46), channel_id=1, source_target_pairs={{0,2},{1,3},{2,0},{3,1},{4,6},{5,7},{6,4},{7,5},{8,10},{9,11},{10,... | collective-permute-start | bytes 442376 | tf_op jit(solution)/shard_map/ppermute | solution.py:49
  20.7 14.0 %collective-permute-start.8 = (bf16[8,9216]{1,0:T(8,128)(2,1)S(1)}, bf16[8,9216]{1,0:T(8,128)(2,1)S(1)}, u32[]{:S(2)}, u32[]{:S(2)}) collective-permute-start(bf16[8,9216]{1,0:T(8,128)(2,1)S(1)} %get-tuple-element.44), channel_id=1, source_target_pairs={{0,4},{1,5},{2,6},{3,7},{4,0},{5,1},{6,2},{7,3},{8,12},{9,13},{10,... | collective-permute-start | bytes 442376 | tf_op jit(solution)/shard_map/ppermute | solution.py:49
  23.7 11.0 %collective-permute-start.9 = (bf16[8,9216]{1,0:T(8,128)(2,1)S(1)}, bf16[8,9216]{1,0:T(8,128)(2,1)S(1)}, u32[]{:S(2)}, u32[]{:S(2)}) collective-permute-start(bf16[8,9216]{1,0:T(8,128)(2,1)S(1)} %get-tuple-element.45), channel_id=1, source_target_pairs={{0,6},{1,7},{2,4},{3,5},{4,2},{5,3},{6,0},{7,1},{8,14},{9,15},{10,... | collective-permute-start | bytes 442376 | tf_op jit(solution)/shard_map/ppermute | solution.py:49
  26.3 12.3 %collective-permute-start.7 = (f16[456,128]{1,0:T(8,128)(2,1)S(1)}, f16[456,128]{1,0:T(8,128)(2,1)S(1)}, u32[]{:S(2)}, u32[]{:S(2)}) collective-permute-start(f16[456,128]{1,0:T(8,128)(2,1)S(1)} %convert_element_type.49), channel_id=1, source_target_pairs={{0,24},{8,16},{16,8},{24,0},{1,25},{9,17},{17,9},{25,1},{2,26},{10... | collective-permute-start | bytes 350216 | tf_op jit(solution)/shard_map/ppermute | solution.py:49
  28.9 10.3 %collective-permute-start.6 = (f16[456,128]{1,0:T(8,128)(2,1)S(1)}, f16[456,128]{1,0:T(8,128)(2,1)S(1)}, u32[]{:S(2)}, u32[]{:S(2)}) collective-permute-start(f16[456,128]{1,0:T(8,128)(2,1)S(1)} %convert_element_type.47), channel_id=1, source_target_pairs={{0,16},{8,24},{16,0},{24,8},{1,17},{9,25},{17,1},{25,9},{2,18},{10... | collective-permute-start | bytes 350216 | tf_op jit(solution)/shard_map/ppermute | solution.py:49
  29.7 9.4 %collective-permute-start.5 = (f16[456,128]{1,0:T(8,128)(2,1)S(1)}, f16[456,128]{1,0:T(8,128)(2,1)S(1)}, u32[]{:S(2)}, u32[]{:S(2)}) collective-permute-start(f16[456,128]{1,0:T(8,128)(2,1)S(1)} %convert_element_type.45), channel_id=1, source_target_pairs={{0,8},{8,0},{16,24},{24,16},{1,9},{9,1},{17,25},{25,17},{2,10},{10... | collective-permute-start | bytes 350216 | tf_op jit(solution)/shard_map/ppermute | solution.py:49
  35.6 6.5 %collective-permute-start.13 = (f16[456,128]{1,0:T(8,128)(2,1)S(1)}, f16[456,128]{1,0:T(8,128)(2,1)S(1)}, u32[]{:S(2)}, u32[]{:S(2)}) collective-permute-start(f16[456,128]{1,0:T(8,128)(2,1)S(1)} %convert_element_type.58), channel_id=1, source_target_pairs={{0,24},{8,16},{16,8},{24,0},{1,25},{9,17},{17,9},{25,1},{2,26},{10... | collective-permute-start | bytes 350216 | tf_op jit(solution)/shard_map/ppermute | solution.py:49
  38.1 5.2 %collective-permute-start.12 = (f16[456,128]{1,0:T(8,128)(2,1)S(1)}, f16[456,128]{1,0:T(8,128)(2,1)S(1)}, u32[]{:S(2)}, u32[]{:S(2)}) collective-permute-start(f16[456,128]{1,0:T(8,128)(2,1)S(1)} %convert_element_type.56), channel_id=1, source_target_pairs={{0,16},{8,24},{16,0},{24,8},{1,17},{9,25},{17,1},{25,9},{2,18},{10... | collective-permute-start | bytes 350216 | tf_op jit(solution)/shard_map/ppermute | solution.py:49
  38.6 4.9 %collective-permute-start.11 = (f16[456,128]{1,0:T(8,128)(2,1)S(1)}, f16[456,128]{1,0:T(8,128)(2,1)S(1)}, u32[]{:S(2)}, u32[]{:S(2)}) collective-permute-start(f16[456,128]{1,0:T(8,128)(2,1)S(1)} %convert_element_type.54), channel_id=1, source_target_pairs={{0,8},{8,0},{16,24},{24,16},{1,9},{9,1},{17,25},{25,17},{2,10},{10... | collective-permute-start | bytes 350216 | tf_op jit(solution)/shard_map/ppermute | solution.py:49

commit v7 on v6

--- a/solution.py
+++ b/solution.py
@@ -104,35 +104,28 @@
     tags = jnp.dot(stack.astype(F32).astype(BF16), spread, preferred_element_type=F32)
     place = lax.broadcasted_iota(jnp.int32, (ROWS, LANES), 1) // count
     lower = lax.broadcasted_iota(jnp.int32, (ROWS, LANES), 0) // (ROWS // CORES)
-    first = (edges[1] - edges[0]) * LANES
     for step in range(places):
         there = partner(here, step, places) * CORES
-        for target in range(CORES):
-            start = pl.multiple_of((there + target) * cols + edges[0] * LANES, LANES)
-            for g in range(groups):
-                outs[step][:, pl.ds((target * groups + g) * first, first)] = img[
-                    pl.ds(g * ROWS, ROWS), pl.ds(start, first)
-                ]
         slot = (step * CORES + lower) % (LANES // count)
-        mine = jnp.where(place == slot, tags, 0.0)
-        outs[step][:, pl.ds(CORES * groups * first, LANES)] = mine.astype(BF16)
-        if len(edges) == 2:
-            continue
-        width = (edges[2] - edges[1]) * LANES
-        for cross in range(CORES):
-            start = pl.multiple_of((there + (core ^ cross)) * cols + edges[1] * LANES, LANES)
-            for g in range(groups):
-                outs[places + cross][step, :, pl.ds(g * width, width)] = img[
-                    pl.ds(g * ROWS, ROWS), pl.ds(start, width)
-                ]
+        mine = jnp.where(place == slot, tags, 0.0).astype(BF16)
+        for chunk in range(len(edges) - 1):
+            width = (edges[chunk + 1] - edges[chunk]) * LANES
+            for cross in range(CORES):
+                out = outs[chunk * CORES + cross]
+                start = (there + (core ^ cross)) * cols + edges[chunk] * LANES
+                across = pl.ds(pl.multiple_of(start, LANES), width)
+                for g in range(groups):
+                    out[step, :, pl.ds(g * width, width)] = img[pl.ds(g * ROWS, ROWS), across]
+                if chunk == 0:
+                    out[step, :, pl.ds(groups * width, LANES)] = mine
 
 
 def pack(images, labels, cols, edges):
     mem = lax.axis_size("mem")
     groups = images.shape[0] // ROWS
-    wide = [groups * (high - low) * LANES for low, high in zip(edges, edges[1:])]
-    shapes = [jax.ShapeDtypeStruct((ROWS, CORES * wide[0] + LANES), BF16)] * (mem // CORES)
-    for width in wide[1:]:
+    shapes = []
+    for chunk, (low, high) in enumerate(zip(edges, edges[1:])):
+        width = groups * (high - low) * LANES + (0 if chunk else LANES)
         shapes += [jax.ShapeDtypeStruct((mem // CORES, ROWS, width), BF16)] * CORES
     outs = pl.pallas_call(
         functools.partial(pack_kernel, mem, cols, edges),
@@ -142,7 +135,7 @@
         name="pack",
         **params(8),
     )(images, labels)
-    return outs[: mem // CORES], outs[mem // CORES :]
+    return list(zip(outs[::CORES], outs[1::CORES]))
 
 
 def join_kernel(kept, crossed, *refs):
@@ -163,27 +156,6 @@
         name="join",
         **params(8),
     )(kept, crossed, *after)
-
-
-def cross_kernel(places, *refs):
-    blocks, out = refs[:places], refs[-1]
-    other = 1 - lax.rem(lax.axis_index("mem"), CORES)
-    span = (blocks[0].shape[1] - LANES) // CORES
-    for step, block in enumerate(blocks):
-        out[step, :, pl.ds(0, span)] = block[:, pl.ds(pl.multiple_of(other * span, LANES), span)]
-        out[step, :, pl.ds(span, LANES)] = block[:, pl.ds(CORES * span, LANES)]
-
-
-def cross(blocks, after):
-    span = (blocks[0].shape[1] - LANES) // CORES
-    return pl.pallas_call(
-        functools.partial(cross_kernel, len(blocks)),
-        out_shape=jax.ShapeDtypeStruct((len(blocks), ROWS, span + LANES), BF16),
-        in_specs=[VMEM] * len(blocks) + [ANY] * len(after),
-        out_specs=VMEM,
-        name="cross",
-        **params(8),
-    )(*blocks, *after)
 
 
 def table_kernel(turns, table, pieces, weights, ctf, square, sem):
@@ -272,39 +244,30 @@
     ]
 
 
-def numer_kernel(mem, count, first, rows, base, tiles, segments, steps, added, pieces, *refs):
+def numer_kernel(mem, count, first, rows, base, tiles, segments, steps, added, ties, pieces, *refs):
     refs = list(refs)
     grp = lax.axis_size("grp")
     lanes = (steps[1] - steps[0]) * CORES * count
     groups = count // ROWS
-    places = mem // CORES
-    core = lax.rem(lax.axis_index("mem"), CORES)
     own = lax.axis_index("grp")
     if not first:
         tags = refs.pop(0)
     for chunk, wide, src, dst, width in segments:
         across = pl.ds(dst * LANES, width * LANES)
-        taken = places if chunk == 0 else steps[1] - steps[0]
+        taken = steps[1] - steps[0]
         msgs, refs = refs[:taken], refs[taken:]
-        if chunk == 0:
-            crossed = refs.pop(0)
-            past = groups * wide * LANES
-        for step in range(*steps):
+        past = groups * wide * LANES
+        far = past + (LANES if chunk == 0 else 0)
+        for step in range(taken):
             for g in range(groups):
                 low = (g * wide + src) * LANES
-                if chunk == 0:
-                    kept = pl.multiple_of(core * (groups * wide * LANES) + low, LANES)
-                    near = msgs[step][:, pl.ds(kept, width * LANES)]
-                    far = crossed[step, :, pl.ds(low, width * LANES)]
-                else:
-                    msg = msgs[step - steps[0]]
-                    near = msg[:, pl.ds(low, width * LANES)]
-                    far = msg[:, pl.ds(groups * wide * LANES + low, width * LANES)]
-                at = (step - steps[0]) * CORES * count + g * ROWS
-                refs[-3][pl.ds(at, ROWS), across] = near
-                refs[-3][pl.ds(at + count, ROWS), across] = far
+                at = step * CORES * count + g * ROWS
+                for cross in range(CORES):
+                    refs[-3][pl.ds(at + cross * count, ROWS), across] = msgs[step][
+                        :, pl.ds(cross * far + low, width * LANES)
+                    ]
     partial = refs[:added]
-    refs = refs[added:]
+    refs = refs[added + ties :]
     if first:
         tags = refs.pop(0)
         per_tile = LANES // count
@@ -313,9 +276,9 @@
             total = jnp.zeros((ROWS, LANES), F32)
             for slot in range(tile * per_tile, (tile + 1) * per_tile, CORES):
                 step = slot // CORES
-                near = msgs[step][:, pl.ds(CORES * past, LANES)].astype(F32)
-                far = crossed[step, :, pl.ds(past, LANES)].astype(F32)
-                total += jnp.concatenate([near[:half] + far[half:], near[half:]], axis=0)
+                one = msgs[step][:, pl.ds(past, LANES)].astype(F32)
+                other = msgs[step][:, pl.ds(far + past, LANES)].astype(F32)
+                total += jnp.concatenate([one[:half] + other[half:], one[half:]], axis=0)
             tags[:, pl.ds(tile * LANES, LANES)] = total
     sums = refs[:grp]
     data, product, parts = refs[grp:]
@@ -377,7 +340,7 @@
                     row += 1
 
 
-def numerators(count, pieces, tags, arrived, chunk, edges, rows, steps, partial=()):
+def numerators(count, pieces, tags, arrived, chunk, edges, rows, steps, partial, after):
     mem, grp = lax.axis_size("mem"), lax.axis_size("grp")
     first = chunk == 0
     here = (rows[chunk], rows[chunk + 1])
@@ -388,7 +351,7 @@
         low, high = max(edges[c], base), min(edges[c + 1], stop)
         if low < high:
             segments.append((c, edges[c + 1] - edges[c], low - edges[c], low - base, high - low))
-            msgs += arrived[c] if c == 0 else arrived[c][slice(*steps)]
+            msgs += arrived[c][slice(*steps)]
     lanes = (steps[1] - steps[0]) * CORES * count
     span = (here[1] - here[0]) * ANGLES
     tiles = stop - base
@@ -398,10 +361,11 @@
     operands = [pieces] + ([] if first else [tags]) + msgs + list(partial)
     outs = pl.pallas_call(
         functools.partial(
-            numer_kernel, mem, count, first, here, base, tiles, tuple(segments), steps, len(partial)
+            numer_kernel, mem, count, first, here, base, tiles, tuple(segments), steps, len(partial),
+            len(after),
         ),
         out_shape=shapes,
-        in_specs=[VMEM] * len(operands),
+        in_specs=[VMEM] * len(operands) + [ANY] * len(after),
         out_specs=[VMEM] * len(shapes),
         scratch_shapes=[
             pltpu.VMEM((lanes, tiles * LANES), BF16),
@@ -410,7 +374,7 @@
         ],
         name="numerators",
         **params(16),
-    )(*operands)
+    )(*operands, *after)
     if first:
         return outs[0], outs[1:]
     return tags, outs
@@ -502,19 +466,15 @@
         table = lax.dynamic_slice_in_dim(ctf_table, lax.axis_index("mem") * span, span, 1)
         table = jnp.pad(table, ((0, 0), (0, cols - span)))
     pieces, weights = tables(table, cols, span // ANGLES)
-    firsts, seconds = pack(images, jnp.stack([classes, bins, rotations]), cols, edges)
-    others = range(places - 1, 0, -1)
-    here = {step: send(firsts[step], "mem", step, CORES) for step in others}
-    here[0] = firsts[0]
-    first = [here[step] for step in range(places)]
-    arrived, after = [], [pieces]
-    if seconds:
-        kept, crossed = seconds[0], send(seconds[1], "mem", 0, CORES, 1)
-        msgs = join(kept, crossed, [first[-1], pieces])
-        here = {step: send(msgs[step], "mem", step, CORES) for step in others}
+    chunks = pack(images, jnp.stack([classes, bins, rotations]), cols, edges)
+    arrived, after, ties = [], [], []
+    for kept, crossed in chunks:
+        msgs = join(kept, send(crossed, "mem", 0, CORES, 1), after)
+        here = {step: send(msgs[step], "mem", step, CORES) for step in range(places - 1, 0, -1)}
         here[0] = msgs[0]
-        arrived, after = [[here[step] for step in range(places)]], [msgs[0]]
-    arrived = [first + [send(cross(first, after), "mem", 0, CORES, 1)]] + arrived
+        arrived.append([here[step] for step in range(places)])
+        after = [pieces]
+        ties = [msgs[0]] if len(arrived) > 1 else []
     tags, sums, blocks = None, [], []
     for chunk in range(len(edges) - 1):
         cuts = [0, places]
@@ -522,7 +482,10 @@
             cuts = [0, places // 2, places]
         here = ()
         for steps in zip(cuts, cuts[1:]):
-            tags, here = numerators(count, pieces, tags, arrived, chunk, edges, rows, steps, here)
+            tie = [] if chunk else ties
+            tags, here = numerators(
+                count, pieces, tags, arrived, chunk, edges, rows, steps, here, tie
+            )
         others = [send(here[step].astype(HALF), "grp", step) for step in range(1, grp)]
         if chunk == 0:
             blocks = [tag_block(part, rows[1] * ANGLES) for part in [here[0]] + others]

time: 45.3 us -> 43.7 us (0.965); the launches traced: 44.4 us -> 43.5 us
  waiting for transfers between devices: 15.9 us -> 13.5 us
  starting transfers between devices: 18.5 us -> 19.9 us
    ppermute x14, waiting for transfers between devices: 15.9 us -> 13.5 us  [send(): return lax.ppermute(value, axis, pairs)]
    ppermute x14, starting transfers between devices: 18.5 us -> 19.9 us  [send(): return lax.ppermute(value, axis, pairs)]
  transfers between devices with their start and end apart: 14 -> 14, of which waited for: 8 -> 6; matrix products, arithmetic and copies ran while one was open for 0% -> 0% of each run, Pallas kernels for 15% -> 15%
where the time goes in v7:
time: 43.7 us; the launch traced here: 43.5 us
  starting transfers between devices  19.9 us (46%)
  waiting for transfers between devices  13.5 us (31%)
  Pallas kernels  7.76 us (18%)
  local copies, waits for them, and re-layouts  1.28 us (3%)
  other arithmetic  0.95 us (2%)
    ppermute x14, starting transfers between devices, send(): return lax.ppermute(value, axis, pairs)  19.9 us
    ppermute x14, waiting for transfers between devices, send(): return lax.ppermute(value, axis, pairs)  13.5 us
    pallas_call x1, Pallas kernels, denominators(): pl.pallas_call(functools.partial(denom_kernel, first, lanes), out_shape=j...  2.74 us
    pallas_call x3, Pallas kernels, numerators(): pl.pallas_call(functools.partial(numer_kernel, mem, count, first, here, b...  2.73 us
    unnamed x4, local copies, waits for them, and re-layouts  1.27 us
    pallas_call x1, Pallas kernels, tables(): pl.pallas_call(functools.partial(table_kernel, turns), out_shape=[jax.Sha...  1.18 us
    pallas_call x1, Pallas kernels, averages(): pl.pallas_call(functools.partial(average_kernel, rows), out_shape=jax.Sha...  0.89 us
  transfers between devices with their start and end apart: 14, of which 6 were waited for; matrix products, arithmetic and copies ran while one was open for 0% of the time, Pallas kernels for 15%

profile of v7, /device:TPU:0, one launch (start us, length us, event | category | flops | bytes accessed | tf_op | source)
XLA Modules:
  0.0 43.5 jit_solution(2883078960886740227)
XLA Ops:
  0.0 0.7 %pad_add_fusion.labels = s32[3,32]{1,0:T(4,128)S(1)} fusion(s32[1,32]{1,0:T(1,128)} %bitcast.3, s32[1,32]{1,0:T(1,128)} %bitcast.4, s32[1,32]{1,0:T(1,128)} %bitcast.5), kind=kLoop, calls=%fused_computation.5 | loop fusion | flops 192 | bytes 768 | tf_op jit(solution)/shard_map/stack | solution.py:469
  0.7 1.3 %copy-done = bf16[32,18432]{1,0:T(8,128)(2,1)S(1)} copy-done((bf16[32,18432]{1,0:T(8,128)(2,1)S(1)}, bf16[32,18432]{1,0:T(8,128)(2,1)}, u32[]{:S(2)}) %copy-start) | copy-done | bytes 1179672
  2.0 0.1 pack.1
  2.1 0.5 %collective-permute-start = (bf16[4,8,4736]{2,1,0:T(8,128)(2,1)S(1)}, bf16[4,8,4736]{2,1,0:T(8,128)(2,1)S(1)}, u32[]{:S(2)}, u32[]{:S(2)}) collective-permute-start(bf16[4,8,4736]{2,1,0:T(8,128)(2,1)S(1)} %get-tuple-element.35), channel_id=1, source_target_pairs={{0,1},{1,0},{2,3},{3,2},{4,5},{5,4},{6,7},{7,6},{8,9},{9,8},{10,11... | collective-permute-start | bytes 909320 | tf_op jit(solution)/shard_map/ppermute | solution.py:49
  2.6 0.1 collective-permute-start.4
  2.7 1.1 %collective-permute-done.crossed = bf16[4,8,4736]{2,1,0:T(8,128)(2,1)S(1)} collective-permute-done((bf16[4,8,4736]{2,1,0:T(8,128)(2,1)S(1)}, bf16[4,8,4736]{2,1,0:T(8,128)(2,1)S(1)}, u32[]{:S(2)}, u32[]{:S(2)}) %collective-permute-start) | collective-permute-done | bytes 303136 | tf_op jit(solution)/shard_map/ppermute | solution.py:49
  3.9 3.0 %collective-permute-start.1 = (bf16[8,9472]{1,0:T(8,128)(2,1)S(1)}, bf16[8,9472]{1,0:T(8,128)(2,1)S(1)}, u32[]{:S(2)}, u32[]{:S(2)}) collective-permute-start(bf16[8,9472]{1,0:T(8,128)(2,1)S(1)} %get-tuple-element.37), channel_id=1, source_target_pairs={{0,2},{1,3},{2,0},{3,1},{4,6},{5,7},{6,4},{7,5},{8,10},{9,11},{10,... | collective-permute-start | bytes 454664 | tf_op jit(solution)/shard_map/ppermute | solution.py:49
  6.9 2.6 %collective-permute-start.2 = (bf16[8,9472]{1,0:T(8,128)(2,1)S(1)}, bf16[8,9472]{1,0:T(8,128)(2,1)S(1)}, u32[]{:S(2)}, u32[]{:S(2)}) collective-permute-start(bf16[8,9472]{1,0:T(8,128)(2,1)S(1)} %get-tuple-element.38), channel_id=1, source_target_pairs={{0,4},{1,5},{2,6},{3,7},{4,0},{5,1},{6,2},{7,3},{8,12},{9,13},{10,... | collective-permute-start | bytes 454664 | tf_op jit(solution)/shard_map/ppermute | solution.py:49
  9.5 1.2 %tables.1 = (bf16[2304,48]{1,0:T(8,128)(2,1)S(1)}, bf16[2304,256]{1,0:T(8,128)(2,1)S(1)}) custom-call(f32[16,18432]{1,0:T(8,128)S(1)} %copy-done.1), custom_call_target="tpu_custom_call" | custom-call | flops 1048576 | bytes 65536 | tf_op jit(solution)/shard_map/tables/pallas_call | solution.py:205
  10.7 1.0 %collective-permute-start.10 = (bf16[8,9216]{1,0:T(8,128)(2,1)S(1)}, bf16[8,9216]{1,0:T(8,128)(2,1)S(1)}, u32[]{:S(2)}, u32[]{:S(2)}) collective-permute-start(bf16[8,9216]{1,0:T(8,128)(2,1)S(1)} %get-tuple-element.50), channel_id=1, source_target_pairs={{0,2},{1,3},{2,0},{3,1},{4,6},{5,7},{6,4},{7,5},{8,10},{9,11},{10,... | collective-permute-start | bytes 442376 | tf_op jit(solution)/shard_map/ppermute | solution.py:49
  11.7 3.5 %collective-permute-start.8 = (bf16[8,9216]{1,0:T(8,128)(2,1)S(1)}, bf16[8,9216]{1,0:T(8,128)(2,1)S(1)}, u32[]{:S(2)}, u32[]{:S(2)}) collective-permute-start(bf16[8,9216]{1,0:T(8,128)(2,1)S(1)} %get-tuple-element.48), channel_id=1, source_target_pairs={{0,4},{1,5},{2,6},{3,7},{4,0},{5,1},{6,2},{7,3},{8,12},{9,13},{10,... | collective-permute-start | bytes 442376 | tf_op jit(solution)/shard_map/ppermute | solution.py:49
  15.2 0.0 collective-permute-done.1.refs_1_
  15.2 2.1 %collective-permute-start.9 = (bf16[8,9216]{1,0:T(8,128)(2,1)S(1)}, bf16[8,9216]{1,0:T(8,128)(2,1)S(1)}, u32[]{:S(2)}, u32[]{:S(2)}) collective-permute-start(bf16[8,9216]{1,0:T(8,128)(2,1)S(1)} %get-tuple-element.49), channel_id=1, source_target_pairs={{0,6},{1,7},{2,4},{3,5},{4,2},{5,3},{6,0},{7,1},{8,14},{9,15},{10,... | collective-permute-start | bytes 442376 | tf_op jit(solution)/shard_map/ppermute | solution.py:49
  17.2 3.9 %collective-permute-done.2.refs_2_ = bf16[8,9472]{1,0:T(8,128)(2,1)S(1)} collective-permute-done((bf16[8,9472]{1,0:T(8,128)(2,1)S(1)}, bf16[8,9472]{1,0:T(8,128)(2,1)S(1)}, u32[]{:S(2)}, u32[]{:S(2)}) %collective-permute-start.2) | collective-permute-done | bytes 151584 | tf_op jit(solution)/shard_map/ppermute | solution.py:49
  21.1 1.2 %numerators.3 = (f32[8,256]{1,0:T(8,128)S(1)}, f32[456,128]{1,0:T(8,128)S(1)}, f32[456,128]{1,0:T(8,128)S(1)}, f32[456,128]{1,0:T(8,128)S(1)}, f32[456,128]{1,0:T(8,128)S(1)}) custom-call(bf16[2304,48]{1,0:T(8,128)(2,1)S(1)} %get-tuple-element.33.refs_0_.pieces, bf16[8,9472]{1,0:T(8,128)(2,1)S(1)} %get-tuple-element.36.refs_0_, ...), custom_call_target="tpu_custom_call" | custom-call | flops 1048576 | bytes 65536 | tf_op jit(solution)/shard_map/numerators/pallas_call | solution.py:362
  22.4 2.5 %collective-permute-start.7 = (f16[456,128]{1,0:T(8,128)(2,1)S(1)}, f16[456,128]{1,0:T(8,128)(2,1)S(1)}, u32[]{:S(2)}, u32[]{:S(2)}) collective-permute-start(f16[456,128]{1,0:T(8,128)(2,1)S(1)} %convert_element_type.49), channel_id=1, source_target_pairs={{0,24},{8,16},{16,8},{24,0},{1,25},{9,17},{17,9},{25,1},{2,26},{10... | collective-permute-start | bytes 350216 | tf_op jit(solution)/shard_map/ppermute | solution.py:49
  25.0 0.6 %collective-permute-start.6 = (f16[456,128]{1,0:T(8,128)(2,1)S(1)}, f16[456,128]{1,0:T(8,128)(2,1)S(1)}, u32[]{:S(2)}, u32[]{:S(2)}) collective-permute-start(f16[456,128]{1,0:T(8,128)(2,1)S(1)} %convert_element_type.47), channel_id=1, source_target_pairs={{0,16},{8,24},{16,0},{24,8},{1,17},{9,25},{17,1},{25,9},{2,18},{10... | collective-permute-start | bytes 350216 | tf_op jit(solution)/shard_map/ppermute | solution.py:49
  25.5 0.0 collective-permute-done.10.refs_2_
  25.6 0.5 %collective-permute-start.5 = (f16[456,128]{1,0:T(8,128)(2,1)S(1)}, f16[456,128]{1,0:T(8,128)(2,1)S(1)}, u32[]{:S(2)}, u32[]{:S(2)}) collective-permute-start(f16[456,128]{1,0:T(8,128)(2,1)S(1)} %convert_element_type.45), channel_id=1, source_target_pairs={{0,8},{8,0},{16,24},{24,16},{1,9},{9,1},{17,25},{25,17},{2,10},{10... | collective-permute-start | bytes 350216 | tf_op jit(solution)/shard_map/ppermute | solution.py:49
  26.1 0.7 %numerators.4 = (f32[456,128]{1,0:T(8,128)S(1)}, f32[456,128]{1,0:T(8,128)S(1)}, f32[456,128]{1,0:T(8,128)S(1)}, f32[456,128]{1,0:T(8,128)S(1)}) custom-call(bf16[2304,48]{1,0:T(8,128)(2,1)S(1)} %get-tuple-element.33.refs_0_.pieces, f32[8,256]{1,0:T(8,128)S(1)} %get-tuple-element.47.refs_0_, bf16[8,9216]{1,0:T(8,128)(2,1)S(1)} %get-tuple-element.42.refs_4_.refs_1_, ...), custom_call_target="tpu_custom_call" | custom-call | flops 1048576 | bytes 65536 | tf_op jit(solution)/shard_map/numerators/pallas_call | solution.py:362
  26.8 7.0 %collective-permute-done.8.refs_1_ = bf16[8,9216]{1,0:T(8,128)(2,1)S(1)} collective-permute-done((bf16[8,9216]{1,0:T(8,128)(2,1)S(1)}, bf16[8,9216]{1,0:T(8,128)(2,1)S(1)}, u32[]{:S(2)}, u32[]{:S(2)}) %collective-permute-start.8) | collective-permute-done | bytes 147488 | tf_op jit(solution)/shard_map/ppermute | solution.py:49
  33.9 0.8 %numerators.5 = (f32[456,128]{1,0:T(8,128)S(1)}, f32[456,128]{1,0:T(8,128)S(1)}, f32[456,128]{1,0:T(8,128)S(1)}, f32[456,128]{1,0:T(8,128)S(1)}) custom-call(bf16[2304,48]{1,0:T(8,128)(2,1)S(1)} %get-tuple-element.33.refs_0_.pieces, f32[8,256]{1,0:T(8,128)S(1)} %get-tuple-element.47.refs_0_, bf16[8,9216]{1,0:T(8,128)(2,1)S(1)} %collective-permute-done.8.refs_1_, ...), custom_call_target="tpu_custom_call" | custom-call | flops 1048576 | bytes 65536 | tf_op jit(solution)/shard_map/numerators/pallas_call | solution.py:362
  34.7 2.5 %collective-permute-start.13 = (f16[456,128]{1,0:T(8,128)(2,1)S(1)}, f16[456,128]{1,0:T(8,128)(2,1)S(1)}, u32[]{:S(2)}, u32[]{:S(2)}) collective-permute-start(f16[456,128]{1,0:T(8,128)(2,1)S(1)} %convert_element_type.58), channel_id=1, source_target_pairs={{0,24},{8,16},{16,8},{24,0},{1,25},{9,17},{17,9},{25,1},{2,26},{10... | collective-permute-start | bytes 350216 | tf_op jit(solution)/shard_map/ppermute | solution.py:49
  37.2 0.5 %collective-permute-start.12 = (f16[456,128]{1,0:T(8,128)(2,1)S(1)}, f16[456,128]{1,0:T(8,128)(2,1)S(1)}, u32[]{:S(2)}, u32[]{:S(2)}) collective-permute-start(f16[456,128]{1,0:T(8,128)(2,1)S(1)} %convert_element_type.56), channel_id=1, source_target_pairs={{0,16},{8,24},{16,0},{24,8},{1,17},{9,25},{17,1},{25,9},{2,18},{10... | collective-permute-start | bytes 350216 | tf_op jit(solution)/shard_map/ppermute | solution.py:49
  37.7 0.5 %collective-permute-start.11 = (f16[456,128]{1,0:T(8,128)(2,1)S(1)}, f16[456,128]{1,0:T(8,128)(2,1)S(1)}, u32[]{:S(2)}, u32[]{:S(2)}) collective-permute-start(f16[456,128]{1,0:T(8,128)(2,1)S(1)} %convert_element_type.54), channel_id=1, source_target_pairs={{0,8},{8,0},{16,24},{24,16},{1,9},{9,1},{17,25},{25,17},{2,10},{10... | collective-permute-start | bytes 350216 | tf_op jit(solution)/shard_map/ppermute | solution.py:49
  38.3 0.1 convert_add_fusion.1.refs_0_
  38.4 2.7 %denominators.1.denom = f32[56,2304]{1,0:T(8,128)S(1)} custom-call(bf16[2304,256]{1,0:T(8,128)(2,1)S(1)} %get-tuple-element.32.weights, f32[8,128]{1,0:T(8,128)S(1)} %slice.12.refs_0_, f32[8,128]{1,0:T(8,128)S(1)} %slice_convert_fusion.2.refs_1_, f32[8,128]{1,0:T(8,128)S(1)} %slice_convert_fusion.1.refs_2_, f32[8,128]{1,0:T(8,128)S(1)} %slice_convert_fusion.refs_3_), custom_call_target="tpu_custom_call" | custom-call | flops 1048576 | bytes 65536 | tf_op jit(solution)/shard_map/denominators/pallas_call | solution.py:415
  41.1 0.1 collective-permute-done.13
  41.2 1.2 %collective-permute-done.12 = f16[456,128]{1,0:T(8,128)(2,1)S(1)} collective-permute-done((f16[456,128]{1,0:T(8,128)(2,1)S(1)}, f16[456,128]{1,0:T(8,128)(2,1)S(1)}, u32[]{:S(2)}, u32[]{:S(2)}) %collective-permute-start.12) | collective-permute-done | bytes 116768 | tf_op jit(solution)/shard_map/ppermute | solution.py:49
  42.4 0.1 collective-permute-done.11
  42.5 0.1 convert_add_fusion.refs_1_
  42.6 0.9 %averages.1 = f32[50,2304]{1,0:T(8,128)} custom-call(f32[56,2304]{1,0:T(8,128)S(1)} %denominators.1.denom, f32[456,128]{1,0:T(8,128)S(1)} %convert_add_fusion.1.refs_0_, f32[456,128]{1,0:T(8,128)S(1)} %convert_add_fusion.refs_1_), custom_call_target="tpu_custom_call" | custom-call | flops 1048576 | bytes 65536 | tf_op jit(solution)/shard_map/averages/pallas_call | solution.py:437
  (22 shorter events, 0.2 us)
Async XLA Ops:
  0.7 1.3 %copy-start = (bf16[32,18432]{1,0:T(8,128)(2,1)S(1)}, bf16[32,18432]{1,0:T(8,128)(2,1)}, u32[]{:S(2)}) copy-start(bf16[32,18432]{1,0:T(8,128)(2,1)} %img.1) | copy-start | bytes 3538948
  2.0 7.5 %copy-start.1 = (f32[16,18432]{1,0:T(8,128)S(1)}, f32[16,18432]{1,0:T(8,128)}, u32[]{:S(2)}) copy-start(f32[16,18432]{1,0:T(8,128)} %table.1) | copy-start | bytes 3538948
  2.1 1.7 %collective-permute-start = (bf16[4,8,4736]{2,1,0:T(8,128)(2,1)S(1)}, bf16[4,8,4736]{2,1,0:T(8,128)(2,1)S(1)}, u32[]{:S(2)}, u32[]{:S(2)}) collective-permute-start(bf16[4,8,4736]{2,1,0:T(8,128)(2,1)S(1)} %get-tuple-element.35), channel_id=1, source_target_pairs={{0,1},{1,0},{2,3},{3,2},{4,5},{5,4},{6,7},{7,6},{8,9},{9,8},{10,11... | collective-permute-start | bytes 909320 | tf_op jit(solution)/shard_map/ppermute | solution.py:49
  2.6 8.1 %collective-permute-start.4 = (bf16[4,8,4608]{2,1,0:T(8,128)(2,1)S(1)}, bf16[4,8,4608]{2,1,0:T(8,128)(2,1)S(1)}, u32[]{:S(2)}, u32[]{:S(2)}) collective-permute-start(bf16[4,8,4608]{2,1,0:T(8,128)(2,1)S(1)} %get-tuple-element.41), channel_id=1, source_target_pairs={{0,1},{1,0},{2,3},{3,2},{4,5},{5,4},{6,7},{7,6},{8,9},{9,8},{10,11... | collective-permute-start | bytes 884744 | tf_op jit(solution)/shard_map/ppermute | solution.py:49
  3.9 11.3 %collective-permute-start.1 = (bf16[8,9472]{1,0:T(8,128)(2,1)S(1)}, bf16[8,9472]{1,0:T(8,128)(2,1)S(1)}, u32[]{:S(2)}, u32[]{:S(2)}) collective-permute-start(bf16[8,9472]{1,0:T(8,128)(2,1)S(1)} %get-tuple-element.37), channel_id=1, source_target_pairs={{0,2},{1,3},{2,0},{3,1},{4,6},{5,7},{6,4},{7,5},{8,10},{9,11},{10,... | collective-permute-start | bytes 454664 | tf_op jit(solution)/shard_map/ppermute | solution.py:49
  6.9 14.3 %collective-permute-start.2 = (bf16[8,9472]{1,0:T(8,128)(2,1)S(1)}, bf16[8,9472]{1,0:T(8,128)(2,1)S(1)}, u32[]{:S(2)}, u32[]{:S(2)}) collective-permute-start(bf16[8,9472]{1,0:T(8,128)(2,1)S(1)} %get-tuple-element.38), channel_id=1, source_target_pairs={{0,4},{1,5},{2,6},{3,7},{4,0},{5,1},{6,2},{7,3},{8,12},{9,13},{10,... | collective-permute-start | bytes 454664 | tf_op jit(solution)/shard_map/ppermute | solution.py:49
  9.5 11.7 %collective-permute-start.3 = (bf16[8,9472]{1,0:T(8,128)(2,1)S(1)}, bf16[8,9472]{1,0:T(8,128)(2,1)S(1)}, u32[]{:S(2)}, u32[]{:S(2)}) collective-permute-start(bf16[8,9472]{1,0:T(8,128)(2,1)S(1)} %get-tuple-element.39), channel_id=1, source_target_pairs={{0,6},{1,7},{2,4},{3,5},{4,2},{5,3},{6,0},{7,1},{8,14},{9,15},{10,... | collective-permute-start | bytes 454664 | tf_op jit(solution)/shard_map/ppermute | solution.py:49
  10.7 14.8 %collective-permute-start.10 = (bf16[8,9216]{1,0:T(8,128)(2,1)S(1)}, bf16[8,9216]{1,0:T(8,128)(2,1)S(1)}, u32[]{:S(2)}, u32[]{:S(2)}) collective-permute-start(bf16[8,9216]{1,0:T(8,128)(2,1)S(1)} %get-tuple-element.50), channel_id=1, source_target_pairs={{0,2},{1,3},{2,0},{3,1},{4,6},{5,7},{6,4},{7,5},{8,10},{9,11},{10,... | collective-permute-start | bytes 442376 | tf_op jit(solution)/shard_map/ppermute | solution.py:49
  11.7 22.2 %collective-permute-start.8 = (bf16[8,9216]{1,0:T(8,128)(2,1)S(1)}, bf16[8,9216]{1,0:T(8,128)(2,1)S(1)}, u32[]{:S(2)}, u32[]{:S(2)}) collective-permute-start(bf16[8,9216]{1,0:T(8,128)(2,1)S(1)} %get-tuple-element.48), channel_id=1, source_target_pairs={{0,4},{1,5},{2,6},{3,7},{4,0},{5,1},{6,2},{7,3},{8,12},{9,13},{10,... | collective-permute-start | bytes 442376 | tf_op jit(solution)/shard_map/ppermute | solution.py:49
  15.2 18.7 %collective-permute-start.9 = (bf16[8,9216]{1,0:T(8,128)(2,1)S(1)}, bf16[8,9216]{1,0:T(8,128)(2,1)S(1)}, u32[]{:S(2)}, u32[]{:S(2)}) collective-permute-start(bf16[8,9216]{1,0:T(8,128)(2,1)S(1)} %get-tuple-element.49), channel_id=1, source_target_pairs={{0,6},{1,7},{2,4},{3,5},{4,2},{5,3},{6,0},{7,1},{8,14},{9,15},{10,... | collective-permute-start | bytes 442376 | tf_op jit(solution)/shard_map/ppermute | solution.py:49
  22.4 15.3 %collective-permute-start.7 = (f16[456,128]{1,0:T(8,128)(2,1)S(1)}, f16[456,128]{1,0:T(8,128)(2,1)S(1)}, u32[]{:S(2)}, u32[]{:S(2)}) collective-permute-start(f16[456,128]{1,0:T(8,128)(2,1)S(1)} %convert_element_type.49), channel_id=1, source_target_pairs={{0,24},{8,16},{16,8},{24,0},{1,25},{9,17},{17,9},{25,1},{2,26},{10... | collective-permute-start | bytes 350216 | tf_op jit(solution)/shard_map/ppermute | solution.py:49
  25.0 13.3 %collective-permute-start.6 = (f16[456,128]{1,0:T(8,128)(2,1)S(1)}, f16[456,128]{1,0:T(8,128)(2,1)S(1)}, u32[]{:S(2)}, u32[]{:S(2)}) collective-permute-start(f16[456,128]{1,0:T(8,128)(2,1)S(1)} %convert_element_type.47), channel_id=1, source_target_pairs={{0,16},{8,24},{16,0},{24,8},{1,17},{9,25},{17,1},{25,9},{2,18},{10... | collective-permute-start | bytes 350216 | tf_op jit(solution)/shard_map/ppermute | solution.py:49
  25.6 12.7 %collective-permute-start.5 = (f16[456,128]{1,0:T(8,128)(2,1)S(1)}, f16[456,128]{1,0:T(8,128)(2,1)S(1)}, u32[]{:S(2)}, u32[]{:S(2)}) collective-permute-start(f16[456,128]{1,0:T(8,128)(2,1)S(1)} %convert_element_type.45), channel_id=1, source_target_pairs={{0,8},{8,0},{16,24},{24,16},{1,9},{9,1},{17,25},{25,17},{2,10},{10... | collective-permute-start | bytes 350216 | tf_op jit(solution)/shard_map/ppermute | solution.py:49
  34.7 6.5 %collective-permute-start.13 = (f16[456,128]{1,0:T(8,128)(2,1)S(1)}, f16[456,128]{1,0:T(8,128)(2,1)S(1)}, u32[]{:S(2)}, u32[]{:S(2)}) collective-permute-start(f16[456,128]{1,0:T(8,128)(2,1)S(1)} %convert_element_type.58), channel_id=1, source_target_pairs={{0,24},{8,16},{16,8},{24,0},{1,25},{9,17},{17,9},{25,1},{2,26},{10... | collective-permute-start | bytes 350216 | tf_op jit(solution)/shard_map/ppermute | solution.py:49
  37.2 5.2 %collective-permute-start.12 = (f16[456,128]{1,0:T(8,128)(2,1)S(1)}, f16[456,128]{1,0:T(8,128)(2,1)S(1)}, u32[]{:S(2)}, u32[]{:S(2)}) collective-permute-start(f16[456,128]{1,0:T(8,128)(2,1)S(1)} %convert_element_type.56), channel_id=1, source_target_pairs={{0,16},{8,24},{16,0},{24,8},{1,17},{9,25},{17,1},{25,9},{2,18},{10... | collective-permute-start | bytes 350216 | tf_op jit(solution)/shard_map/ppermute | solution.py:49
  37.7 4.8 %collective-permute-start.11 = (f16[456,128]{1,0:T(8,128)(2,1)S(1)}, f16[456,128]{1,0:T(8,128)(2,1)S(1)}, u32[]{:S(2)}, u32[]{:S(2)}) collective-permute-start(f16[456,128]{1,0:T(8,128)(2,1)S(1)} %convert_element_type.54), channel_id=1, source_target_pairs={{0,8},{8,0},{16,24},{24,16},{1,9},{9,1},{17,25},{25,17},{2,10},{10... | collective-permute-start | bytes 350216 | tf_op jit(solution)/shard_map/ppermute | solution.py:49

commit v8 on v7

--- a/solution.py
+++ b/solution.py
@@ -252,6 +252,8 @@
     own = lax.axis_index("grp")
     if not first:
         tags = refs.pop(0)
+    elif added:
+        earlier = refs.pop(0)
     for chunk, wide, src, dst, width in segments:
         across = pl.ds(dst * LANES, width * LANES)
         taken = steps[1] - steps[0]
@@ -282,7 +284,7 @@
             tags[:, pl.ds(tile * LANES, LANES)] = total
     sums = refs[:grp]
     data, product, parts = refs[grp:]
-    label = tags[:, pl.ds(steps[0] * CORES * count, lanes)].astype(jnp.int32)
+    label = tags[...].astype(jnp.int32)
     key = label[0:1] * CPAD + label[1:2]
     spot = label[2:3]
     turn = label[3:4]
@@ -329,12 +331,15 @@
             here = (pl.ds(tile * CPG, CPG), pl.ds(0, width))
             value = result[step * CPAD : step * CPAD + CPG, tile * LANES : tile * LANES + width]
             sums[step][here] = value + partial[step][here] if partial else value
-        if first:
+        if first and steps[1] == mem // CORES:
+            every = label
+            if added:
+                every = jnp.concatenate([earlier[...].astype(jnp.int32), label], axis=1)
             target = partner(own, step, grp)
-            local = jnp.where(label[0:1] == target, label[1:2], -1)
+            local = jnp.where(every[0:1] == target, every[1:2], -1)
             row = CPG * len(stacked(result.shape[1]))
-            for kind in (local, spot, turn):
-                for tile in range(lanes // LANES):
+            for kind in (local, every[2:3], every[3:4]):
+                for tile in range(every.shape[1] // LANES):
                     value = kind[:, tile * LANES : (tile + 1) * LANES].astype(F32)
                     sums[step][pl.ds(row, 1), :] = value
                     row += 1
@@ -356,9 +361,9 @@
     span = (here[1] - here[0]) * ANGLES
     tiles = stop - base
     shapes = [jax.ShapeDtypeStruct((ROWS, lanes), F32)] if first else []
-    tall = sum_rows(span, lanes if first else 0)
+    tall = sum_rows(span, mem * count if first else 0)
     shapes += [jax.ShapeDtypeStruct((tall, LANES), F32)] * grp
-    operands = [pieces] + ([] if first else [tags]) + msgs + list(partial)
+    operands = [pieces] + ([] if tags is None else [tags]) + msgs + list(partial)
     outs = pl.pallas_call(
         functools.partial(
             numer_kernel, mem, count, first, here, base, tiles, tuple(segments), steps, len(partial),
@@ -475,17 +480,19 @@
         arrived.append([here[step] for step in range(places)])
         after = [pieces]
         ties = [msgs[0]] if len(arrived) > 1 else []
-    tags, sums, blocks = None, [], []
+    tags, sums, blocks = [], [], []
     for chunk in range(len(edges) - 1):
         cuts = [0, places]
-        if chunk > 0 and places // 2 * CORES * count % LANES == 0:
+        if places // 2 * CORES * count % LANES == 0:
             cuts = [0, places // 2, places]
-        here = ()
-        for steps in zip(cuts, cuts[1:]):
-            tie = [] if chunk else ties
-            tags, here = numerators(
-                count, pieces, tags, arrived, chunk, edges, rows, steps, here, tie
+        here, last = (), None
+        for part, steps in enumerate(zip(cuts, cuts[1:])):
+            known, tie = (tags[part], []) if chunk else (last, ties)
+            last, here = numerators(
+                count, pieces, known, arrived, chunk, edges, rows, steps, here, tie
             )
+            if chunk == 0:
+                tags.append(last)
         others = [send(here[step].astype(HALF), "grp", step) for step in range(1, grp)]
         if chunk == 0:
             blocks = [tag_block(part, rows[1] * ANGLES) for part in [here[0]] + others]

time: 43.7 us -> 43.7 us (level)
    pallas_call x3 -> x4, Pallas kernels: 2.73 us -> 2.98 us  [numerators(): pl.pallas_call(functools.partial(numer_kernel, mem, count, first, here, b...]
  transfers between devices with their start and end apart: 14 -> 14, of which waited for: 6 -> 6; matrix products, arithmetic and copies ran while one was open for 0% -> 0% of each run, Pallas kernels for 15% -> 16%
where the time goes in v8:
time: 43.7 us; the launch traced here: 43.5 us
  starting transfers between devices  19.9 us (46%)
  waiting for transfers between devices  13.3 us (30%)
  Pallas kernels  8.01 us (18%)
  local copies, waits for them, and re-layouts  1.28 us (3%)
  other arithmetic  0.95 us (2%)
    ppermute x14, starting transfers between devices, send(): return lax.ppermute(value, axis, pairs)  19.9 us
    ppermute x14, waiting for transfers between devices, send(): return lax.ppermute(value, axis, pairs)  13.3 us
    pallas_call x4, Pallas kernels, numerators(): pl.pallas_call(functools.partial(numer_kernel, mem, count, first, here, b...  2.98 us
    pallas_call x1, Pallas kernels, denominators(): pl.pallas_call(functools.partial(denom_kernel, first, lanes), out_shape=j...  2.75 us
    unnamed x4, local copies, waits for them, and re-layouts  1.27 us
    pallas_call x1, Pallas kernels, tables(): pl.pallas_call(functools.partial(table_kernel, turns), out_shape=[jax.Sha...  1.18 us
    pallas_call x1, Pallas kernels, averages(): pl.pallas_call(functools.partial(average_kernel, rows), out_shape=jax.Sha...  0.89 us
  transfers between devices with their start and end apart: 14, of which 6 were waited for; matrix products, arithmetic and copies ran while one was open for 0% of the time, Pallas kernels for 16%

profile of v8, /device:TPU:0, one launch (start us, length us, event | category | flops | bytes accessed | tf_op | source)
XLA Modules:
  0.0 43.5 jit_solution(10425624942060274860)
XLA Ops:
  0.0 0.7 %pad_add_fusion.labels = s32[3,32]{1,0:T(4,128)S(1)} fusion(s32[1,32]{1,0:T(1,128)} %bitcast.3, s32[1,32]{1,0:T(1,128)} %bitcast.4, s32[1,32]{1,0:T(1,128)} %bitcast.5), kind=kLoop, calls=%fused_computation.5 | loop fusion | flops 192 | bytes 768 | tf_op jit(solution)/shard_map/stack | solution.py:474
  0.7 1.3 %copy-done = bf16[32,18432]{1,0:T(8,128)(2,1)S(1)} copy-done((bf16[32,18432]{1,0:T(8,128)(2,1)S(1)}, bf16[32,18432]{1,0:T(8,128)(2,1)}, u32[]{:S(2)}) %copy-start) | copy-done | bytes 1179672
  2.0 0.1 pack.1
  2.1 0.5 %collective-permute-start = (bf16[4,8,4736]{2,1,0:T(8,128)(2,1)S(1)}, bf16[4,8,4736]{2,1,0:T(8,128)(2,1)S(1)}, u32[]{:S(2)}, u32[]{:S(2)}) collective-permute-start(bf16[4,8,4736]{2,1,0:T(8,128)(2,1)S(1)} %get-tuple-element.40), channel_id=1, source_target_pairs={{0,1},{1,0},{2,3},{3,2},{4,5},{5,4},{6,7},{7,6},{8,9},{9,8},{10,11... | collective-permute-start | bytes 909320 | tf_op jit(solution)/shard_map/ppermute | solution.py:49
  2.6 0.1 collective-permute-start.2
  2.7 1.1 %collective-permute-done.crossed = bf16[4,8,4736]{2,1,0:T(8,128)(2,1)S(1)} collective-permute-done((bf16[4,8,4736]{2,1,0:T(8,128)(2,1)S(1)}, bf16[4,8,4736]{2,1,0:T(8,128)(2,1)S(1)}, u32[]{:S(2)}, u32[]{:S(2)}) %collective-permute-start) | collective-permute-done | bytes 303136 | tf_op jit(solution)/shard_map/ppermute | solution.py:49
  3.9 3.0 %collective-permute-start.1 = (bf16[8,9472]{1,0:T(8,128)(2,1)S(1)}, bf16[8,9472]{1,0:T(8,128)(2,1)S(1)}, u32[]{:S(2)}, u32[]{:S(2)}) collective-permute-start(bf16[8,9472]{1,0:T(8,128)(2,1)S(1)} %get-tuple-element.42), channel_id=1, source_target_pairs={{0,2},{1,3},{2,0},{3,1},{4,6},{5,7},{6,4},{7,5},{8,10},{9,11},{10,... | collective-permute-start | bytes 454664 | tf_op jit(solution)/shard_map/ppermute | solution.py:49
  6.9 2.6 %collective-permute-start.3 = (bf16[8,9472]{1,0:T(8,128)(2,1)S(1)}, bf16[8,9472]{1,0:T(8,128)(2,1)S(1)}, u32[]{:S(2)}, u32[]{:S(2)}) collective-permute-start(bf16[8,9472]{1,0:T(8,128)(2,1)S(1)} %get-tuple-element.47), channel_id=1, source_target_pairs={{0,4},{1,5},{2,6},{3,7},{4,0},{5,1},{6,2},{7,3},{8,12},{9,13},{10,... | collective-permute-start | bytes 454664 | tf_op jit(solution)/shard_map/ppermute | solution.py:49
  9.5 0.0 collective-permute-start.4
  9.5 1.2 %tables.1 = (bf16[2304,48]{1,0:T(8,128)(2,1)S(1)}, bf16[2304,256]{1,0:T(8,128)(2,1)S(1)}) custom-call(f32[16,18432]{1,0:T(8,128)S(1)} %copy-done.1), custom_call_target="tpu_custom_call" | custom-call | flops 1048576 | bytes 65536 | tf_op jit(solution)/shard_map/tables/pallas_call | solution.py:205
  10.7 1.0 %collective-permute-start.10 = (bf16[8,9216]{1,0:T(8,128)(2,1)S(1)}, bf16[8,9216]{1,0:T(8,128)(2,1)S(1)}, u32[]{:S(2)}, u32[]{:S(2)}) collective-permute-start(bf16[8,9216]{1,0:T(8,128)(2,1)S(1)} %get-tuple-element.60), channel_id=1, source_target_pairs={{0,2},{1,3},{2,0},{3,1},{4,6},{5,7},{6,4},{7,5},{8,10},{9,11},{10,... | collective-permute-start | bytes 442376 | tf_op jit(solution)/shard_map/ppermute | solution.py:49
  11.7 3.5 %collective-permute-start.8 = (bf16[8,9216]{1,0:T(8,128)(2,1)S(1)}, bf16[8,9216]{1,0:T(8,128)(2,1)S(1)}, u32[]{:S(2)}, u32[]{:S(2)}) collective-permute-start(bf16[8,9216]{1,0:T(8,128)(2,1)S(1)} %get-tuple-element.58), channel_id=1, source_target_pairs={{0,4},{1,5},{2,6},{3,7},{4,0},{5,1},{6,2},{7,3},{8,12},{9,13},{10,... | collective-permute-start | bytes 442376 | tf_op jit(solution)/shard_map/ppermute | solution.py:49
  15.2 2.1 %collective-permute-start.9 = (bf16[8,9216]{1,0:T(8,128)(2,1)S(1)}, bf16[8,9216]{1,0:T(8,128)(2,1)S(1)}, u32[]{:S(2)}, u32[]{:S(2)}) collective-permute-start(bf16[8,9216]{1,0:T(8,128)(2,1)S(1)} %get-tuple-element.59), channel_id=1, source_target_pairs={{0,6},{1,7},{2,4},{3,5},{4,2},{5,3},{6,0},{7,1},{8,14},{9,15},{10,... | collective-permute-start | bytes 442376 | tf_op jit(solution)/shard_map/ppermute | solution.py:49
  17.2 0.7 %numerators.4 = (f32[8,128]{1,0:T(8,128)S(1)}, f32[456,128]{1,0:T(8,128)S(1)}, f32[456,128]{1,0:T(8,128)S(1)}, f32[456,128]{1,0:T(8,128)S(1)}, f32[456,128]{1,0:T(8,128)S(1)}) custom-call(bf16[2304,48]{1,0:T(8,128)(2,1)S(1)} %get-tuple-element.38.refs_0_.pieces, bf16[8,9472]{1,0:T(8,128)(2,1)S(1)} %get-tuple-element.41.refs_0_, ...), custom_call_target="tpu_custom_call" | custom-call | flops 1048576 | bytes 65536 | tf_op jit(solution)/shard_map/numerators/pallas_call | solution.py:367
  18.0 3.2 %collective-permute-done.3.refs_1_ = bf16[8,9472]{1,0:T(8,128)(2,1)S(1)} collective-permute-done((bf16[8,9472]{1,0:T(8,128)(2,1)S(1)}, bf16[8,9472]{1,0:T(8,128)(2,1)S(1)}, u32[]{:S(2)}, u32[]{:S(2)}) %collective-permute-start.3) | collective-permute-done | bytes 151584 | tf_op jit(solution)/shard_map/ppermute | solution.py:49
  21.1 0.8 %numerators.5 = (f32[8,128]{1,0:T(8,128)S(1)}, f32[456,128]{1,0:T(8,128)S(1)}, f32[456,128]{1,0:T(8,128)S(1)}, f32[456,128]{1,0:T(8,128)S(1)}, f32[456,128]{1,0:T(8,128)S(1)}) custom-call(bf16[2304,48]{1,0:T(8,128)(2,1)S(1)} %get-tuple-element.38.refs_0_.pieces, f32[8,128]{1,0:T(8,128)S(1)} %get-tuple-element.46.refs_0_, ...), custom_call_target="tpu_custom_call" | custom-call | flops 1048576 | bytes 65536 | tf_op jit(solution)/shard_map/numerators/pallas_call | solution.py:367
  21.9 2.5 %collective-permute-start.7 = (f16[456,128]{1,0:T(8,128)(2,1)S(1)}, f16[456,128]{1,0:T(8,128)(2,1)S(1)}, u32[]{:S(2)}, u32[]{:S(2)}) collective-permute-start(f16[456,128]{1,0:T(8,128)(2,1)S(1)} %convert_element_type.49), channel_id=1, source_target_pairs={{0,24},{8,16},{16,8},{24,0},{1,25},{9,17},{17,9},{25,1},{2,26},{10... | collective-permute-start | bytes 350216 | tf_op jit(solution)/shard_map/ppermute | solution.py:49
  24.5 0.6 %collective-permute-start.6 = (f16[456,128]{1,0:T(8,128)(2,1)S(1)}, f16[456,128]{1,0:T(8,128)(2,1)S(1)}, u32[]{:S(2)}, u32[]{:S(2)}) collective-permute-start(f16[456,128]{1,0:T(8,128)(2,1)S(1)} %convert_element_type.47), channel_id=1, source_target_pairs={{0,16},{8,24},{16,0},{24,8},{1,17},{9,25},{17,1},{25,9},{2,18},{10... | collective-permute-start | bytes 350216 | tf_op jit(solution)/shard_map/ppermute | solution.py:49
  25.1 0.5 %collective-permute-start.5 = (f16[456,128]{1,0:T(8,128)(2,1)S(1)}, f16[456,128]{1,0:T(8,128)(2,1)S(1)}, u32[]{:S(2)}, u32[]{:S(2)}) collective-permute-start(f16[456,128]{1,0:T(8,128)(2,1)S(1)} %convert_element_type.45), channel_id=1, source_target_pairs={{0,8},{8,0},{16,24},{24,16},{1,9},{9,1},{17,25},{25,17},{2,10},{10... | collective-permute-start | bytes 350216 | tf_op jit(solution)/shard_map/ppermute | solution.py:49
  25.6 0.7 %numerators.6 = (f32[456,128]{1,0:T(8,128)S(1)}, f32[456,128]{1,0:T(8,128)S(1)}, f32[456,128]{1,0:T(8,128)S(1)}, f32[456,128]{1,0:T(8,128)S(1)}) custom-call(bf16[2304,48]{1,0:T(8,128)(2,1)S(1)} %get-tuple-element.38.refs_0_.pieces, f32[8,128]{1,0:T(8,128)S(1)} %get-tuple-element.46.refs_0_, bf16[8,9216]{1,0:T(8,128)(2,1)S(1)} %get-tuple-element.45.refs_2_.refs_7_.refs_1_, ...), custom_call_target="tpu_custom_call" | custom-call | flops 1048576 | bytes 65536 | tf_op jit(solution)/shard_map/numerators/pallas_call | solution.py:367
  26.4 7.5 %collective-permute-done.8.refs_1_ = bf16[8,9216]{1,0:T(8,128)(2,1)S(1)} collective-permute-done((bf16[8,9216]{1,0:T(8,128)(2,1)S(1)}, bf16[8,9216]{1,0:T(8,128)(2,1)S(1)}, u32[]{:S(2)}, u32[]{:S(2)}) %collective-permute-start.8) | collective-permute-done | bytes 147488 | tf_op jit(solution)/shard_map/ppermute | solution.py:49
  33.9 0.7 %numerators.7 = (f32[456,128]{1,0:T(8,128)S(1)}, f32[456,128]{1,0:T(8,128)S(1)}, f32[456,128]{1,0:T(8,128)S(1)}, f32[456,128]{1,0:T(8,128)S(1)}) custom-call(bf16[2304,48]{1,0:T(8,128)(2,1)S(1)} %get-tuple-element.38.refs_0_.pieces, f32[8,128]{1,0:T(8,128)S(1)} %get-tuple-element.57.refs_0_, bf16[8,9216]{1,0:T(8,128)(2,1)S(1)} %collective-permute-done.8.refs_1_, ...), custom_call_target="tpu_custom_call" | custom-call | flops 1048576 | bytes 65536 | tf_op jit(solution)/shard_map/numerators/pallas_call | solution.py:367
  34.7 2.5 %collective-permute-start.13 = (f16[456,128]{1,0:T(8,128)(2,1)S(1)}, f16[456,128]{1,0:T(8,128)(2,1)S(1)}, u32[]{:S(2)}, u32[]{:S(2)}) collective-permute-start(f16[456,128]{1,0:T(8,128)(2,1)S(1)} %convert_element_type.58), channel_id=1, source_target_pairs={{0,24},{8,16},{16,8},{24,0},{1,25},{9,17},{17,9},{25,1},{2,26},{10... | collective-permute-start | bytes 350216 | tf_op jit(solution)/shard_map/ppermute | solution.py:49
  37.2 0.5 %collective-permute-start.12 = (f16[456,128]{1,0:T(8,128)(2,1)S(1)}, f16[456,128]{1,0:T(8,128)(2,1)S(1)}, u32[]{:S(2)}, u32[]{:S(2)}) collective-permute-start(f16[456,128]{1,0:T(8,128)(2,1)S(1)} %convert_element_type.56), channel_id=1, source_target_pairs={{0,16},{8,24},{16,0},{24,8},{1,17},{9,25},{17,1},{25,9},{2,18},{10... | collective-permute-start | bytes 350216 | tf_op jit(solution)/shard_map/ppermute | solution.py:49
  37.7 0.5 %collective-permute-start.11 = (f16[456,128]{1,0:T(8,128)(2,1)S(1)}, f16[456,128]{1,0:T(8,128)(2,1)S(1)}, u32[]{:S(2)}, u32[]{:S(2)}) collective-permute-start(f16[456,128]{1,0:T(8,128)(2,1)S(1)} %convert_element_type.54), channel_id=1, source_target_pairs={{0,8},{8,0},{16,24},{24,16},{1,9},{9,1},{17,25},{25,17},{2,10},{10... | collective-permute-start | bytes 350216 | tf_op jit(solution)/shard_map/ppermute | solution.py:49
  38.3 0.1 convert_add_fusion.1.refs_0_
  38.4 2.7 %denominators.1.denom = f32[56,2304]{1,0:T(8,128)S(1)} custom-call(bf16[2304,256]{1,0:T(8,128)(2,1)S(1)} %get-tuple-element.37.weights, f32[8,128]{1,0:T(8,128)S(1)} %slice.12.refs_0_, f32[8,128]{1,0:T(8,128)S(1)} %slice_convert_fusion.2.refs_1_, f32[8,128]{1,0:T(8,128)S(1)} %slice_convert_fusion.1.refs_2_, f32[8,128]{1,0:T(8,128)S(1)} %slice_convert_fusion.refs_3_), custom_call_target="tpu_custom_call" | custom-call | flops 1048576 | bytes 65536 | tf_op jit(solution)/shard_map/denominators/pallas_call | solution.py:420
  41.1 0.1 collective-permute-done.13
  41.2 1.2 %collective-permute-done.12 = f16[456,128]{1,0:T(8,128)(2,1)S(1)} collective-permute-done((f16[456,128]{1,0:T(8,128)(2,1)S(1)}, f16[456,128]{1,0:T(8,128)(2,1)S(1)}, u32[]{:S(2)}, u32[]{:S(2)}) %collective-permute-start.12) | collective-permute-done | bytes 116768 | tf_op jit(solution)/shard_map/ppermute | solution.py:49
  42.4 0.1 collective-permute-done.11
  42.5 0.1 convert_add_fusion.refs_1_
  42.6 0.9 %averages.1 = f32[50,2304]{1,0:T(8,128)} custom-call(f32[56,2304]{1,0:T(8,128)S(1)} %denominators.1.denom, f32[456,128]{1,0:T(8,128)S(1)} %convert_add_fusion.1.refs_0_, f32[456,128]{1,0:T(8,128)S(1)} %convert_add_fusion.refs_1_), custom_call_target="tpu_custom_call" | custom-call | flops 1048576 | bytes 65536 | tf_op jit(solution)/shard_map/averages/pallas_call | solution.py:442
  (23 shorter events, 0.2 us)
Async XLA Ops:
  0.7 1.3 %copy-start = (bf16[32,18432]{1,0:T(8,128)(2,1)S(1)}, bf16[32,18432]{1,0:T(8,128)(2,1)}, u32[]{:S(2)}) copy-start(bf16[32,18432]{1,0:T(8,128)(2,1)} %img.1) | copy-start | bytes 3538948
  2.0 7.5 %copy-start.1 = (f32[16,18432]{1,0:T(8,128)S(1)}, f32[16,18432]{1,0:T(8,128)}, u32[]{:S(2)}) copy-start(f32[16,18432]{1,0:T(8,128)} %table.1) | copy-start | bytes 3538948
  2.1 1.7 %collective-permute-start = (bf16[4,8,4736]{2,1,0:T(8,128)(2,1)S(1)}, bf16[4,8,4736]{2,1,0:T(8,128)(2,1)S(1)}, u32[]{:S(2)}, u32[]{:S(2)}) collective-permute-start(bf16[4,8,4736]{2,1,0:T(8,128)(2,1)S(1)} %get-tuple-element.40), channel_id=1, source_target_pairs={{0,1},{1,0},{2,3},{3,2},{4,5},{5,4},{6,7},{7,6},{8,9},{9,8},{10,11... | collective-permute-start | bytes 909320 | tf_op jit(solution)/shard_map/ppermute | solution.py:49
  2.6 8.1 %collective-permute-start.2 = (bf16[4,8,4608]{2,1,0:T(8,128)(2,1)S(1)}, bf16[4,8,4608]{2,1,0:T(8,128)(2,1)S(1)}, u32[]{:S(2)}, u32[]{:S(2)}) collective-permute-start(bf16[4,8,4608]{2,1,0:T(8,128)(2,1)S(1)} %get-tuple-element.44), channel_id=1, source_target_pairs={{0,1},{1,0},{2,3},{3,2},{4,5},{5,4},{6,7},{7,6},{8,9},{9,8},{10,11... | collective-permute-start | bytes 884744 | tf_op jit(solution)/shard_map/ppermute | solution.py:49
  3.9 11.3 %collective-permute-start.1 = (bf16[8,9472]{1,0:T(8,128)(2,1)S(1)}, bf16[8,9472]{1,0:T(8,128)(2,1)S(1)}, u32[]{:S(2)}, u32[]{:S(2)}) collective-permute-start(bf16[8,9472]{1,0:T(8,128)(2,1)S(1)} %get-tuple-element.42), channel_id=1, source_target_pairs={{0,2},{1,3},{2,0},{3,1},{4,6},{5,7},{6,4},{7,5},{8,10},{9,11},{10,... | collective-permute-start | bytes 454664 | tf_op jit(solution)/shard_map/ppermute | solution.py:49
  6.9 14.3 %collective-permute-start.3 = (bf16[8,9472]{1,0:T(8,128)(2,1)S(1)}, bf16[8,9472]{1,0:T(8,128)(2,1)S(1)}, u32[]{:S(2)}, u32[]{:S(2)}) collective-permute-start(bf16[8,9472]{1,0:T(8,128)(2,1)S(1)} %get-tuple-element.47), channel_id=1, source_target_pairs={{0,4},{1,5},{2,6},{3,7},{4,0},{5,1},{6,2},{7,3},{8,12},{9,13},{10,... | collective-permute-start | bytes 454664 | tf_op jit(solution)/shard_map/ppermute | solution.py:49
  9.5 11.7 %collective-permute-start.4 = (bf16[8,9472]{1,0:T(8,128)(2,1)S(1)}, bf16[8,9472]{1,0:T(8,128)(2,1)S(1)}, u32[]{:S(2)}, u32[]{:S(2)}) collective-permute-start(bf16[8,9472]{1,0:T(8,128)(2,1)S(1)} %get-tuple-element.48), channel_id=1, source_target_pairs={{0,6},{1,7},{2,4},{3,5},{4,2},{5,3},{6,0},{7,1},{8,14},{9,15},{10,... | collective-permute-start | bytes 454664 | tf_op jit(solution)/shard_map/ppermute | solution.py:49
  10.7 14.4 %collective-permute-start.10 = (bf16[8,9216]{1,0:T(8,128)(2,1)S(1)}, bf16[8,9216]{1,0:T(8,128)(2,1)S(1)}, u32[]{:S(2)}, u32[]{:S(2)}) collective-permute-start(bf16[8,9216]{1,0:T(8,128)(2,1)S(1)} %get-tuple-element.60), channel_id=1, source_target_pairs={{0,2},{1,3},{2,0},{3,1},{4,6},{5,7},{6,4},{7,5},{8,10},{9,11},{10,... | collective-permute-start | bytes 442376 | tf_op jit(solution)/shard_map/ppermute | solution.py:49
  11.7 22.2 %collective-permute-start.8 = (bf16[8,9216]{1,0:T(8,128)(2,1)S(1)}, bf16[8,9216]{1,0:T(8,128)(2,1)S(1)}, u32[]{:S(2)}, u32[]{:S(2)}) collective-permute-start(bf16[8,9216]{1,0:T(8,128)(2,1)S(1)} %get-tuple-element.58), channel_id=1, source_target_pairs={{0,4},{1,5},{2,6},{3,7},{4,0},{5,1},{6,2},{7,3},{8,12},{9,13},{10,... | collective-permute-start | bytes 442376 | tf_op jit(solution)/shard_map/ppermute | solution.py:49
  15.2 18.7 %collective-permute-start.9 = (bf16[8,9216]{1,0:T(8,128)(2,1)S(1)}, bf16[8,9216]{1,0:T(8,128)(2,1)S(1)}, u32[]{:S(2)}, u32[]{:S(2)}) collective-permute-start(bf16[8,9216]{1,0:T(8,128)(2,1)S(1)} %get-tuple-element.59), channel_id=1, source_target_pairs={{0,6},{1,7},{2,4},{3,5},{4,2},{5,3},{6,0},{7,1},{8,14},{9,15},{10,... | collective-permute-start | bytes 442376 | tf_op jit(solution)/shard_map/ppermute | solution.py:49
  21.9 15.8 %collective-permute-start.7 = (f16[456,128]{1,0:T(8,128)(2,1)S(1)}, f16[456,128]{1,0:T(8,128)(2,1)S(1)}, u32[]{:S(2)}, u32[]{:S(2)}) collective-permute-start(f16[456,128]{1,0:T(8,128)(2,1)S(1)} %convert_element_type.49), channel_id=1, source_target_pairs={{0,24},{8,16},{16,8},{24,0},{1,25},{9,17},{17,9},{25,1},{2,26},{10... | collective-permute-start | bytes 350216 | tf_op jit(solution)/shard_map/ppermute | solution.py:49
  24.5 13.8 %collective-permute-start.6 = (f16[456,128]{1,0:T(8,128)(2,1)S(1)}, f16[456,128]{1,0:T(8,128)(2,1)S(1)}, u32[]{:S(2)}, u32[]{:S(2)}) collective-permute-start(f16[456,128]{1,0:T(8,128)(2,1)S(1)} %convert_element_type.47), channel_id=1, source_target_pairs={{0,16},{8,24},{16,0},{24,8},{1,17},{9,25},{17,1},{25,9},{2,18},{10... | collective-permute-start | bytes 350216 | tf_op jit(solution)/shard_map/ppermute | solution.py:49
  25.1 13.2 %collective-permute-start.5 = (f16[456,128]{1,0:T(8,128)(2,1)S(1)}, f16[456,128]{1,0:T(8,128)(2,1)S(1)}, u32[]{:S(2)}, u32[]{:S(2)}) collective-permute-start(f16[456,128]{1,0:T(8,128)(2,1)S(1)} %convert_element_type.45), channel_id=1, source_target_pairs={{0,8},{8,0},{16,24},{24,16},{1,9},{9,1},{17,25},{25,17},{2,10},{10... | collective-permute-start | bytes 350216 | tf_op jit(solution)/shard_map/ppermute | solution.py:49
  34.7 6.5 %collective-permute-start.13 = (f16[456,128]{1,0:T(8,128)(2,1)S(1)}, f16[456,128]{1,0:T(8,128)(2,1)S(1)}, u32[]{:S(2)}, u32[]{:S(2)}) collective-permute-start(f16[456,128]{1,0:T(8,128)(2,1)S(1)} %convert_element_type.58), channel_id=1, source_target_pairs={{0,24},{8,16},{16,8},{24,0},{1,25},{9,17},{17,9},{25,1},{2,26},{10... | collective-permute-start | bytes 350216 | tf_op jit(solution)/shard_map/ppermute | solution.py:49
  37.2 5.2 %collective-permute-start.12 = (f16[456,128]{1,0:T(8,128)(2,1)S(1)}, f16[456,128]{1,0:T(8,128)(2,1)S(1)}, u32[]{:S(2)}, u32[]{:S(2)}) collective-permute-start(f16[456,128]{1,0:T(8,128)(2,1)S(1)} %convert_element_type.56), channel_id=1, source_target_pairs={{0,16},{8,24},{16,0},{24,8},{1,17},{9,25},{17,1},{25,9},{2,18},{10... | collective-permute-start | bytes 350216 | tf_op jit(solution)/shard_map/ppermute | solution.py:49
  37.7 4.8 %collective-permute-start.11 = (f16[456,128]{1,0:T(8,128)(2,1)S(1)}, f16[456,128]{1,0:T(8,128)(2,1)S(1)}, u32[]{:S(2)}, u32[]{:S(2)}) collective-permute-start(f16[456,128]{1,0:T(8,128)(2,1)S(1)} %convert_element_type.54), channel_id=1, source_target_pairs={{0,8},{8,0},{16,24},{24,16},{1,9},{9,1},{17,25},{25,17},{2,10},{10... | collective-permute-start | bytes 350216 | tf_op jit(solution)/shard_map/ppermute | solution.py:49

commit v9 on v7

--- a/solution.py
+++ b/solution.py
@@ -424,12 +424,18 @@
 
 
 def average_kernel(rows, denom, *refs):
-    sums, out = refs[:-1], refs[-1]
+    *sums, final, out, sems = refs
+    copies = []
     for chunk in range(len(rows) - 1):
         for tile, width in stacked((rows[chunk + 1] - rows[chunk]) * ANGLES):
             across = pl.ds(rows[chunk] * ANGLES + tile * LANES, width)
             total = sums[chunk][pl.ds(tile * CPG, CPG), pl.ds(0, width)]
             out[:, across] = total / (denom[:CPG, across] + wiener_term)
+        across = pl.ds(rows[chunk] * ANGLES, (rows[chunk + 1] - rows[chunk]) * ANGLES)
+        copies.append(pltpu.make_async_copy(out.at[:, across], final.at[:, across], sems.at[chunk]))
+        copies[-1].start()
+    for copy in copies:
+        copy.wait()
 
 
 def averages(denom, sums, rows):
@@ -438,7 +444,11 @@
         functools.partial(average_kernel, rows),
         out_shape=jax.ShapeDtypeStruct((CPG, span), F32),
         in_specs=[VMEM] * (1 + len(sums)),
-        out_specs=VMEM,
+        out_specs=HBM,
+        scratch_shapes=[
+            pltpu.VMEM((CPG, span), F32),
+            pltpu.SemaphoreType.DMA((len(sums),)),
+        ],
         name="averages",
         **params(8),
     )(denom, *sums)

time: 43.7 us -> 43.7 us (level)
  no operation moved by 1% of the time
where the time goes in v9:
time: 43.7 us; the launch traced here: 43.5 us
  starting transfers between devices  19.9 us (46%)
  waiting for transfers between devices  13.5 us (31%)
  Pallas kernels  7.73 us (18%)
  local copies, waits for them, and re-layouts  1.28 us (3%)
  other arithmetic  0.95 us (2%)
    ppermute x14, starting transfers between devices, send(): return lax.ppermute(value, axis, pairs)  19.9 us
    ppermute x14, waiting for transfers between devices, send(): return lax.ppermute(value, axis, pairs)  13.5 us
    pallas_call x1, Pallas kernels, denominators(): pl.pallas_call(functools.partial(denom_kernel, first, lanes), out_shape=j...  2.74 us
    pallas_call x3, Pallas kernels, numerators(): pl.pallas_call(functools.partial(numer_kernel, mem, count, first, here, b...  2.73 us
    unnamed x4, local copies, waits for them, and re-layouts  1.27 us
    pallas_call x1, Pallas kernels, tables(): pl.pallas_call(functools.partial(table_kernel, turns), out_shape=[jax.Sha...  1.18 us
  transfers between devices with their start and end apart: 14, of which 6 were waited for; matrix products, arithmetic and copies ran while one was open for 0% of the time, Pallas kernels for 15%

profile of v9, /device:TPU:0, one launch (start us, length us, event | category | flops | bytes accessed | tf_op | source)
XLA Modules:
  0.0 43.5 jit_solution(4166984982968958108)
XLA Ops:
  0.0 0.7 %pad_add_fusion.labels = s32[3,32]{1,0:T(4,128)S(1)} fusion(s32[1,32]{1,0:T(1,128)} %bitcast.3, s32[1,32]{1,0:T(1,128)} %bitcast.4, s32[1,32]{1,0:T(1,128)} %bitcast.5), kind=kLoop, calls=%fused_computation.5 | loop fusion | flops 192 | bytes 768 | tf_op jit(solution)/shard_map/stack | solution.py:479
  0.7 1.3 %copy-done = bf16[32,18432]{1,0:T(8,128)(2,1)S(1)} copy-done((bf16[32,18432]{1,0:T(8,128)(2,1)S(1)}, bf16[32,18432]{1,0:T(8,128)(2,1)}, u32[]{:S(2)}) %copy-start) | copy-done | bytes 1179672
  2.0 0.1 pack.1
  2.1 0.5 %collective-permute-start = (bf16[4,8,4736]{2,1,0:T(8,128)(2,1)S(1)}, bf16[4,8,4736]{2,1,0:T(8,128)(2,1)S(1)}, u32[]{:S(2)}, u32[]{:S(2)}) collective-permute-start(bf16[4,8,4736]{2,1,0:T(8,128)(2,1)S(1)} %get-tuple-element.35), channel_id=1, source_target_pairs={{0,1},{1,0},{2,3},{3,2},{4,5},{5,4},{6,7},{7,6},{8,9},{9,8},{10,11... | collective-permute-start | bytes 909320 | tf_op jit(solution)/shard_map/ppermute | solution.py:49
  2.6 0.1 collective-permute-start.4
  2.7 1.1 %collective-permute-done.crossed = bf16[4,8,4736]{2,1,0:T(8,128)(2,1)S(1)} collective-permute-done((bf16[4,8,4736]{2,1,0:T(8,128)(2,1)S(1)}, bf16[4,8,4736]{2,1,0:T(8,128)(2,1)S(1)}, u32[]{:S(2)}, u32[]{:S(2)}) %collective-permute-start) | collective-permute-done | bytes 303136 | tf_op jit(solution)/shard_map/ppermute | solution.py:49
  3.9 3.0 %collective-permute-start.1 = (bf16[8,9472]{1,0:T(8,128)(2,1)S(1)}, bf16[8,9472]{1,0:T(8,128)(2,1)S(1)}, u32[]{:S(2)}, u32[]{:S(2)}) collective-permute-start(bf16[8,9472]{1,0:T(8,128)(2,1)S(1)} %get-tuple-element.37), channel_id=1, source_target_pairs={{0,2},{1,3},{2,0},{3,1},{4,6},{5,7},{6,4},{7,5},{8,10},{9,11},{10,... | collective-permute-start | bytes 454664 | tf_op jit(solution)/shard_map/ppermute | solution.py:49
  6.9 2.6 %collective-permute-start.2 = (bf16[8,9472]{1,0:T(8,128)(2,1)S(1)}, bf16[8,9472]{1,0:T(8,128)(2,1)S(1)}, u32[]{:S(2)}, u32[]{:S(2)}) collective-permute-start(bf16[8,9472]{1,0:T(8,128)(2,1)S(1)} %get-tuple-element.38), channel_id=1, source_target_pairs={{0,4},{1,5},{2,6},{3,7},{4,0},{5,1},{6,2},{7,3},{8,12},{9,13},{10,... | collective-permute-start | bytes 454664 | tf_op jit(solution)/shard_map/ppermute | solution.py:49
  9.5 0.0 collective-permute-start.3
  9.5 1.2 %tables.1 = (bf16[2304,48]{1,0:T(8,128)(2,1)S(1)}, bf16[2304,256]{1,0:T(8,128)(2,1)S(1)}) custom-call(f32[16,18432]{1,0:T(8,128)S(1)} %copy-done.1), custom_call_target="tpu_custom_call" | custom-call | flops 1048576 | bytes 65536 | tf_op jit(solution)/shard_map/tables/pallas_call | solution.py:205
  10.7 1.0 %collective-permute-start.10 = (bf16[8,9216]{1,0:T(8,128)(2,1)S(1)}, bf16[8,9216]{1,0:T(8,128)(2,1)S(1)}, u32[]{:S(2)}, u32[]{:S(2)}) collective-permute-start(bf16[8,9216]{1,0:T(8,128)(2,1)S(1)} %get-tuple-element.50), channel_id=1, source_target_pairs={{0,2},{1,3},{2,0},{3,1},{4,6},{5,7},{6,4},{7,5},{8,10},{9,11},{10,... | collective-permute-start | bytes 442376 | tf_op jit(solution)/shard_map/ppermute | solution.py:49
  11.7 3.5 %collective-permute-start.8 = (bf16[8,9216]{1,0:T(8,128)(2,1)S(1)}, bf16[8,9216]{1,0:T(8,128)(2,1)S(1)}, u32[]{:S(2)}, u32[]{:S(2)}) collective-permute-start(bf16[8,9216]{1,0:T(8,128)(2,1)S(1)} %get-tuple-element.48), channel_id=1, source_target_pairs={{0,4},{1,5},{2,6},{3,7},{4,0},{5,1},{6,2},{7,3},{8,12},{9,13},{10,... | collective-permute-start | bytes 442376 | tf_op jit(solution)/shard_map/ppermute | solution.py:49
  15.2 0.0 collective-permute-done.1.refs_1_
  15.2 2.1 %collective-permute-start.9 = (bf16[8,9216]{1,0:T(8,128)(2,1)S(1)}, bf16[8,9216]{1,0:T(8,128)(2,1)S(1)}, u32[]{:S(2)}, u32[]{:S(2)}) collective-permute-start(bf16[8,9216]{1,0:T(8,128)(2,1)S(1)} %get-tuple-element.49), channel_id=1, source_target_pairs={{0,6},{1,7},{2,4},{3,5},{4,2},{5,3},{6,0},{7,1},{8,14},{9,15},{10,... | collective-permute-start | bytes 442376 | tf_op jit(solution)/shard_map/ppermute | solution.py:49
  17.2 3.9 %collective-permute-done.2.refs_2_ = bf16[8,9472]{1,0:T(8,128)(2,1)S(1)} collective-permute-done((bf16[8,9472]{1,0:T(8,128)(2,1)S(1)}, bf16[8,9472]{1,0:T(8,128)(2,1)S(1)}, u32[]{:S(2)}, u32[]{:S(2)}) %collective-permute-start.2) | collective-permute-done | bytes 151584 | tf_op jit(solution)/shard_map/ppermute | solution.py:49
  21.1 1.2 %numerators.3 = (f32[8,256]{1,0:T(8,128)S(1)}, f32[456,128]{1,0:T(8,128)S(1)}, f32[456,128]{1,0:T(8,128)S(1)}, f32[456,128]{1,0:T(8,128)S(1)}, f32[456,128]{1,0:T(8,128)S(1)}) custom-call(bf16[2304,48]{1,0:T(8,128)(2,1)S(1)} %get-tuple-element.33.refs_0_.pieces, bf16[8,9472]{1,0:T(8,128)(2,1)S(1)} %get-tuple-element.36.refs_0_, ...), custom_call_target="tpu_custom_call" | custom-call | flops 1048576 | bytes 65536 | tf_op jit(solution)/shard_map/numerators/pallas_call | solution.py:362
  22.4 2.5 %collective-permute-start.7 = (f16[456,128]{1,0:T(8,128)(2,1)S(1)}, f16[456,128]{1,0:T(8,128)(2,1)S(1)}, u32[]{:S(2)}, u32[]{:S(2)}) collective-permute-start(f16[456,128]{1,0:T(8,128)(2,1)S(1)} %convert_element_type.49), channel_id=1, source_target_pairs={{0,24},{8,16},{16,8},{24,0},{1,25},{9,17},{17,9},{25,1},{2,26},{10... | collective-permute-start | bytes 350216 | tf_op jit(solution)/shard_map/ppermute | solution.py:49
  25.0 0.6 %collective-permute-start.6 = (f16[456,128]{1,0:T(8,128)(2,1)S(1)}, f16[456,128]{1,0:T(8,128)(2,1)S(1)}, u32[]{:S(2)}, u32[]{:S(2)}) collective-permute-start(f16[456,128]{1,0:T(8,128)(2,1)S(1)} %convert_element_type.47), channel_id=1, source_target_pairs={{0,16},{8,24},{16,0},{24,8},{1,17},{9,25},{17,1},{25,9},{2,18},{10... | collective-permute-start | bytes 350216 | tf_op jit(solution)/shard_map/ppermute | solution.py:49
  25.6 0.5 %collective-permute-start.5 = (f16[456,128]{1,0:T(8,128)(2,1)S(1)}, f16[456,128]{1,0:T(8,128)(2,1)S(1)}, u32[]{:S(2)}, u32[]{:S(2)}) collective-permute-start(f16[456,128]{1,0:T(8,128)(2,1)S(1)} %convert_element_type.45), channel_id=1, source_target_pairs={{0,8},{8,0},{16,24},{24,16},{1,9},{9,1},{17,25},{25,17},{2,10},{10... | collective-permute-start | bytes 350216 | tf_op jit(solution)/shard_map/ppermute | solution.py:49
  26.1 0.7 %numerators.4 = (f32[456,128]{1,0:T(8,128)S(1)}, f32[456,128]{1,0:T(8,128)S(1)}, f32[456,128]{1,0:T(8,128)S(1)}, f32[456,128]{1,0:T(8,128)S(1)}) custom-call(bf16[2304,48]{1,0:T(8,128)(2,1)S(1)} %get-tuple-element.33.refs_0_.pieces, f32[8,256]{1,0:T(8,128)S(1)} %get-tuple-element.47.refs_0_, bf16[8,9216]{1,0:T(8,128)(2,1)S(1)} %get-tuple-element.42.refs_4_.refs_1_, ...), custom_call_target="tpu_custom_call" | custom-call | flops 1048576 | bytes 65536 | tf_op jit(solution)/shard_map/numerators/pallas_call | solution.py:362
  26.8 7.0 %collective-permute-done.8.refs_1_ = bf16[8,9216]{1,0:T(8,128)(2,1)S(1)} collective-permute-done((bf16[8,9216]{1,0:T(8,128)(2,1)S(1)}, bf16[8,9216]{1,0:T(8,128)(2,1)S(1)}, u32[]{:S(2)}, u32[]{:S(2)}) %collective-permute-start.8) | collective-permute-done | bytes 147488 | tf_op jit(solution)/shard_map/ppermute | solution.py:49
  33.9 0.8 %numerators.5 = (f32[456,128]{1,0:T(8,128)S(1)}, f32[456,128]{1,0:T(8,128)S(1)}, f32[456,128]{1,0:T(8,128)S(1)}, f32[456,128]{1,0:T(8,128)S(1)}) custom-call(bf16[2304,48]{1,0:T(8,128)(2,1)S(1)} %get-tuple-element.33.refs_0_.pieces, f32[8,256]{1,0:T(8,128)S(1)} %get-tuple-element.47.refs_0_, bf16[8,9216]{1,0:T(8,128)(2,1)S(1)} %collective-permute-done.8.refs_1_, ...), custom_call_target="tpu_custom_call" | custom-call | flops 1048576 | bytes 65536 | tf_op jit(solution)/shard_map/numerators/pallas_call | solution.py:362
  34.7 2.5 %collective-permute-start.13 = (f16[456,128]{1,0:T(8,128)(2,1)S(1)}, f16[456,128]{1,0:T(8,128)(2,1)S(1)}, u32[]{:S(2)}, u32[]{:S(2)}) collective-permute-start(f16[456,128]{1,0:T(8,128)(2,1)S(1)} %convert_element_type.58), channel_id=1, source_target_pairs={{0,24},{8,16},{16,8},{24,0},{1,25},{9,17},{17,9},{25,1},{2,26},{10... | collective-permute-start | bytes 350216 | tf_op jit(solution)/shard_map/ppermute | solution.py:49
  37.2 0.5 %collective-permute-start.12 = (f16[456,128]{1,0:T(8,128)(2,1)S(1)}, f16[456,128]{1,0:T(8,128)(2,1)S(1)}, u32[]{:S(2)}, u32[]{:S(2)}) collective-permute-start(f16[456,128]{1,0:T(8,128)(2,1)S(1)} %convert_element_type.56), channel_id=1, source_target_pairs={{0,16},{8,24},{16,0},{24,8},{1,17},{9,25},{17,1},{25,9},{2,18},{10... | collective-permute-start | bytes 350216 | tf_op jit(solution)/shard_map/ppermute | solution.py:49
  37.7 0.5 %collective-permute-start.11 = (f16[456,128]{1,0:T(8,128)(2,1)S(1)}, f16[456,128]{1,0:T(8,128)(2,1)S(1)}, u32[]{:S(2)}, u32[]{:S(2)}) collective-permute-start(f16[456,128]{1,0:T(8,128)(2,1)S(1)} %convert_element_type.54), channel_id=1, source_target_pairs={{0,8},{8,0},{16,24},{24,16},{1,9},{9,1},{17,25},{25,17},{2,10},{10... | collective-permute-start | bytes 350216 | tf_op jit(solution)/shard_map/ppermute | solution.py:49
  38.3 0.1 convert_add_fusion.1.refs_0_
  38.4 2.7 %denominators.1.denom = f32[56,2304]{1,0:T(8,128)S(1)} custom-call(bf16[2304,256]{1,0:T(8,128)(2,1)S(1)} %get-tuple-element.32.weights, f32[8,128]{1,0:T(8,128)S(1)} %slice.12.refs_0_, f32[8,128]{1,0:T(8,128)S(1)} %slice_convert_fusion.2.refs_1_, f32[8,128]{1,0:T(8,128)S(1)} %slice_convert_fusion.1.refs_2_, f32[8,128]{1,0:T(8,128)S(1)} %slice_convert_fusion.refs_3_), custom_call_target="tpu_custom_call" | custom-call | flops 1048576 | bytes 65536 | tf_op jit(solution)/shard_map/denominators/pallas_call | solution.py:415
  41.1 0.1 collective-permute-done.13
  41.2 1.2 %collective-permute-done.12 = f16[456,128]{1,0:T(8,128)(2,1)S(1)} collective-permute-done((f16[456,128]{1,0:T(8,128)(2,1)S(1)}, f16[456,128]{1,0:T(8,128)(2,1)S(1)}, u32[]{:S(2)}, u32[]{:S(2)}) %collective-permute-start.12) | collective-permute-done | bytes 116768 | tf_op jit(solution)/shard_map/ppermute | solution.py:49
  42.4 0.1 collective-permute-done.11
  42.5 0.1 convert_add_fusion.refs_1_
  42.6 0.9 %averages.1 = f32[50,2304]{1,0:T(8,128)} custom-call(f32[56,2304]{1,0:T(8,128)S(1)} %denominators.1.denom, f32[456,128]{1,0:T(8,128)S(1)} %convert_add_fusion.1.refs_0_, f32[456,128]{1,0:T(8,128)S(1)} %convert_add_fusion.refs_1_), custom_call_target="tpu_custom_call" | custom-call | flops 1048576 | bytes 65536 | tf_op jit(solution)/shard_map/averages/pallas_call | solution.py:443
  (22 shorter events, 0.2 us)
Async XLA Ops:
  0.7 1.3 %copy-start = (bf16[32,18432]{1,0:T(8,128)(2,1)S(1)}, bf16[32,18432]{1,0:T(8,128)(2,1)}, u32[]{:S(2)}) copy-start(bf16[32,18432]{1,0:T(8,128)(2,1)} %img.1) | copy-start | bytes 3538948
  2.0 7.5 %copy-start.1 = (f32[16,18432]{1,0:T(8,128)S(1)}, f32[16,18432]{1,0:T(8,128)}, u32[]{:S(2)}) copy-start(f32[16,18432]{1,0:T(8,128)} %table.1) | copy-start | bytes 3538948
  2.1 1.7 %collective-permute-start = (bf16[4,8,4736]{2,1,0:T(8,128)(2,1)S(1)}, bf16[4,8,4736]{2,1,0:T(8,128)(2,1)S(1)}, u32[]{:S(2)}, u32[]{:S(2)}) collective-permute-start(bf16[4,8,4736]{2,1,0:T(8,128)(2,1)S(1)} %get-tuple-element.35), channel_id=1, source_target_pairs={{0,1},{1,0},{2,3},{3,2},{4,5},{5,4},{6,7},{7,6},{8,9},{9,8},{10,11... | collective-permute-start | bytes 909320 | tf_op jit(solution)/shard_map/ppermute | solution.py:49
  2.6 8.1 %collective-permute-start.4 = (bf16[4,8,4608]{2,1,0:T(8,128)(2,1)S(1)}, bf16[4,8,4608]{2,1,0:T(8,128)(2,1)S(1)}, u32[]{:S(2)}, u32[]{:S(2)}) collective-permute-start(bf16[4,8,4608]{2,1,0:T(8,128)(2,1)S(1)} %get-tuple-element.41), channel_id=1, source_target_pairs={{0,1},{1,0},{2,3},{3,2},{4,5},{5,4},{6,7},{7,6},{8,9},{9,8},{10,11... | collective-permute-start | bytes 884744 | tf_op jit(solution)/shard_map/ppermute | solution.py:49
  3.9 11.3 %collective-permute-start.1 = (bf16[8,9472]{1,0:T(8,128)(2,1)S(1)}, bf16[8,9472]{1,0:T(8,128)(2,1)S(1)}, u32[]{:S(2)}, u32[]{:S(2)}) collective-permute-start(bf16[8,9472]{1,0:T(8,128)(2,1)S(1)} %get-tuple-element.37), channel_id=1, source_target_pairs={{0,2},{1,3},{2,0},{3,1},{4,6},{5,7},{6,4},{7,5},{8,10},{9,11},{10,... | collective-permute-start | bytes 454664 | tf_op jit(solution)/shard_map/ppermute | solution.py:49
  6.9 14.3 %collective-permute-start.2 = (bf16[8,9472]{1,0:T(8,128)(2,1)S(1)}, bf16[8,9472]{1,0:T(8,128)(2,1)S(1)}, u32[]{:S(2)}, u32[]{:S(2)}) collective-permute-start(bf16[8,9472]{1,0:T(8,128)(2,1)S(1)} %get-tuple-element.38), channel_id=1, source_target_pairs={{0,4},{1,5},{2,6},{3,7},{4,0},{5,1},{6,2},{7,3},{8,12},{9,13},{10,... | collective-permute-start | bytes 454664 | tf_op jit(solution)/shard_map/ppermute | solution.py:49
  9.5 11.7 %collective-permute-start.3 = (bf16[8,9472]{1,0:T(8,128)(2,1)S(1)}, bf16[8,9472]{1,0:T(8,128)(2,1)S(1)}, u32[]{:S(2)}, u32[]{:S(2)}) collective-permute-start(bf16[8,9472]{1,0:T(8,128)(2,1)S(1)} %get-tuple-element.39), channel_id=1, source_target_pairs={{0,6},{1,7},{2,4},{3,5},{4,2},{5,3},{6,0},{7,1},{8,14},{9,15},{10,... | collective-permute-start | bytes 454664 | tf_op jit(solution)/shard_map/ppermute | solution.py:49
  10.7 14.8 %collective-permute-start.10 = (bf16[8,9216]{1,0:T(8,128)(2,1)S(1)}, bf16[8,9216]{1,0:T(8,128)(2,1)S(1)}, u32[]{:S(2)}, u32[]{:S(2)}) collective-permute-start(bf16[8,9216]{1,0:T(8,128)(2,1)S(1)} %get-tuple-element.50), channel_id=1, source_target_pairs={{0,2},{1,3},{2,0},{3,1},{4,6},{5,7},{6,4},{7,5},{8,10},{9,11},{10,... | collective-permute-start | bytes 442376 | tf_op jit(solution)/shard_map/ppermute | solution.py:49
  11.7 22.2 %collective-permute-start.8 = (bf16[8,9216]{1,0:T(8,128)(2,1)S(1)}, bf16[8,9216]{1,0:T(8,128)(2,1)S(1)}, u32[]{:S(2)}, u32[]{:S(2)}) collective-permute-start(bf16[8,9216]{1,0:T(8,128)(2,1)S(1)} %get-tuple-element.48), channel_id=1, source_target_pairs={{0,4},{1,5},{2,6},{3,7},{4,0},{5,1},{6,2},{7,3},{8,12},{9,13},{10,... | collective-permute-start | bytes 442376 | tf_op jit(solution)/shard_map/ppermute | solution.py:49
  15.2 18.7 %collective-permute-start.9 = (bf16[8,9216]{1,0:T(8,128)(2,1)S(1)}, bf16[8,9216]{1,0:T(8,128)(2,1)S(1)}, u32[]{:S(2)}, u32[]{:S(2)}) collective-permute-start(bf16[8,9216]{1,0:T(8,128)(2,1)S(1)} %get-tuple-element.49), channel_id=1, source_target_pairs={{0,6},{1,7},{2,4},{3,5},{4,2},{5,3},{6,0},{7,1},{8,14},{9,15},{10,... | collective-permute-start | bytes 442376 | tf_op jit(solution)/shard_map/ppermute | solution.py:49
  22.4 15.3 %collective-permute-start.7 = (f16[456,128]{1,0:T(8,128)(2,1)S(1)}, f16[456,128]{1,0:T(8,128)(2,1)S(1)}, u32[]{:S(2)}, u32[]{:S(2)}) collective-permute-start(f16[456,128]{1,0:T(8,128)(2,1)S(1)} %convert_element_type.49), channel_id=1, source_target_pairs={{0,24},{8,16},{16,8},{24,0},{1,25},{9,17},{17,9},{25,1},{2,26},{10... | collective-permute-start | bytes 350216 | tf_op jit(solution)/shard_map/ppermute | solution.py:49
  25.0 13.3 %collective-permute-start.6 = (f16[456,128]{1,0:T(8,128)(2,1)S(1)}, f16[456,128]{1,0:T(8,128)(2,1)S(1)}, u32[]{:S(2)}, u32[]{:S(2)}) collective-permute-start(f16[456,128]{1,0:T(8,128)(2,1)S(1)} %convert_element_type.47), channel_id=1, source_target_pairs={{0,16},{8,24},{16,0},{24,8},{1,17},{9,25},{17,1},{25,9},{2,18},{10... | collective-permute-start | bytes 350216 | tf_op jit(solution)/shard_map/ppermute | solution.py:49
  25.6 12.7 %collective-permute-start.5 = (f16[456,128]{1,0:T(8,128)(2,1)S(1)}, f16[456,128]{1,0:T(8,128)(2,1)S(1)}, u32[]{:S(2)}, u32[]{:S(2)}) collective-permute-start(f16[456,128]{1,0:T(8,128)(2,1)S(1)} %convert_element_type.45), channel_id=1, source_target_pairs={{0,8},{8,0},{16,24},{24,16},{1,9},{9,1},{17,25},{25,17},{2,10},{10... | collective-permute-start | bytes 350216 | tf_op jit(solution)/shard_map/ppermute | solution.py:49
  34.7 6.5 %collective-permute-start.13 = (f16[456,128]{1,0:T(8,128)(2,1)S(1)}, f16[456,128]{1,0:T(8,128)(2,1)S(1)}, u32[]{:S(2)}, u32[]{:S(2)}) collective-permute-start(f16[456,128]{1,0:T(8,128)(2,1)S(1)} %convert_element_type.58), channel_id=1, source_target_pairs={{0,24},{8,16},{16,8},{24,0},{1,25},{9,17},{17,9},{25,1},{2,26},{10... | collective-permute-start | bytes 350216 | tf_op jit(solution)/shard_map/ppermute | solution.py:49
  37.2 5.2 %collective-permute-start.12 = (f16[456,128]{1,0:T(8,128)(2,1)S(1)}, f16[456,128]{1,0:T(8,128)(2,1)S(1)}, u32[]{:S(2)}, u32[]{:S(2)}) collective-permute-start(f16[456,128]{1,0:T(8,128)(2,1)S(1)} %convert_element_type.56), channel_id=1, source_target_pairs={{0,16},{8,24},{16,0},{24,8},{1,17},{9,25},{17,1},{25,9},{2,18},{10... | collective-permute-start | bytes 350216 | tf_op jit(solution)/shard_map/ppermute | solution.py:49
  37.7 4.8 %collective-permute-start.11 = (f16[456,128]{1,0:T(8,128)(2,1)S(1)}, f16[456,128]{1,0:T(8,128)(2,1)S(1)}, u32[]{:S(2)}, u32[]{:S(2)}) collective-permute-start(f16[456,128]{1,0:T(8,128)(2,1)S(1)} %convert_element_type.54), channel_id=1, source_target_pairs={{0,8},{8,0},{16,24},{24,16},{1,9},{9,1},{17,25},{25,17},{2,10},{10... | collective-permute-start | bytes 350216 | tf_op jit(solution)/shard_map/ppermute | solution.py:49
